TPU v7x, 32 devices: a whole 2x2x4 slice. The times are simulated.
32 devices in a mesh: dp: 4 (over z), mp: 8 (over y, x, core).
Axes of the slice: x: 2, y: 2, z: 4, core: 2. Of those that a mesh axis runs over, the one named last changes fastest.
Arguments:
- output_gradient: bfloat16 [3072, 8192], P('dp', 'mp'), may hold values from -6 to 6
- saved_gate_value: bfloat16 [3072, 14336], P('dp', 'mp'), may hold values from -6 to 6
- saved_up_value: bfloat16 [3072, 14336], P('dp', 'mp'), may hold values from -6 to 6
- down_weight: bfloat16 [14336, 8192], P('mp', 'dp'), may hold values from -0.046875 to 0.046875
- adapter_first_weight: bfloat16 [64, 64, 14336], P('dp', None, 'mp'), may hold values from -0.046875 to 0.046875
- adapter_second_weight: bfloat16 [64, 64, 8192], P('dp', None, 'mp'), may hold values from -0.0625 to 0.0625
- adapter_of_block: int32 [48], replicated, may hold values from 0 to 63, as said below
- slot_of_adapter: int32 [64], replicated, may hold values from 0 to 63, as said below
Outputs:
- d_gate: bfloat16 [3072, 14336], P('dp', 'mp')
- d_up: bfloat16 [3072, 14336], P('dp', 'mp')
- grad_a: float32 [64, 64, 14336], P('dp', None, 'mp')
- grad_b: float32 [64, 64, 8192], P('dp', None, 'mp')
Inputs may be any that keep to these rules, and one draw needn't show every extreme that they name: `adapter_of_block`: block k holds tokens k * 64 to k * 64 + 63; group g holds blocks g * 12 onward. Slot s belongs to owner s // 16; the blocks of one group use adapters of any one owner at most 3 times, and in every draw one owner takes exactly 3 blocks of every group. A permutation: adapter a is stored at index slot_of_adapter[a] of adapter_first_weight, adapter_second_weight, grad_a and grad_b.
All inputs are finite; a program needn't handle non-finite values.
Results may differ from a plain program's by a relative error of at most 0.0057.
Values may be sent and summed in bfloat16 or wider, within the bound.
No kernel may reach another device: no remote copies, remote signals or barrier semaphores. Data moves between devices by JAX's collectives and lax.ppermute only.
A program may use at most 128 MiB of HBM per device.

v0:
```python
import jax
import jax.numpy as jnp
from jax import lax
from jax.sharding import PartitionSpec as P

ADAPTER_RANK = 64
BLK = 64


adapter_scale = 2.0


def shards(
    output_gradient,
    saved_gate_value,
    saved_up_value,
    down_weight,
    adapter_first_weight,
    adapter_second_weight,
    adapter_of_block,
    slot_of_adapter,
):
    groups = lax.axis_size("dp")
    my_group = lax.axis_index("dp")
    tok_rows = output_gradient.shape[0]
    blocks = tok_rows // BLK
    owner_totals = adapter_first_weight.shape[0]
    adapters = slot_of_adapter.shape[0]
    ff_local = saved_gate_value.shape[1]
    d_local = output_gradient.shape[1]
    capacity = (blocks + groups - 1) // groups
    gate_float = saved_gate_value.astype(jnp.float32)
    up_float = saved_up_value.astype(jnp.float32)
    squash = jax.nn.sigmoid(gate_float)
    activated = gate_float * squash
    hidden = (activated * up_float).astype(jnp.bfloat16)
    match_table = adapter_of_block[:, None] == jnp.arange(adapters, dtype=jnp.int32)[None, :]
    slot_of_block = jnp.sum(jnp.where(match_table, slot_of_adapter[None, :], 0), axis=1)
    owners = (slot_of_block // owner_totals).reshape(groups, blocks)
    local_slot = (slot_of_block % owner_totals).reshape(groups, blocks)
    block_index = jnp.arange(blocks, dtype=jnp.int32)
    earlier = (owners[:, :, None] == owners[:, None, :]) & (
        block_index[None, None, :] < block_index[None, :, None]
    )
    ranks = jnp.sum(earlier.astype(jnp.int32), axis=2)
    owned_here = owners == my_group
    rank_values = jnp.arange(capacity, dtype=jnp.int32)
    hits = owned_here[:, None, :] & (ranks[:, None, :] == rank_values[None, :, None])
    incoming_valid = jnp.any(hits, axis=2)
    arriving_slot = jnp.sum(jnp.where(hits, local_slot[:, None, :], 0), axis=2)
    own_owner = lax.dynamic_index_in_dim(owners, my_group, 0, keepdims=False)
    own_rank = lax.dynamic_index_in_dim(ranks, my_group, 0, keepdims=False)
    own_index = own_owner * capacity + own_rank
    a_send = jnp.where(
        incoming_valid[:, :, None, None],
        jnp.take(adapter_first_weight, arriving_slot, axis=0),
        jnp.zeros((), adapter_first_weight.dtype),
    )
    b_send = jnp.where(
        incoming_valid[:, :, None, None],
        jnp.take(adapter_second_weight, arriving_slot, axis=0),
        jnp.zeros((), adapter_second_weight.dtype),
    )
    a_recv, b_recv = (
        lax.all_to_all(a_send, "dp", split_axis=0, concat_axis=0, tiled=True),
        lax.all_to_all(b_send, "dp", split_axis=0, concat_axis=0, tiled=True),
    )
    first_factor_blocks = jnp.take(
        a_recv.reshape(groups * capacity, ADAPTER_RANK, ff_local), own_index, axis=0
    )
    second_factor_blocks = jnp.take(
        b_recv.reshape(groups * capacity, ADAPTER_RANK, d_local), own_index, axis=0
    )
    hidden_blocks = hidden.reshape(blocks, BLK, ff_local)
    output_blocks = output_gradient.reshape(blocks, BLK, d_local)
    down_part = jnp.einsum(
        "btf,brf->btr", hidden_blocks, first_factor_blocks, preferred_element_type=jnp.float32
    )
    back_part = jnp.einsum(
        "btd,brd->btr", output_blocks, second_factor_blocks, preferred_element_type=jnp.float32
    )
    summed_total = lax.psum(jnp.concatenate([down_part, back_part], axis=2), "mp")
    downward_factor = summed_total[:, :, :ADAPTER_RANK].astype(jnp.bfloat16)
    backward_factor = (adapter_scale * summed_total[:, :, ADAPTER_RANK:]).astype(jnp.bfloat16)
    out_whole = lax.all_gather(output_gradient, "mp", axis=1, tiled=True)
    side_term = jnp.einsum(
        "btr,brf->btf", backward_factor, first_factor_blocks, preferred_element_type=jnp.float32
    ).reshape(tok_rows, ff_local)
    d_hidden = side_term + lax.dot_general(
        out_whole,
        lax.all_gather(down_weight, "dp", axis=1, tiled=True),
        (((1,), (1,)), ((), ())),
        preferred_element_type=jnp.float32,
    )
    d_gate = (d_hidden * up_float * squash * (1.0 + gate_float * (1.0 - squash))).astype(
        jnp.bfloat16
    )
    d_up = (d_hidden * activated).astype(jnp.bfloat16)
    group_values = jnp.arange(groups, dtype=jnp.int32)
    route_table = (own_owner[None, None, :] == group_values[:, None, None]) & (
        own_rank[None, None, :] == rank_values[None, :, None]
    )
    route_valid = jnp.any(route_table, axis=2)
    route_block = jnp.sum(jnp.where(route_table, block_index[None, None, :], 0), axis=2)
    factors = jnp.concatenate([downward_factor, backward_factor], axis=2)
    send_h = jnp.where(
        route_valid[:, :, None, None],
        jnp.take(hidden_blocks, route_block, axis=0),
        jnp.zeros((), jnp.bfloat16),
    )
    send_o = jnp.where(
        route_valid[:, :, None, None],
        jnp.take(output_blocks, route_block, axis=0),
        jnp.zeros((), jnp.bfloat16),
    )
    send_f = jnp.where(
        route_valid[:, :, None, None],
        jnp.take(factors, route_block, axis=0),
        jnp.zeros((), jnp.bfloat16),
    )
    recv_h, recv_o, recv_f = (
        lax.all_to_all(send_h, "dp", split_axis=0, concat_axis=0, tiled=True),
        lax.all_to_all(send_o, "dp", split_axis=0, concat_axis=0, tiled=True),
        lax.all_to_all(send_f, "dp", split_axis=0, concat_axis=0, tiled=True),
    )
    terms_a = jnp.einsum(
        "gctr,gctf->gcrf",
        recv_f[:, :, :, ADAPTER_RANK:],
        recv_h,
        preferred_element_type=jnp.float32,
    ).astype(jnp.bfloat16)
    terms_b = (
        adapter_scale
        * jnp.einsum(
            "gctr,gctd->gcrd",
            recv_f[:, :, :, :ADAPTER_RANK],
            recv_o,
            preferred_element_type=jnp.float32,
        )
    ).astype(jnp.bfloat16)
    flat_slot = arriving_slot.reshape(groups * capacity)
    flat_valid = incoming_valid.reshape(groups * capacity)
    selector = (
        (flat_slot[None, :] == jnp.arange(owner_totals, dtype=jnp.int32)[:, None])
        & flat_valid[None, :]
    ).astype(jnp.bfloat16)
    grad_a = jnp.dot(
        selector,
        terms_a.reshape(groups * capacity, ADAPTER_RANK * ff_local),
        preferred_element_type=jnp.float32,
    ).reshape(owner_totals, ADAPTER_RANK, ff_local)
    grad_b = jnp.dot(
        selector,
        terms_b.reshape(groups * capacity, ADAPTER_RANK * d_local),
        preferred_element_type=jnp.float32,
    ).reshape(owner_totals, ADAPTER_RANK, d_local)
    return (d_gate, d_up, grad_a, grad_b)


def solution(mesh):
    in_specs = (
        P("dp", "mp"),
        P("dp", "mp"),
        P("dp", "mp"),
        P("mp", "dp"),
        P("dp", None, "mp"),
        P("dp", None, "mp"),
        P(),
        P(),
    )
    out_specs = (P("dp", "mp"), P("dp", "mp"), P("dp", None, "mp"), P("dp", None, "mp"))
    return jax.shard_map(shards, mesh=mesh, in_specs=in_specs, out_specs=out_specs, check_vma=False)
```

profile of v0, /device:TPU:10, one launch (start us, length us, event | category | flops | bytes accessed | tf_op | source)
XLA Modules:
  0.0 793.0 jit_solution(11467985727100427440)
XLA Ops:
  11.4 2.8 select_select_fusion.3
  14.2 5.3 all-to-all-start.1
  19.5 2.8 gather_fusion
  24.2 29.0 %all-to-all-done.1 = bf16[4,3,64,1024]{3,2,1,0:T(8,128)(2,1)} async-done(((bf16[4,3,64,1024]{3,2,1,0:T(8,128)(2,1)}), bf16[4,3,64,1024]{3,2,1,0:T(8,128)(2,1)}, u32[]{:S(2)}, u32[]{:S(2)}) %all-to-all-start.1) | async-done | bytes 1572896 | tf_op jit(solution)/shard_map/all_to_all | solution.py:66
  53.2 7.9 all-to-all-start
  61.8 5.0 fusion
  69.6 50.0 %all-to-all-done = bf16[4,3,64,1792]{3,2,1,0:T(8,128)(2,1)} async-done(((bf16[4,3,64,1792]{3,2,1,0:T(8,128)(2,1)}), bf16[4,3,64,1792]{3,2,1,0:T(8,128)(2,1)}, u32[]{:S(2)}, u32[]{:S(2)}) %all-to-all-start) | async-done | bytes 2752544 | tf_op jit(solution)/shard_map/all_to_all | solution.py:65
  119.6 2.5 gather_fusion.1
  122.1 3.7 fusion.19
  128.7 2.5 gather_fusion.5
  133.5 7.0 all-to-all-start.3
  140.6 3.3 gather_fusion.6
  143.8 38.5 %all-reduce.2.cloned.1.call-done = f32[12,64,128]{2,1,0:T(8,128)} async-done(((f32[12,64,128]{2,1,0:T(8,128)}), f32[12,64,128]{2,1,0:T(8,128)}) %all-reduce.2.cloned.1.call-update) | async-done | bytes 393232 | tf_op jit(solution)/shard_map/psum | solution.py:82
  186.0 13.0 %all-to-all-done.3 = bf16[4,3,64,1792]{3,2,1,0:T(8,128)(2,1)S(1)} async-done(((bf16[4,3,64,1792]{3,2,1,0:T(8,128)(2,1)}), bf16[4,3,64,1792]{3,2,1,0:T(8,128)(2,1)S(1)}, u32[]{:S(2)}, u32[]{:S(2)}) %all-to-all-start.3) | async-done | bytes 2752544 | tf_op jit(solution)/shard_map/all_to_all | solution.py:122
  199.0 6.6 all-to-all-start.2
  205.6 2.8 select_select_fusion.2
  208.4 3.0 all-to-all-done.2
  211.4 5.8 all-to-all-start.4
  217.4 5.5 fusion.18
  226.2 7.3 copy.103
  233.5 14.8 %all-to-all-done.4 = bf16[4,3,64,1024]{3,2,1,0:T(8,128)(2,1)} async-done(((bf16[4,3,64,1024]{3,2,1,0:T(8,128)(2,1)}), bf16[4,3,64,1024]{3,2,1,0:T(8,128)(2,1)}, u32[]{:S(2)}, u32[]{:S(2)}) %all-to-all-start.4) | async-done | bytes 1572896 | tf_op jit(solution)/shard_map/all_to_all | solution.py:123
  251.8 4.7 copy.104
  256.4 492.0 %all-gather.5.cloned.1.call-done = bf16[1792,8192]{1,0:T(8,128)(2,1)} async-done(((bf16[1792,2048]{1,0:T(8,128)(2,1)}), bf16[1792,8192]{1,0:T(8,128)(2,1)}) %all-gather.5.cloned.1.call-update) | async-done | bytes 29360144 | tf_op jit(solution)/shard_map/all_gather | solution.py:91
  748.4 38.0 %multiply_convert_fusion = (bf16[768,1792]{1,0:T(8,128)(2,1)}, bf16[768,1792]{1,0:T(8,128)(2,1)}) fusion(bf16[768,1792]{1,0:T(8,128)(2,1)} %param.9, bf16[768,1792]{1,0:T(8,128)(2,1)} %param.10, bf16[768,8192]{1,0:T(8,128)(2,1)} %all-gather.3.cloned.1.call-done, bf16[1792,8192]{1,0:T(8,128)(2,1)} %all-gather.5.cloned.1.call-done, f32[12,64,1792]{2,1,0:T(8,128)} %fusion.18), kind=kOutput, calls=%fused_computation.21 | convolution fusion | flops 22570598400 | bytes 58458112 | tf_op jit(solution)/shard_map/dot_general | solution.py:89
  (71 shorter events, 25.1 us)
Async XLA Ops:
  7.2 2.4 copy-start
  14.2 39.0 %all-to-all-start.1 = ((bf16[4,3,64,1024]{3,2,1,0:T(8,128)(2,1)}), bf16[4,3,64,1024]{3,2,1,0:T(8,128)(2,1)}, u32[]{:S(2)}, u32[]{:S(2)}) async-start(bf16[4,3,64,1024]{3,2,1,0:T(8,128)(2,1)} %select_select_fusion.3), calls=%async_computation.1 | async-start | bytes 3145728 | tf_op jit(solution)/shard_map/all_to_all | solution.py:66
  24.2 37.5 %copy-start.4 = (bf16[768,1792]{1,0:T(8,128)(2,1)S(1)}, bf16[768,1792]{1,0:T(8,128)(2,1)}, u32[]{:S(2)}) copy-start(bf16[768,1792]{1,0:T(8,128)(2,1)} %param.9) | copy-start | bytes 8257540
  53.2 66.4 %all-to-all-start = ((bf16[4,3,64,1792]{3,2,1,0:T(8,128)(2,1)}), bf16[4,3,64,1792]{3,2,1,0:T(8,128)(2,1)}, u32[]{:S(2)}, u32[]{:S(2)}) async-start(bf16[4,3,64,1792]{3,2,1,0:T(8,128)(2,1)} %select_select_fusion.1), calls=%async_computation | async-start | bytes 5505024 | tf_op jit(solution)/shard_map/all_to_all | solution.py:65
  61.2 121.2 %all-reduce.2.cloned.1.call-start = ((), (), s32[]{:S(2)}) async-start(), calls=%async_computation.5 | async-start | bytes 786432 | tf_op jit(solution)/shard_map/psum | solution.py:82
  66.7 2.2 copy-start.3
  122.1 6.2 copy-start.2
  126.8 129.6 %all-gather.3.cloned.1.call-start = ((), (), s32[]{:S(2)}) async-start(), calls=%async_computation.6 | async-start | bytes 14155776 | tf_op jit(solution)/shard_map/all_gather | solution.py:85
  127.6 0.8 copy-start.6
  127.6 0.8 copy-start.5
  127.6 620.8 %all-gather.5.cloned.1.call-start = ((), (), s32[]{:S(2)}) async-start(), calls=%async_computation.7 | async-start | bytes 36700160 | tf_op jit(solution)/shard_map/all_gather | solution.py:91
  133.5 65.5 %all-to-all-start.3 = ((bf16[4,3,64,1792]{3,2,1,0:T(8,128)(2,1)}), bf16[4,3,64,1792]{3,2,1,0:T(8,128)(2,1)S(1)}, u32[]{:S(2)}, u32[]{:S(2)}) async-start(bf16[4,3,64,1792]{3,2,1,0:T(8,128)(2,1)} %select_select_fusion), calls=%async_computation.3 | async-start | bytes 5505024 | tf_op jit(solution)/shard_map/all_to_all | solution.py:122
  199.0 12.4 %all-to-all-start.2 = ((bf16[4,3,64,128]{3,2,1,0:T(8,128)(2,1)}), bf16[4,3,64,128]{3,2,1,0:T(8,128)(2,1)S(1)}, u32[]{:S(2)}, u32[]{:S(2)}) async-start(bf16[4,3,64,128]{3,2,1,0:T(8,128)(2,1)} %select_select_fusion.4), calls=%async_computation.2 | async-start | bytes 393216 | tf_op jit(solution)/shard_map/all_to_all | solution.py:124
  211.4 36.9 %all-to-all-start.4 = ((bf16[4,3,64,1024]{3,2,1,0:T(8,128)(2,1)}), bf16[4,3,64,1024]{3,2,1,0:T(8,128)(2,1)}, u32[]{:S(2)}, u32[]{:S(2)}) async-start(bf16[4,3,64,1024]{3,2,1,0:T(8,128)(2,1)} %select_select_fusion.2), calls=%async_computation.4 | async-start | bytes 3145728 | tf_op jit(solution)/shard_map/all_to_all | solution.py:123
  748.4 38.1 %copy-start.1 = (bf16[16,64,1024]{2,1,0:T(8,128)(2,1)S(1)}, bf16[16,64,1024]{2,1,0:T(8,128)(2,1)}, u32[]{:S(2)}) copy-start(bf16[16,64,1024]{2,1,0:T(8,128)(2,1)} %param.13) | copy-start | bytes 6291460
Sparse Core Ops, SparseCore 0:
  126.9 55.3 all-reduce.1
  184.2 72.1 all-gather.2
  258.0 490.3 all-gather.4
where the time goes:
time: 798 us; the launch traced here: 793 us
  waiting for transfers between devices  642 us (80%)
  matrix products  54.3 us (7%)
  starting transfers between devices  32.8 us (4%)
  local copies, waits for them, and re-layouts  30.2 us (4%)
  other arithmetic  20 us (3%)
  between operations  14 us (2%)
    all_gather x1, waiting for transfers between devices, shards(): lax.all_gather(down_weight, 'dp', axis=1, tiled=True)  492 us
    all_to_all x1, waiting for transfers between devices, shards(): lax.all_to_all(a_send, 'dp', split_axis=0, concat_axis=0, tiled=True)  50 us
    psum x1, waiting for transfers between devices, shards(): lax.psum(jnp.concatenate([down_part, back_part], axis=2), 'mp')  38.5 us
    dot_general x1, matrix products, shards(): lax.dot_general(out_whole, lax.all_gather(down_weight, 'dp', axis=1, tile...  38 us
    all_to_all x1, waiting for transfers between devices, shards(): lax.all_to_all(b_send, 'dp', split_axis=0, concat_axis=0, tiled=True)  29 us
  transfers between devices with their start and end apart: 8, of which 7 were waited for; matrix products, arithmetic and copies ran while one was open for 7% of the time, Pallas kernels for 0%

commit v1 on v0

v1 whole, which is shorter than its diff:
```python
import jax
import jax.numpy as jnp
from jax import lax
from jax.sharding import PartitionSpec as P

ADAPTER_RANK = 64
BLK = 64


adapter_scale = 2.0


def sum_over_mp(x):
    size = lax.axis_size("mp")
    if size & (size - 1):
        return lax.psum(x, "mp")
    bit = 1
    while bit < size:
        x = x + lax.ppermute(x, "mp", [(i, i ^ bit) for i in range(size)])
        bit *= 2
    return x


def gather_over_mp(x):
    size = lax.axis_size("mp")
    if size != 8:
        return lax.all_gather(x, "mp", axis=0)

    def swap(v, bits):
        return lax.ppermute(v, "mp", [(i, i ^ bits) for i in range(size)])

    half = x.shape[0] // 2
    x1 = swap(x, 1)
    x2, x4 = swap(x, 2), swap(x, 4)
    x6 = jnp.concatenate([swap(x4[:half], 2), swap(x2[half:], 4)])
    x3, x5 = swap(x2, 1), swap(x4, 1)
    x7 = swap(x6, 1)
    return jnp.take(
        jnp.stack([x, x1, x2, x3, x4, x5, x6, x7]),
        jnp.arange(size, dtype=jnp.int32) ^ lax.axis_index("mp"),
        axis=0,
    )


def pick(values, table, my_group):
    places = sorted(set(table))
    result = values[places[0]]
    mine = jnp.asarray(table, jnp.int32)[jnp.minimum(my_group, len(table) - 1)]
    for place in places[1:]:
        result = jnp.where(mine == place, values[place], result)
    return result


def shards(
    output_gradient,
    saved_gate_value,
    saved_up_value,
    down_weight,
    adapter_first_weight,
    adapter_second_weight,
    adapter_of_block,
    slot_of_adapter,
):
    groups = lax.axis_size("dp")
    members = lax.axis_size("mp")
    my_group = lax.axis_index("dp")
    tok_rows = output_gradient.shape[0]
    blocks = tok_rows // BLK
    owner_totals = adapter_first_weight.shape[0]
    adapters = slot_of_adapter.shape[0]
    ff_local = saved_gate_value.shape[1]
    d_local = output_gradient.shape[1]
    slice_width = down_weight.shape[1]
    capacity = (blocks + groups - 1) // groups

    match_table = adapter_of_block[:, None] == jnp.arange(adapters, dtype=jnp.int32)[None, :]
    slot_of_block = jnp.sum(jnp.where(match_table, slot_of_adapter[None, :], 0), axis=1)
    owners = (slot_of_block // owner_totals).reshape(groups, blocks)
    local_slot = (slot_of_block % owner_totals).reshape(groups, blocks)
    block_index = jnp.arange(blocks, dtype=jnp.int32)
    earlier = (owners[:, :, None] == owners[:, None, :]) & (
        block_index[None, None, :] < block_index[None, :, None]
    )
    ranks = jnp.sum(earlier.astype(jnp.int32), axis=2)
    rank_values = jnp.arange(capacity, dtype=jnp.int32)
    hits = (owners == my_group)[:, None, :] & (ranks[:, None, :] == rank_values[None, :, None])
    incoming_valid = jnp.any(hits, axis=2)
    arriving_slot = jnp.sum(jnp.where(hits, local_slot[:, None, :], 0), axis=2)
    own_owner = lax.dynamic_index_in_dim(owners, my_group, 0, keepdims=False)
    own_rank = lax.dynamic_index_in_dim(ranks, my_group, 0, keepdims=False)
    group_values = jnp.arange(groups, dtype=jnp.int32)
    route_table = (own_owner[None, None, :] == group_values[:, None, None]) & (
        own_rank[None, None, :] == rank_values[None, :, None]
    )
    route_valid = jnp.any(route_table, axis=2)
    route_block = jnp.sum(jnp.where(route_table, block_index[None, None, :], 0), axis=2)

    def to_owners(rows):
        sent = jnp.where(
            route_valid[:, :, None, None],
            jnp.take(rows.reshape(blocks, BLK, rows.shape[1]), route_block, axis=0),
            jnp.zeros((), rows.dtype),
        )
        return lax.all_to_all(sent, "dp", split_axis=0, concat_axis=0, tiled=True)

    recv_o = to_owners(output_gradient)
    share = tok_rows // members
    by_tokens = lax.all_to_all(
        output_gradient.reshape(members, share, d_local), "mp", split_axis=0, concat_axis=0, tiled=True
    )
    by_tokens = by_tokens.transpose(1, 0, 2).reshape(share, groups, slice_width).transpose(1, 0, 2)
    by_slice = lax.all_to_all(by_tokens, "dp", split_axis=0, concat_axis=0, tiled=True)
    out_slices = gather_over_mp(by_slice)

    gate_float = saved_gate_value.astype(jnp.float32)
    up_float = saved_up_value.astype(jnp.float32)
    squash = jax.nn.sigmoid(gate_float)
    activated = gate_float * squash
    hidden = (activated * up_float).astype(jnp.bfloat16)
    recv_h = to_owners(hidden)

    a_here = jnp.take(adapter_first_weight, arriving_slot, axis=0)
    b_here = jnp.take(adapter_second_weight, arriving_slot, axis=0)
    back_factor = (
        adapter_scale
        * sum_over_mp(
            jnp.einsum("gctd,gcrd->gctr", recv_o, b_here, preferred_element_type=jnp.float32)
        )
    ).astype(jnp.bfloat16)
    down_factor = sum_over_mp(
        jnp.einsum("gctf,gcrf->gctr", recv_h, a_here, preferred_element_type=jnp.float32)
    ).astype(jnp.bfloat16)

    spread = jnp.where(
        hits.transpose(0, 2, 1)[:, :, None, :, None],
        back_factor.transpose(0, 2, 1, 3)[:, None],
        jnp.zeros((), jnp.bfloat16),
    ).reshape(groups, tok_rows, capacity * ADAPTER_RANK)
    a_rows = a_here.reshape(groups, capacity * ADAPTER_RANK, ff_local)
    order = [
        sorted(range(groups), key=lambda target: (-abs(target - i), -target)) for i in range(groups)
    ]
    place = [[order[i].index(target) for target in range(groups)] for i in range(groups)]
    order_here = jnp.asarray(order, jnp.int32)[my_group]
    partial = []
    for k in range(groups):
        target = order_here[k]
        rows = lax.dynamic_index_in_dim(out_slices, target, 1, keepdims=False).reshape(
            tok_rows, slice_width
        )
        base = lax.dot_general(
            rows, down_weight, (((1,), (1,)), ((), ())), preferred_element_type=jnp.float32
        )
        side = jnp.dot(
            lax.dynamic_index_in_dim(spread, target, 0, keepdims=False),
            lax.dynamic_index_in_dim(a_rows, target, 0, keepdims=False),
            preferred_element_type=jnp.float32,
        )
        partial.append((base + side).astype(jnp.bfloat16))

    from_left = from_right = None
    for step in range(1, groups):
        reach = groups - step
        send_r = pick(partial, [place[i][i + reach] for i in range(step)], my_group)
        send_l = pick(
            partial,
            [place[groups - 1 - i][groups - 1 - i - reach] for i in range(step)],
            groups - 1 - my_group,
        )
        if from_left is not None:
            send_r = (send_r.astype(jnp.float32) + from_left.astype(jnp.float32)).astype(jnp.bfloat16)
            send_l = (send_l.astype(jnp.float32) + from_right.astype(jnp.float32)).astype(jnp.bfloat16)
        from_left = lax.ppermute(send_r, "dp", [(i, i + 1) for i in range(step)])
        from_right = lax.ppermute(
            send_l, "dp", [(groups - 1 - i, groups - 2 - i) for i in range(step)]
        )
    d_hidden = partial[groups - 1].astype(jnp.float32)
    if from_left is not None:
        d_hidden = d_hidden + from_left.astype(jnp.float32) + from_right.astype(jnp.float32)
    d_gate = (d_hidden * up_float * squash * (1.0 + gate_float * (1.0 - squash))).astype(
        jnp.bfloat16
    )
    d_up = (d_hidden * activated).astype(jnp.bfloat16)

    terms_a = jnp.einsum(
        "gctr,gctf->gcrf", back_factor, recv_h, preferred_element_type=jnp.float32
    ).astype(jnp.bfloat16)
    terms_b = (
        adapter_scale
        * jnp.einsum("gctr,gctd->gcrd", down_factor, recv_o, preferred_element_type=jnp.float32)
    ).astype(jnp.bfloat16)
    flat_slot = arriving_slot.reshape(groups * capacity)
    flat_valid = incoming_valid.reshape(groups * capacity)
    selector = (
        (flat_slot[None, :] == jnp.arange(owner_totals, dtype=jnp.int32)[:, None])
        & flat_valid[None, :]
    ).astype(jnp.bfloat16)
    grad_a = jnp.dot(
        selector,
        terms_a.reshape(groups * capacity, ADAPTER_RANK * ff_local),
        preferred_element_type=jnp.float32,
    ).reshape(owner_totals, ADAPTER_RANK, ff_local)
    grad_b = jnp.dot(
        selector,
        terms_b.reshape(groups * capacity, ADAPTER_RANK * d_local),
        preferred_element_type=jnp.float32,
    ).reshape(owner_totals, ADAPTER_RANK, d_local)
    return (d_gate, d_up, grad_a, grad_b)


def solution(mesh):
    in_specs = (
        P("dp", "mp"),
        P("dp", "mp"),
        P("dp", "mp"),
        P("mp", "dp"),
        P("dp", None, "mp"),
        P("dp", None, "mp"),
        P(),
        P(),
    )
    out_specs = (P("dp", "mp"), P("dp", "mp"), P("dp", None, "mp"), P("dp", None, "mp"))
    return jax.shard_map(shards, mesh=mesh, in_specs=in_specs, out_specs=out_specs, check_vma=False)
```

time: 798 us -> 573 us (0.72)
  waiting for transfers between devices: 642 us -> 331 us
  local copies, waits for them, and re-layouts: 30.2 us -> 78.5 us
  other arithmetic: 20 us -> 34.2 us
  starting transfers between devices: 32.8 us -> 46.7 us
    all_gather x2 -> x0, waiting for transfers between devices: 492 us -> none  [the longest x1 492 us: shards(): lax.all_gather(down_weight, 'dp', axis=1, tiled=True)]
    ppermute x0 -> x20, waiting for transfers between devices: none -> 207 us  [the longest x3 141 us: shards(): from_left = lax.ppermute(send_r, 'dp', [(i, i + 1) for i in range(step)])]
    psum x1 -> x0, waiting for transfers between devices: 38.5 us -> none  [shards(): lax.psum(jnp.concatenate([down_part, back_part], axis=2), 'mp')]
    ppermute x0 -> x20, starting transfers between devices: none -> 21.7 us  [the longest x3 7.95 us: shards(): lax.ppermute(send_l, 'dp', [(groups - 1 - i, groups - 2 - i) for i in ran...]
    unnamed x16 -> x36, local copies, waits for them, and re-layouts: 12 us -> 26.8 us
    all_to_all x5 -> x4, waiting for transfers between devices: 110 us -> 124 us  [the longest x2 78.4 us: to_owners(): return lax.all_to_all(sent, 'dp', split_axis=0, concat_axis=0, tiled=True)]
    gather x7 -> x5, local copies, waits for them, and re-layouts: 15.6 us -> 24.6 us  [the longest x1 11 us: gather_over_mp(): jnp.take(jnp.stack([x, x1, x2, x3, x4, x5, x6, x7]), jnp.arange(size, dty...]
    select_n x8 -> x7, other arithmetic: 10.2 us -> 18.9 us  [the longest x2 6.8 us: gather_over_mp(): jnp.take(jnp.stack([x, x1, x2, x3, x4, x5, x6, x7]), jnp.arange(size, dty...]
  transfers between devices with their start and end apart: 8 -> 24, of which waited for: 7 -> 15; matrix products, arithmetic and copies ran while one was open for 7% -> 16% of each run, Pallas kernels for 0% -> 0%
where the time goes in v1:
time: 573 us; the launch traced here: 563 us
  waiting for transfers between devices  331 us (58%)
  local copies, waits for them, and re-layouts  78.5 us (14%)
  matrix products  61.6 us (11%)
  starting transfers between devices  46.7 us (8%)
  other arithmetic  34.2 us (6%)
  between operations  11 us (2%)
    ppermute x3, waiting for transfers between devices, shards(): from_left = lax.ppermute(send_r, 'dp', [(i, i + 1) for i in range(step)])  141 us
    all_to_all x2, waiting for transfers between devices, to_owners(): return lax.all_to_all(sent, 'dp', split_axis=0, concat_axis=0, tiled=True)  78.4 us
    ppermute x6, waiting for transfers between devices, sum_over_mp(): x = x + lax.ppermute(x, 'mp', [(i, i ^ bit) for i in range(size)])  45.9 us
    dot_general x4, matrix products, shards(): lax.dot_general(rows, down_weight, (((1,), (1,)), ((), ())), preferred_el...  34.9 us
    unnamed x36, local copies, waits for them, and re-layouts  26.8 us
    all_to_all x1, waiting for transfers between devices, shards(): lax.all_to_all(by_tokens, 'dp', split_axis=0, concat_axis=0, tiled=True)  26.1 us
    all_to_all x1, waiting for transfers between devices, shards(): lax.all_to_all(output_gradient.reshape(members, share, d_local), 'mp', sp...  19.4 us
    all_to_all x2, starting transfers between devices, to_owners(): return lax.all_to_all(sent, 'dp', split_axis=0, concat_axis=0, tiled=True)  14.8 us
  transfers between devices with their start and end apart: 24, of which 15 were waited for; matrix products, arithmetic and copies ran while one was open for 16% of the time, Pallas kernels for 0%

profile of v1, /device:TPU:10, one launch (start us, length us, event | category | flops | bytes accessed | tf_op | source)
XLA Modules:
  0.0 562.8 jit_solution(14122157061356391053)
XLA Ops:
  5.8 19.4 %all-to-all-done = bf16[8,96,1024]{2,1,0:T(8,128)(2,1)} async-done(((bf16[8,96,1024]{2,1,0:T(8,128)(2,1)}), bf16[8,96,1024]{2,1,0:T(8,128)(2,1)}, u32[]{:S(2)}, u32[]{:S(2)}) %all-to-all-start) | async-done | bytes 1572896 | tf_op jit(solution)/shard_map/all_to_all | solution.py:108
  35.9 5.3 all-to-all-start.1
  49.0 26.1 %all-to-all-done.1 = bf16[4,96,2048]{2,1,0:T(8,128)(2,1)} async-done(((bf16[4,96,2048]{2,1,0:T(8,128)(2,1)}), bf16[4,96,2048]{2,1,0:T(8,128)(2,1)}, u32[]{:S(2)}, u32[]{:S(2)}) %all-to-all-start.1) | async-done | bytes 1572896 | tf_op jit(solution)/shard_map/all_to_all | solution.py:112
  75.1 8.2 %all-to-all-start.2 = ((bf16[4,3,64,1024]{3,2,1,0:T(8,128)(2,1)}), bf16[4,3,64,1024]{3,2,1,0:T(8,128)(2,1)}, u32[]{:S(2)}, u32[]{:S(2)}) async-start(bf16[4,3,64,1024]{3,2,1,0:T(8,128)(2,1)} %select_select_fusion.1), calls=%async_computation.2 | async-start | bytes 3145728 | tf_op jit(solution)/shard_map/all_to_all | solution.py:104
  94.2 22.2 %all-to-all-done.2 = bf16[4,3,64,1024]{3,2,1,0:T(8,128)(2,1)} async-done(((bf16[4,3,64,1024]{3,2,1,0:T(8,128)(2,1)}), bf16[4,3,64,1024]{3,2,1,0:T(8,128)(2,1)}, u32[]{:S(2)}, u32[]{:S(2)}) %all-to-all-start.2) | async-done | bytes 1572896 | tf_op jit(solution)/shard_map/all_to_all | solution.py:104
  128.1 10.7 %collective-permute-done.9 = f32[4,3,64,64]{3,2,1,0:T(8,128)S(1)} collective-permute-done((f32[4,3,64,64]{3,2,1,0:T(8,128)S(1)}, f32[4,3,64,64]{3,2,1,0:T(8,128)S(1)}, u32[]{:S(2)}, u32[]{:S(2)}) %collective-permute-start.9) | collective-permute-done | bytes 196640 | tf_op jit(solution)/shard_map/ppermute | solution.py:19
  140.7 24.4 %collective-permute-done.10 = f32[4,3,64,64]{3,2,1,0:T(8,128)S(1)} collective-permute-done((f32[4,3,64,64]{3,2,1,0:T(8,128)S(1)}, f32[4,3,64,64]{3,2,1,0:T(8,128)S(1)}, u32[]{:S(2)}, u32[]{:S(2)}) %collective-permute-start.10) | collective-permute-done | bytes 196640 | tf_op jit(solution)/shard_map/ppermute | solution.py:19
  182.7 12.6 %collective-permute-done.5 = bf16[2,96,2048]{2,1,0:T(8,128)(2,1)S(1)} collective-permute-done((bf16[2,96,2048]{2,1,0:T(8,128)(2,1)S(1)}, bf16[2,96,2048]{2,1,0:T(8,128)(2,1)S(1)}, u32[]{:S(2)}, u32[]{:S(2)}) %collective-permute-start.5) | collective-permute-done | bytes 786464 | tf_op jit(solution)/shard_map/ppermute | solution.py:30
  204.6 11.0 %gather_fusion = bf16[8,4,96,2048]{3,2,1,0:T(8,128)(2,1)} fusion(bf16[8,4,96,2048]{3,2,1,0:T(8,128)(2,1)} %bitcast_dynamic-update-slice_fusion, s32[1024]{0:T(1024)S(1)} %pad_clamp_fusion.2), kind=kCustom, calls=%fused_computation | custom fusion | bytes 25165856 | tf_op jit(solution)/shard_map/jit(_take)/gather | solution.py:38
  215.6 6.8 %broadcast_select_fusion = bf16[8,4,96,2048]{3,2,1,0:T(8,128)(2,1)S(1)} fusion(bf16[8,4,96,2048]{3,2,1,0:T(8,128)(2,1)} %gather_fusion, pred[8]{0:T(512)(128)(4,1)S(1)} %compare_and_fusion.2), kind=kLoop, calls=%fused_computation.5 | loop fusion | flops 6291456 | bytes 25165832 | tf_op jit(solution)/shard_map/jit(_take)/select_n | solution.py:38
  226.5 5.9 %fusion.62 = f32[768,1792]{1,0:T(8,128)S(1)} fusion(bf16[768,2048]{1,0:T(8,128)(2,1)S(1)} %bitcast.140, bf16[1792,2048]{1,0:T(8,128)(2,1)S(1)} %bitcast.144), kind=kOutput, calls=%fused_computation.141 | convolution fusion | flops 5637144576 | bytes 15990784 | tf_op jit(solution)/shard_map/dot_general | solution.py:151
  241.6 9.9 %fusion.61 = f32[768,1792]{1,0:T(8,128)S(1)} fusion(bf16[768,2048]{1,0:T(8,128)(2,1)} %bitcast.139, bf16[1792,2048]{1,0:T(8,128)(2,1)} %param.15), kind=kOutput, calls=%fused_computation.140 | convolution fusion | flops 5637144576 | bytes 15990784 | tf_op jit(solution)/shard_map/dot_general | solution.py:151
  251.5 49.8 %collective-permute-done.11 = bf16[768,1792]{1,0:T(8,128)(2,1)} collective-permute-done((bf16[768,1792]{1,0:T(8,128)(2,1)}, bf16[768,1792]{1,0:T(8,128)(2,1)}, u32[]{:S(2)}, u32[]{:S(2)}) %collective-permute-start.11) | collective-permute-done | bytes 2752544 | tf_op jit(solution)/shard_map/ppermute | solution.py:173
  301.3 7.2 %add_convert_fusion.3 = (bf16[768,1792]{1,0:T(8,128)(2,1)}, bf16[768,1792]{1,0:T(8,128)(2,1)}, bf16[768,1792]{1,0:T(8,128)(2,1)}) fusion(bf16[768,1792]{1,0:T(8,128)(2,1)} %collective-permute-done.11, bf16[768,1792]{1,0:T(8,128)(2,1)} %add_convert_fusion.4, pred[]{:T(512)} %bitcast.33, bf16[768,1792]{1,0:T(8,128)(2,1)} %collective-permute-done.14, ...), kind=kOutput, calls=%fused_computation.24 | convolution fusion | flops 544997376 | bytes 23005184 | tf_op jit(solution)/shard_map/dot_general | solution.py:154
  315.8 10.1 %fusion.60 = f32[768,1792]{1,0:T(8,128)S(1)} fusion(bf16[768,2048]{1,0:T(8,128)(2,1)} %bitcast.138, bf16[1792,2048]{1,0:T(8,128)(2,1)} %param.15), kind=kOutput, calls=%fused_computation.139 | convolution fusion | flops 5637144576 | bytes 15990784 | tf_op jit(solution)/shard_map/dot_general | solution.py:151
  326.8 45.6 %collective-permute-done.12 = bf16[768,1792]{1,0:T(8,128)(2,1)} collective-permute-done((bf16[768,1792]{1,0:T(8,128)(2,1)}, bf16[768,1792]{1,0:T(8,128)(2,1)}, u32[]{:S(2)}, u32[]{:S(2)}) %collective-permute-start.12) | collective-permute-done | bytes 2752544 | tf_op jit(solution)/shard_map/ppermute | solution.py:173
  376.5 6.0 %add_convert_fusion.2 = (bf16[768,1792]{1,0:T(8,128)(2,1)}, bf16[768,1792]{1,0:T(8,128)(2,1)S(1)}) fusion(bf16[768,1792]{1,0:T(8,128)(2,1)} %collective-permute-done.12, bf16[768,1792]{1,0:T(8,128)(2,1)S(1)} %add_convert_fusion.6, bf16[768,1792]{1,0:T(8,128)(2,1)S(1)} %copy-done.2, pred[]{:T(512)} %bitcast.24, bf16[768,1792]{1,0:T(8,128)(2,1)} %collective-permute-done.15), kind=kLoop, calls=%fused_computation.23 | loop fusion | flops 12386304 | bytes 16515073 | tf_op jit(solution)/shard_map/convert_element_type | solution.py:171
  388.7 9.0 %fusion.59 = f32[768,1792]{1,0:T(8,128)S(1)} fusion(bf16[768,2048]{1,0:T(8,128)(2,1)S(1)} %bitcast.137, bf16[1792,2048]{1,0:T(8,128)(2,1)} %param.15), kind=kOutput, calls=%fused_computation.138 | convolution fusion | flops 5637144576 | bytes 15990784 | tf_op jit(solution)/shard_map/dot_general | solution.py:151
  398.7 46.0 %collective-permute-done.13 = bf16[768,1792]{1,0:T(8,128)(2,1)S(1)} collective-permute-done((bf16[768,1792]{1,0:T(8,128)(2,1)}, bf16[768,1792]{1,0:T(8,128)(2,1)S(1)}, u32[]{:S(2)}, u32[]{:S(2)}) %collective-permute-start.13) | collective-permute-done | bytes 2752544 | tf_op jit(solution)/shard_map/ppermute | solution.py:173
  446.6 7.8 %multiply_convert_fusion = (bf16[768,1792]{1,0:T(8,128)(2,1)}, bf16[768,1792]{1,0:T(8,128)(2,1)}, bf16[768,1792]{1,0:T(8,128)(2,1)}) fusion(bf16[768,1792]{1,0:T(8,128)(2,1)} %collective-permute-done.16, bf16[768,1792]{1,0:T(8,128)(2,1)S(1)} %collective-permute-done.13, bf16[768,1792]{1,0:T(8,128)(2,1)S(1)} %add_convert_fusion.7, ...), kind=kLoop, calls=%fused_computation.19 | loop fusion | flops 30277632 | bytes 22020096 | tf_op jit(solution)/shard_map/convert_element_type | solution.py:183
  462.2 6.7 %all-to-all-start.3 = ((bf16[4,3,64,1792]{3,2,1,0:T(8,128)(2,1)}), bf16[4,3,64,1792]{3,2,1,0:T(8,128)(2,1)}, u32[]{:S(2)}, u32[]{:S(2)}) async-start(bf16[4,3,64,1792]{3,2,1,0:T(8,128)(2,1)} %select_select_fusion), calls=%async_computation.3 | async-start | bytes 5505024 | tf_op jit(solution)/shard_map/all_to_all | solution.py:104
  469.3 56.2 %all-to-all-done.3 = bf16[4,3,64,1792]{3,2,1,0:T(8,128)(2,1)} async-done(((bf16[4,3,64,1792]{3,2,1,0:T(8,128)(2,1)}), bf16[4,3,64,1792]{3,2,1,0:T(8,128)(2,1)}, u32[]{:S(2)}, u32[]{:S(2)}) %all-to-all-start.3) | async-done | bytes 2752544 | tf_op jit(solution)/shard_map/all_to_all | solution.py:104
  533.9 9.6 %collective-permute-done.18 = f32[4,3,64,64]{3,2,1,0:T(8,128)S(1)} collective-permute-done((f32[4,3,64,64]{3,2,1,0:T(8,128)S(1)}, f32[4,3,64,64]{3,2,1,0:T(8,128)S(1)}, u32[]{:S(2)}, u32[]{:S(2)}) %collective-permute-start.18) | collective-permute-done | bytes 196640 | tf_op jit(solution)/shard_map/ppermute | solution.py:19
  545.9 7.3 %copy.83 = f32[16,64,1792]{2,1,0:T(8,128)} copy(f32[16,64,1792]{2,0,1:T(8,128)S(1)} %fusion.8) | data formatting | bytes 14680064
  (145 shorter events, 128.3 us)
Async XLA Ops:
  0.7 24.5 %all-to-all-start = ((bf16[8,96,1024]{2,1,0:T(8,128)(2,1)}), bf16[8,96,1024]{2,1,0:T(8,128)(2,1)}, u32[]{:S(2)}, u32[]{:S(2)}) async-start(bf16[8,96,1024]{2,1,0:T(8,128)(2,1)} %bitcast.133), calls=%async_computation | async-start | bytes 3145728 | tf_op jit(solution)/shard_map/all_to_all | solution.py:108
  35.9 39.2 %all-to-all-start.1 = ((bf16[4,96,2048]{2,1,0:T(8,128)(2,1)}), bf16[4,96,2048]{2,1,0:T(8,128)(2,1)}, u32[]{:S(2)}, u32[]{:S(2)}) async-start(bf16[4,96,2048]{2,1,0:T(8,128)(2,1)} %bitcast.132), calls=%async_computation.1 | async-start | bytes 3145728 | tf_op jit(solution)/shard_map/all_to_all | solution.py:112
  75.1 41.4 %all-to-all-start.2 = ((bf16[4,3,64,1024]{3,2,1,0:T(8,128)(2,1)}), bf16[4,3,64,1024]{3,2,1,0:T(8,128)(2,1)}, u32[]{:S(2)}, u32[]{:S(2)}) async-start(bf16[4,3,64,1024]{3,2,1,0:T(8,128)(2,1)} %select_select_fusion.1), calls=%async_computation.2 | async-start | bytes 3145728 | tf_op jit(solution)/shard_map/all_to_all | solution.py:104
  91.7 79.5 %collective-permute-start.1 = (bf16[4,96,2048]{2,1,0:T(8,128)(2,1)}, bf16[4,96,2048]{2,1,0:T(8,128)(2,1)}, u32[]{:S(2)}, u32[]{:S(2)}) collective-permute-start(bf16[4,96,2048]{2,1,0:T(8,128)(2,1)} %all-to-all-done.1), channel_id=1, source_target_pairs={{0,2},{1,3},{2,0},{3,1},{4,6},{5,7},{6,4},{7,5},{8,10},{9,11},{10,... | collective-permute-start | bytes 4718600 | tf_op jit(solution)/shard_map/ppermute | solution.py:30
  119.0 9.0 %collective-permute-start.8 = (f32[4,3,64,64]{3,2,1,0:T(8,128)S(1)}, f32[4,3,64,64]{3,2,1,0:T(8,128)S(1)}, u32[]{:S(2)}, u32[]{:S(2)}) collective-permute-start(f32[4,3,64,64]{3,2,1,0:T(8,128)S(1)} %fusion.15), channel_id=1, source_target_pairs={{0,1},{1,0},{2,3},{3,2},{4,5},{5,4},{6,7},{7,6},{8,9},{9,8},{10,11... | collective-permute-start | bytes 589832 | tf_op jit(solution)/shard_map/ppermute | solution.py:19
  119.7 57.5 %collective-permute-start = (bf16[4,96,2048]{2,1,0:T(8,128)(2,1)}, bf16[4,96,2048]{2,1,0:T(8,128)(2,1)}, u32[]{:S(2)}, u32[]{:S(2)}) collective-permute-start(bf16[4,96,2048]{2,1,0:T(8,128)(2,1)} %all-to-all-done.1), channel_id=1, source_target_pairs={{0,1},{1,0},{2,3},{3,2},{4,5},{5,4},{6,7},{7,6},{8,9},{9,8},{10,11... | collective-permute-start | bytes 4718600 | tf_op jit(solution)/shard_map/ppermute | solution.py:30
  120.2 53.9 %collective-permute-start.3 = (bf16[4,96,2048]{2,1,0:T(8,128)(2,1)}, bf16[4,96,2048]{2,1,0:T(8,128)(2,1)}, u32[]{:S(2)}, u32[]{:S(2)}) collective-permute-start(bf16[4,96,2048]{2,1,0:T(8,128)(2,1)} %all-to-all-done.1), channel_id=1, source_target_pairs={{0,4},{1,5},{2,6},{3,7},{4,0},{5,1},{6,2},{7,3},{8,12},{9,13},{10,... | collective-permute-start | bytes 4718600 | tf_op jit(solution)/shard_map/ppermute | solution.py:30
  128.0 10.8 %collective-permute-start.9 = (f32[4,3,64,64]{3,2,1,0:T(8,128)S(1)}, f32[4,3,64,64]{3,2,1,0:T(8,128)S(1)}, u32[]{:S(2)}, u32[]{:S(2)}) collective-permute-start(f32[4,3,64,64]{3,2,1,0:T(8,128)S(1)} %add.173), channel_id=1, source_target_pairs={{0,2},{1,3},{2,0},{3,1},{4,6},{5,7},{6,4},{7,5},{8,10},{9,11},{10,... | collective-permute-start | bytes 589832 | tf_op jit(solution)/shard_map/ppermute | solution.py:19
  138.9 26.2 %collective-permute-start.10 = (f32[4,3,64,64]{3,2,1,0:T(8,128)S(1)}, f32[4,3,64,64]{3,2,1,0:T(8,128)S(1)}, u32[]{:S(2)}, u32[]{:S(2)}) collective-permute-start(f32[4,3,64,64]{3,2,1,0:T(8,128)S(1)} %add.174), channel_id=1, source_target_pairs={{0,4},{1,5},{2,6},{3,7},{4,0},{5,1},{6,2},{7,3},{8,12},{9,13},{10,... | collective-permute-start | bytes 589832 | tf_op jit(solution)/shard_map/ppermute | solution.py:19
  171.2 25.5 %collective-permute-start.2 = (bf16[4,96,2048]{2,1,0:T(8,128)(2,1)}, bf16[4,96,2048]{2,1,0:T(8,128)(2,1)S(1)}, u32[]{:S(2)}, u32[]{:S(2)}) collective-permute-start(bf16[4,96,2048]{2,1,0:T(8,128)(2,1)} %collective-permute-done.1), channel_id=1, source_target_pairs={{0,1},{1,0},{2,3},{3,2},{4,5},{5,4},{6,7},{7,6},{8,9},{9,8},{10,11... | collective-permute-start | bytes 4718600 | tf_op jit(solution)/shard_map/ppermute | solution.py:30
  175.3 20.0 %collective-permute-start.5 = (bf16[2,96,2048]{2,1,0:T(8,128)(2,1)S(1)}, bf16[2,96,2048]{2,1,0:T(8,128)(2,1)S(1)}, u32[]{:S(2)}, u32[]{:S(2)}) collective-permute-start(bf16[2,96,2048]{2,1,0:T(8,128)(2,1)S(1)} %slice.38), channel_id=1, source_target_pairs={{0,2},{1,3},{2,0},{3,1},{4,6},{5,7},{6,4},{7,5},{8,10},{9,11},{10,... | collective-permute-start | bytes 2359304 | tf_op jit(solution)/shard_map/ppermute | solution.py:30
  176.5 20.0 %collective-permute-start.6 = (bf16[2,96,2048]{2,1,0:T(8,128)(2,1)S(1)}, bf16[2,96,2048]{2,1,0:T(8,128)(2,1)S(1)}, u32[]{:S(2)}, u32[]{:S(2)}) collective-permute-start(bf16[2,96,2048]{2,1,0:T(8,128)(2,1)S(1)} %slice.39), channel_id=1, source_target_pairs={{0,4},{1,5},{2,6},{3,7},{4,0},{5,1},{6,2},{7,3},{8,12},{9,13},{10,... | collective-permute-start | bytes 2359304 | tf_op jit(solution)/shard_map/ppermute | solution.py:30
  176.9 23.9 %collective-permute-start.4 = (bf16[4,96,2048]{2,1,0:T(8,128)(2,1)}, bf16[4,96,2048]{2,1,0:T(8,128)(2,1)S(1)}, u32[]{:S(2)}, u32[]{:S(2)}) collective-permute-start(bf16[4,96,2048]{2,1,0:T(8,128)(2,1)} %collective-permute-done.3), channel_id=1, source_target_pairs={{0,1},{1,0},{2,3},{3,2},{4,5},{5,4},{6,7},{7,6},{8,9},{9,8},{10,11... | collective-permute-start | bytes 4718600 | tf_op jit(solution)/shard_map/ppermute | solution.py:30
  196.6 6.7 %collective-permute-start.7 = (bf16[4,96,2048]{2,1,0:T(8,128)(2,1)S(1)}, bf16[4,96,2048]{2,1,0:T(8,128)(2,1)S(1)}, u32[]{:S(2)}, u32[]{:S(2)}) collective-permute-start(bf16[4,96,2048]{2,1,0:T(8,128)(2,1)S(1)} %constant_dynamic-update-slice_fusion), channel_id=1, source_target_pairs={{0,1},{1,0},{2,3},{3,2},{4,5},{5,4},{6,7},{7,6},{8,9},{9,8},{10,11... | collective-permute-start | bytes 4718600 | tf_op jit(solution)/shard_map/ppermute | solution.py:30
  236.0 65.3 %collective-permute-start.11 = (bf16[768,1792]{1,0:T(8,128)(2,1)}, bf16[768,1792]{1,0:T(8,128)(2,1)}, u32[]{:S(2)}, u32[]{:S(2)}) collective-permute-start(bf16[768,1792]{1,0:T(8,128)(2,1)} %add_convert_fusion.4), channel_id=1, source_target_pairs={{0,8},{1,9},{2,10},{3,11},{4,12},{5,13},{6,14},{7,15}} | collective-permute-start | bytes 8257544 | tf_op jit(solution)/shard_map/ppermute | solution.py:173
  237.3 64.0 %collective-permute-start.14 = (bf16[768,1792]{1,0:T(8,128)(2,1)}, bf16[768,1792]{1,0:T(8,128)(2,1)}, u32[]{:S(2)}, u32[]{:S(2)}) collective-permute-start(bf16[768,1792]{1,0:T(8,128)(2,1)} %add_convert_fusion.4), channel_id=1, source_target_pairs={{24,16},{25,17},{26,18},{27,19},{28,20},{29,21},{30,22},{31,23}} | collective-permute-start | bytes 8257544 | tf_op jit(solution)/shard_map/ppermute | solution.py:174
  308.5 63.9 %collective-permute-start.12 = (bf16[768,1792]{1,0:T(8,128)(2,1)}, bf16[768,1792]{1,0:T(8,128)(2,1)}, u32[]{:S(2)}, u32[]{:S(2)}) collective-permute-start(bf16[768,1792]{1,0:T(8,128)(2,1)} %get-tuple-element.33), channel_id=1, source_target_pairs={{0,8},{8,16},{1,9},{9,17},{2,10},{10,18},{3,11},{11,19},{4,12},{12... | collective-permute-start | bytes 8257544 | tf_op jit(solution)/shard_map/ppermute | solution.py:173
  313.2 63.3 %collective-permute-start.15 = (bf16[768,1792]{1,0:T(8,128)(2,1)}, bf16[768,1792]{1,0:T(8,128)(2,1)}, u32[]{:S(2)}, u32[]{:S(2)}) collective-permute-start(bf16[768,1792]{1,0:T(8,128)(2,1)} %get-tuple-element.34), channel_id=1, source_target_pairs={{24,16},{16,8},{25,17},{17,9},{26,18},{18,10},{27,19},{19,11},{28,... | collective-permute-start | bytes 8257544 | tf_op jit(solution)/shard_map/ppermute | solution.py:174
  382.5 62.3 %collective-permute-start.13 = (bf16[768,1792]{1,0:T(8,128)(2,1)}, bf16[768,1792]{1,0:T(8,128)(2,1)S(1)}, u32[]{:S(2)}, u32[]{:S(2)}) collective-permute-start(bf16[768,1792]{1,0:T(8,128)(2,1)} %get-tuple-element.35), channel_id=1, source_target_pairs={{0,8},{8,16},{16,24},{1,9},{9,17},{17,25},{2,10},{10,18},{18,26},{... | collective-permute-start | bytes 8257544 | tf_op jit(solution)/shard_map/ppermute | solution.py:173
  384.4 62.2 %collective-permute-start.16 = (bf16[768,1792]{1,0:T(8,128)(2,1)S(1)}, bf16[768,1792]{1,0:T(8,128)(2,1)}, u32[]{:S(2)}, u32[]{:S(2)}) collective-permute-start(bf16[768,1792]{1,0:T(8,128)(2,1)S(1)} %get-tuple-element.36), channel_id=1, source_target_pairs={{24,16},{16,8},{8,0},{25,17},{17,9},{9,1},{26,18},{18,10},{10,2},{... | collective-permute-start | bytes 8257544 | tf_op jit(solution)/shard_map/ppermute | solution.py:174
  462.2 63.3 %all-to-all-start.3 = ((bf16[4,3,64,1792]{3,2,1,0:T(8,128)(2,1)}), bf16[4,3,64,1792]{3,2,1,0:T(8,128)(2,1)}, u32[]{:S(2)}, u32[]{:S(2)}) async-start(bf16[4,3,64,1792]{3,2,1,0:T(8,128)(2,1)} %select_select_fusion), calls=%async_computation.3 | async-start | bytes 5505024 | tf_op jit(solution)/shard_map/all_to_all | solution.py:104
  529.0 2.8 collective-permute-start.17
  531.9 11.6 %collective-permute-start.18 = (f32[4,3,64,64]{3,2,1,0:T(8,128)S(1)}, f32[4,3,64,64]{3,2,1,0:T(8,128)S(1)}, u32[]{:S(2)}, u32[]{:S(2)}) collective-permute-start(f32[4,3,64,64]{3,2,1,0:T(8,128)S(1)} %add.194), channel_id=1, source_target_pairs={{0,2},{1,3},{2,0},{3,1},{4,6},{5,7},{6,4},{7,5},{8,10},{9,11},{10,... | collective-permute-start | bytes 589832 | tf_op jit(solution)/shard_map/ppermute | solution.py:19
  543.6 10.9 %collective-permute-start.19 = (f32[4,3,64,64]{3,2,1,0:T(8,128)S(1)}, f32[4,3,64,64]{3,2,1,0:T(8,128)S(1)}, u32[]{:S(2)}, u32[]{:S(2)}) collective-permute-start(f32[4,3,64,64]{3,2,1,0:T(8,128)S(1)} %add.195), channel_id=1, source_target_pairs={{0,4},{1,5},{2,6},{3,7},{4,0},{5,1},{6,2},{7,3},{8,12},{9,13},{10,... | collective-permute-start | bytes 589832 | tf_op jit(solution)/shard_map/ppermute | solution.py:19
  (13 other events, 313.3 us)

commit v2 on v1

v2 whole, which is shorter than its diff:
```python
import functools

import jax
import jax.numpy as jnp
from jax import lax
from jax.experimental import pallas as pl
from jax.experimental.pallas import tpu as pltpu
from jax.sharding import PartitionSpec as P

ADAPTER_RANK = 64
BLK = 64
VMEM_BYTES = 48 * 1024 * 1024


adapter_scale = 2.0


def sum_over_mp(x):
    size = lax.axis_size("mp")
    if size & (size - 1):
        return lax.psum(x, "mp")
    bit = 1
    while bit < size:
        x = x + lax.ppermute(x, "mp", [(i, i ^ bit) for i in range(size)])
        bit *= 2
    return x


def exchange_over_dp(parts):
    size = lax.axis_size("dp")
    me = lax.axis_index("dp")
    if size > 4:
        return lax.all_to_all(parts, "dp", split_axis=0, concat_axis=0, tiled=True)
    got = [lax.dynamic_index_in_dim(parts, me, 0, keepdims=False)]
    for shift in range(1, size):
        sent = lax.dynamic_index_in_dim(parts, (me + shift) % size, 0, keepdims=False)
        got.append(lax.ppermute(sent, "dp", [(i, (i + shift) % size) for i in range(size)]))
    index = (me - jnp.arange(size, dtype=jnp.int32)) % size
    return jnp.take(jnp.stack(got), index, axis=0)


def slices_to_planes(out, groups, members):
    tok_rows, d_local = out.shape
    share = tok_rows // members
    me = lax.axis_index("mp")
    my_group = lax.axis_index("dp")
    if members % groups or members > 8:
        moved = lax.all_to_all(
            out.reshape(members, share, d_local), "mp", split_axis=0, concat_axis=0, tiled=True
        )
        moved = moved.transpose(1, 0, 2).reshape(share, groups, -1).transpose(1, 0, 2)
        return lax.all_to_all(moved, "dp", split_axis=0, concat_axis=0, tiled=True)
    per = members // groups
    got = []
    chunks = out.reshape(members, share, d_local)
    for turn in range(members):
        pairs = []
        for g in range(groups):
            for m in range(members):
                to = (g * per + m % per + turn) % members
                pairs.append((g * members + m, (m // per) * members + to))
        to = (my_group * per + me % per + turn) % members
        sent = lax.dynamic_index_in_dim(chunks, to, 0, keepdims=False)
        got.append(lax.ppermute(sent, ("dp", "mp"), pairs))
    index = (me - jnp.arange(members, dtype=jnp.int32)) % members
    ordered = jnp.take(jnp.stack(got), index, axis=0)
    return (
        ordered.reshape(groups, per, share, d_local)
        .transpose(0, 2, 1, 3)
        .reshape(groups, share, per * d_local)
    )


def gather_over_mp(x):
    size = lax.axis_size("mp")
    me = lax.axis_index("mp")
    groups, share, width = x.shape
    if size != 8 or share % 32:
        whole = lax.all_gather(x, "mp", axis=1, tiled=True)
        return [whole], [jnp.zeros((), jnp.int32)]

    def swap(v, bits):
        return lax.ppermute(v, "mp", [(i, i ^ bits) for i in range(size)])

    half = share // 2
    x2, x4 = swap(x, 2), swap(x, 4)
    x1 = swap(x, 1)
    x6a, x6b = swap(x4[:, :half], 2), swap(x2[:, half:], 4)
    x3, x5 = swap(x2, 1), swap(x4, 1)
    x7a, x7b = swap(x6a, 1), swap(x6b, 1)
    pieces = [x, x1, x2, x3, x4, x5, x6a, x6b, x7a, x7b]
    owners = [0, 1, 2, 3, 4, 5, 6, 6, 7, 7]
    extra = [0, 0, 0, 0, 0, 0, 0, half, 0, half]
    return pieces, [(me ^ k) * share + e for k, e in zip(owners, extra)]


def partial_kernel(count, aligned, info, *refs):
    pieces, (w_ref, s_ref, a_ref), outs, rows_ref = (
        refs[:count],
        refs[count : count + 3],
        refs[count + 3 : -1],
        refs[-1],
    )

    @pl.when(pl.program_id(0) == 0)
    def _():
        for k, piece in enumerate(pieces):
            rows = piece.shape[1]
            if count == 1:
                rows_ref[...] = piece[0]
            else:
                start = pl.multiple_of(info[1 + k], aligned)
                rows_ref[pl.ds(start, rows), :] = piece[0]

    half = outs[0].shape[0]
    for h, out in enumerate(outs):
        span = slice(h * half, (h + 1) * half)
        total = lax.dot_general(
            rows_ref[span, :], w_ref[...], (((1,), (1,)), ((), ())), preferred_element_type=jnp.float32
        )
        total += jnp.dot(s_ref[0, span, :], a_ref[0], preferred_element_type=jnp.float32)
        out[...] = total.astype(out.dtype)


def partial_sums(target, pieces, starts, weight, spread, a_rows, halves, dtype):
    ff_local, width = weight.shape
    tok_rows, side = spread.shape[1:]
    tile = 256 if ff_local % 256 == 0 else ff_local
    info = jnp.stack([target, *starts]).astype(jnp.int32)
    aligned = functools.reduce(
        lambda a, b: a if b % a == 0 else 16, [p.shape[1] for p in pieces], 16
    )
    return pl.pallas_call(
        functools.partial(partial_kernel, len(pieces), aligned),
        grid_spec=pltpu.PrefetchScalarGridSpec(
            num_scalar_prefetch=1,
            grid=(ff_local // tile,),
            in_specs=[
                pl.BlockSpec((1, p.shape[1], width), lambda n, info: (info[0], 0, 0)) for p in pieces
            ]
            + [
                pl.BlockSpec((tile, width), lambda n, info: (n, 0)),
                pl.BlockSpec((1, tok_rows, side), lambda n, info: (info[0], 0, 0)),
                pl.BlockSpec((1, side, tile), lambda n, info: (info[0], 0, n)),
            ],
            out_specs=[
                pl.BlockSpec((tok_rows // halves, tile), lambda n, info: (0, n))
                for _ in range(halves)
            ],
            scratch_shapes=[pltpu.VMEM((tok_rows, width), jnp.bfloat16)],
        ),
        out_shape=[
            jax.ShapeDtypeStruct((tok_rows // halves, ff_local), dtype) for _ in range(halves)
        ],
        compiler_params=pltpu.CompilerParams(vmem_limit_bytes=VMEM_BYTES),
        name="partial_sums",
    )(info, *pieces, weight, spread, a_rows)


def finish_kernel(own, left, right, gate, up, *rest):
    d_gate, d_up = rest[-2:]
    d_hidden = own[...] + left[...].astype(jnp.float32) + right[...].astype(jnp.float32)
    gate_float = gate[...].astype(jnp.float32)
    up_float = up[...].astype(jnp.float32)
    squash = jax.nn.sigmoid(gate_float)
    d_gate[...] = (d_hidden * up_float * squash * (1.0 + gate_float * (1.0 - squash))).astype(
        d_gate.dtype
    )
    d_up[...] = (d_hidden * (gate_float * squash)).astype(d_up.dtype)


def finish(own, left, right, gate, up, part, earlier):
    rows, ff_local = own.shape
    step = 64 if rows % 64 == 0 else rows
    steps = rows // step
    here = pl.BlockSpec((step, ff_local), lambda i: (i, 0))
    there = pl.BlockSpec((step, ff_local), lambda i: (part * steps + i, 0))
    before = [] if earlier is None else list(earlier)
    return pl.pallas_call(
        finish_kernel,
        grid=(steps,),
        in_specs=[here, here, here, there, there] + [pl.BlockSpec(memory_space=pl.ANY)] * len(before),
        out_specs=[there, there],
        out_shape=[jax.ShapeDtypeStruct(gate.shape, gate.dtype) for _ in range(2)],
        input_output_aliases={5: 0, 6: 1} if before else {},
        compiler_params=pltpu.CompilerParams(vmem_limit_bytes=VMEM_BYTES),
        name="finish",
    )(own, left, right, gate, up, *before)


def shards(
    output_gradient,
    saved_gate_value,
    saved_up_value,
    down_weight,
    adapter_first_weight,
    adapter_second_weight,
    adapter_of_block,
    slot_of_adapter,
):
    groups = lax.axis_size("dp")
    members = lax.axis_size("mp")
    my_group = lax.axis_index("dp")
    tok_rows = output_gradient.shape[0]
    blocks = tok_rows // BLK
    owner_totals = adapter_first_weight.shape[0]
    adapters = slot_of_adapter.shape[0]
    ff_local = saved_gate_value.shape[1]
    d_local = output_gradient.shape[1]
    capacity = (blocks + groups - 1) // groups
    halves = 2

    by_slice = slices_to_planes(output_gradient, groups, members)
    pieces, starts = gather_over_mp(by_slice)

    match_table = adapter_of_block[:, None] == jnp.arange(adapters, dtype=jnp.int32)[None, :]
    slot_of_block = jnp.sum(jnp.where(match_table, slot_of_adapter[None, :], 0), axis=1)
    owners = (slot_of_block // owner_totals).reshape(groups, blocks)
    local_slot = (slot_of_block % owner_totals).reshape(groups, blocks)
    block_index = jnp.arange(blocks, dtype=jnp.int32)
    earlier = (owners[:, :, None] == owners[:, None, :]) & (
        block_index[None, None, :] < block_index[None, :, None]
    )
    ranks = jnp.sum(earlier.astype(jnp.int32), axis=2)
    rank_values = jnp.arange(capacity, dtype=jnp.int32)
    hits = (owners == my_group)[:, None, :] & (ranks[:, None, :] == rank_values[None, :, None])
    incoming_valid = jnp.any(hits, axis=2)
    arriving_slot = jnp.sum(jnp.where(hits, local_slot[:, None, :], 0), axis=2)
    own_owner = lax.dynamic_index_in_dim(owners, my_group, 0, keepdims=False)
    own_rank = lax.dynamic_index_in_dim(ranks, my_group, 0, keepdims=False)
    group_values = jnp.arange(groups, dtype=jnp.int32)
    route_table = (own_owner[None, None, :] == group_values[:, None, None]) & (
        own_rank[None, None, :] == rank_values[None, :, None]
    )
    route_valid = jnp.any(route_table, axis=2)
    route_block = jnp.sum(jnp.where(route_table, block_index[None, None, :], 0), axis=2)

    def to_owners(rows):
        sent = jnp.where(
            route_valid[:, :, None, None],
            jnp.take(rows.reshape(blocks, BLK, rows.shape[1]), route_block, axis=0),
            jnp.zeros((), rows.dtype),
        )
        return exchange_over_dp(sent)

    recv_o = to_owners(output_gradient)
    gate_float = saved_gate_value.astype(jnp.float32)
    hidden = (
        gate_float * jax.nn.sigmoid(gate_float) * saved_up_value.astype(jnp.float32)
    ).astype(jnp.bfloat16)
    recv_h = to_owners(hidden)

    a_here = jnp.take(adapter_first_weight, arriving_slot, axis=0)
    b_here = jnp.take(adapter_second_weight, arriving_slot, axis=0)
    back_factor = (
        adapter_scale
        * sum_over_mp(
            jnp.einsum("gctd,gcrd->gctr", recv_o, b_here, preferred_element_type=jnp.float32)
        )
    ).astype(jnp.bfloat16)
    down_factor = sum_over_mp(
        jnp.einsum("gctf,gcrf->gctr", recv_h, a_here, preferred_element_type=jnp.float32)
    ).astype(jnp.bfloat16)

    spread = jnp.where(
        hits.transpose(0, 2, 1)[:, :, None, :, None],
        back_factor.transpose(0, 2, 1, 3)[:, None],
        jnp.zeros((), jnp.bfloat16),
    ).reshape(groups, tok_rows, capacity * ADAPTER_RANK)
    a_rows = a_here.reshape(groups, capacity * ADAPTER_RANK, ff_local)

    def partial_for(target, dtype=jnp.bfloat16):
        return partial_sums(
            target, pieces, starts, down_weight, spread, a_rows, halves, dtype
        )

    def joined(a, *more):
        total = a.astype(jnp.float32)
        for m in more:
            total = total + m.astype(jnp.float32)
        return total.astype(jnp.bfloat16)

    last = groups - 1
    nothing = [jnp.zeros((tok_rows // halves, ff_local), jnp.bfloat16)] * halves
    from_left, from_right = nothing, nothing
    for step in range(1, groups):
        reach = groups - step
        to_right = jnp.where(my_group + reach <= last, my_group + reach, 0)
        to_left = jnp.where(my_group >= reach, my_group - reach, 0)
        pairs_r = [(i, i + 1) for i in range(step)]
        pairs_l = [(last - i, last - 1 - i) for i in range(step)]
        if step <= reach:
            part = partial_for(jnp.where(my_group + reach <= last, to_right, to_left))
            if step > 1:
                part = [joined(p, a, b) for p, a, b in zip(part, from_left, from_right)]
            send_r = send_l = part
        else:
            send_r = [joined(p, a) for p, a in zip(partial_for(to_right), from_left)]
            send_l = [joined(p, a) for p, a in zip(partial_for(to_left), from_right)]
        from_left = [lax.ppermute(s, "dp", pairs_r) for s in send_r]
        from_right = [lax.ppermute(s, "dp", pairs_l) for s in send_l]
    own = partial_for(my_group, jnp.float32)
    done = None
    for h in range(halves):
        done = finish(
            own[h], from_left[h], from_right[h], saved_gate_value, saved_up_value, h, done
        )
    d_gate, d_up = done

    terms_a = jnp.einsum(
        "gctr,gctf->gcrf", back_factor, recv_h, preferred_element_type=jnp.float32
    ).astype(jnp.bfloat16)
    terms_b = (
        adapter_scale
        * jnp.einsum("gctr,gctd->gcrd", down_factor, recv_o, preferred_element_type=jnp.float32)
    ).astype(jnp.bfloat16)
    flat_slot = arriving_slot.reshape(groups * capacity)
    flat_valid = incoming_valid.reshape(groups * capacity)
    selector = (
        (flat_slot[None, :] == jnp.arange(owner_totals, dtype=jnp.int32)[:, None])
        & flat_valid[None, :]
    ).astype(jnp.bfloat16)
    grad_a = jnp.dot(
        selector,
        terms_a.reshape(groups * capacity, ADAPTER_RANK * ff_local),
        preferred_element_type=jnp.float32,
    ).reshape(owner_totals, ADAPTER_RANK, ff_local)
    grad_b = jnp.dot(
        selector,
        terms_b.reshape(groups * capacity, ADAPTER_RANK * d_local),
        preferred_element_type=jnp.float32,
    ).reshape(owner_totals, ADAPTER_RANK, d_local)
    return (d_gate, d_up, grad_a, grad_b)


def solution(mesh):
    in_specs = (
        P("dp", "mp"),
        P("dp", "mp"),
        P("dp", "mp"),
        P("mp", "dp"),
        P("dp", None, "mp"),
        P("dp", None, "mp"),
        P(),
        P(),
    )
    out_specs = (P("dp", "mp"), P("dp", "mp"), P("dp", None, "mp"), P("dp", None, "mp"))
    return jax.shard_map(shards, mesh=mesh, in_specs=in_specs, out_specs=out_specs, check_vma=False)
```

time: 573 us -> 481 us (0.84); the launches traced: 563 us -> 479 us
  waiting for transfers between devices: 331 us -> 145 us
  starting transfers between devices: 46.7 us -> 152 us
  Pallas kernels: 0 us -> 69.9 us
  matrix products: 61.6 us -> 10.9 us
  local copies, waits for them, and re-layouts: 78.5 us -> 64.8 us
  between operations: 11 us -> 1.59 us
    all_to_all x4 -> x0, waiting for transfers between devices: 124 us -> none  [the longest x2 78.4 us: to_owners(): return lax.all_to_all(sent, 'dp', split_axis=0, concat_axis=0, tiled=True)]
    ppermute x6 -> x26, starting transfers between devices: 15.8 us -> 108 us  [the longest x8 65.1 us: slices_to_planes(): got.append(lax.ppermute(sent, ('dp', 'mp'), pairs))]
    pallas_call x0 -> x7, Pallas kernels: none -> 69.9 us  [the longest x5 58.1 us: partial_sums(): pl.pallas_call(functools.partial(partial_kernel, len(pieces), aligned), g...]
    dot_general x8 -> x0, matrix products: 47.5 us -> none  [the longest x4 34.9 us: shards(): lax.dot_general(rows, down_weight, (((1,), (1,)), ((), ())), preferred_el...]
    ppermute x6 -> x26, waiting for transfers between devices: 147 us -> 102 us  [the longest x6 58.3 us: exchange_over_dp(): lax.ppermute(sent, 'dp', [(i, (i + shift) % size) for i in range(size)])]
    ppermute x8 -> x9, starting transfers between devices: 1.65 us -> 36.7 us  [swap(): return lax.ppermute(v, 'mp', [(i, i ^ bits) for i in range(size)])]
    all_to_all x4 -> x0, starting transfers between devices: 25 us -> none  [the longest x2 14.8 us: to_owners(): return lax.all_to_all(sent, 'dp', split_axis=0, concat_axis=0, tiled=True)]
    ppermute x6, waiting for transfers between devices: 45.9 us -> 34.8 us  [sum_over_mp(): x = x + lax.ppermute(x, 'mp', [(i, i ^ bit) for i in range(size)])]
  transfers between devices with their start and end apart: 24 -> 41, of which waited for: 15 -> 13; matrix products, arithmetic and copies ran while one was open for 16% -> 22% of each run, Pallas kernels for 0% -> 11%
where the time goes in v2:
time: 481 us; the launch traced here: 479 us
  starting transfers between devices  152 us (32%)
  waiting for transfers between devices  145 us (30%)
  Pallas kernels  69.9 us (15%)
  local copies, waits for them, and re-layouts  64.8 us (13%)
  other arithmetic  35.1 us (7%)
  matrix products  10.9 us (2%)
    ppermute x8, starting transfers between devices, slices_to_planes(): got.append(lax.ppermute(sent, ('dp', 'mp'), pairs))  65.1 us
    ppermute x6, waiting for transfers between devices, exchange_over_dp(): lax.ppermute(sent, 'dp', [(i, (i + shift) % size) for i in range(size)])  58.3 us
    pallas_call x5, Pallas kernels, partial_sums(): pl.pallas_call(functools.partial(partial_kernel, len(pieces), aligned), g...  58.1 us
    ppermute x9, starting transfers between devices, swap(): return lax.ppermute(v, 'mp', [(i, i ^ bits) for i in range(size)])  36.7 us
    ppermute x6, waiting for transfers between devices, sum_over_mp(): x = x + lax.ppermute(x, 'mp', [(i, i ^ bit) for i in range(size)])  34.8 us
    ppermute x6, waiting for transfers between devices, shards(): from_left = [lax.ppermute(s, 'dp', pairs_r) for s in send_r]  28.4 us
    unnamed x73, local copies, waits for them, and re-layouts  23.9 us
    ppermute x6, starting transfers between devices, exchange_over_dp(): lax.ppermute(sent, 'dp', [(i, (i + shift) % size) for i in range(size)])  16.6 us
  transfers between devices with their start and end apart: 41, of which 13 were waited for; matrix products, arithmetic and copies ran while one was open for 22% of the time, Pallas kernels for 11%

profile of v2, /device:TPU:10, one launch (start us, length us, event | category | flops | bytes accessed | tf_op | source)
XLA Modules:
  0.0 479.3 jit_solution(1439461451907721478)
XLA Ops:
  22.9 12.8 %collective-permute-start.5 = (bf16[96,1024]{1,0:T(8,128)(2,1)}, bf16[96,1024]{1,0:T(8,128)(2,1)S(1)}, u32[]{:S(2)}, u32[]{:S(2)}) collective-permute-start(bf16[96,1024]{1,0:T(8,128)(2,1)} %get-tuple-element.60), channel_id=1, source_target_pairs={{0,5},{1,6},{2,13},{3,14},{4,21},{5,22},{6,29},{7,30},{8,7},{9,0},... | collective-permute-start | bytes 589832 | tf_op jit(solution)/shard_map/ppermute | solution.py:64
  37.3 25.8 %collective-permute-start.6 = (bf16[96,1024]{1,0:T(8,128)(2,1)}, bf16[96,1024]{1,0:T(8,128)(2,1)S(1)}, u32[]{:S(2)}, u32[]{:S(2)}) collective-permute-start(bf16[96,1024]{1,0:T(8,128)(2,1)} %get-tuple-element.59), channel_id=1, source_target_pairs={{0,6},{1,7},{2,14},{3,15},{4,22},{5,23},{6,30},{7,31},{8,0},{9,1},... | collective-permute-start | bytes 589832 | tf_op jit(solution)/shard_map/ppermute | solution.py:64
  64.7 15.0 %collective-permute-start.7 = (bf16[96,1024]{1,0:T(8,128)(2,1)S(1)}, bf16[96,1024]{1,0:T(8,128)(2,1)S(1)}, u32[]{:S(2)}, u32[]{:S(2)}) collective-permute-start(bf16[96,1024]{1,0:T(8,128)(2,1)S(1)} %get-tuple-element.58), channel_id=1, source_target_pairs={{0,7},{1,0},{2,15},{3,8},{4,23},{5,16},{6,31},{7,24},{8,1},{9,2},{... | collective-permute-start | bytes 589832 | tf_op jit(solution)/shard_map/ppermute | solution.py:64
  94.8 34.3 %collective-permute-start.9 = (bf16[4,96,2048]{2,1,0:T(8,128)(2,1)}, bf16[4,96,2048]{2,1,0:T(8,128)(2,1)}, u32[]{:S(2)}, u32[]{:S(2)}) collective-permute-start(bf16[4,96,2048]{2,1,0:T(8,128)(2,1)} %bitcast.63.refs_0_), channel_id=1, source_target_pairs={{0,2},{1,3},{2,0},{3,1},{4,6},{5,7},{6,4},{7,5},{8,10},{9,11},{10,... | collective-permute-start | bytes 4718600 | tf_op jit(solution)/shard_map/ppermute | solution.py:83
  141.2 29.0 %collective-permute-done.21 = f32[4,3,64,64]{3,2,1,0:T(8,128)S(1)} collective-permute-done((f32[4,3,64,64]{3,2,1,0:T(8,128)S(1)}, f32[4,3,64,64]{3,2,1,0:T(8,128)S(1)}, u32[]{:S(2)}, u32[]{:S(2)}) %collective-permute-start.21) | collective-permute-done | bytes 196640 | tf_op jit(solution)/shard_map/ppermute | solution.py:24
  187.9 5.2 %collective-permute-done.13.refs_6_ = bf16[4,48,2048]{2,1,0:T(8,128)(2,1)S(1)} collective-permute-done((bf16[4,48,2048]{2,1,0:T(8,128)(2,1)S(1)}, bf16[4,48,2048]{2,1,0:T(8,128)(2,1)S(1)}, u32[]{:S(2)}, u32[]{:S(2)}) %collective-permute-start.13) | collective-permute-done | bytes 786464 | tf_op jit(solution)/shard_map/ppermute | solution.py:83
  206.6 4.8 select_n.383
  214.0 12.1 %partial_sums.8 = (bf16[384,1792]{1,0:T(8,128)(2,1)S(1)}, bf16[384,1792]{1,0:T(8,128)(2,1)}) custom-call(s32[11]{0:T(128)S(1)} %stack.183.info, bf16[4,96,2048]{2,1,0:T(8,128)(2,1)} %bitcast.63.refs_0_, bf16[4,96,2048]{2,1,0:T(8,128)(2,1)} %collective-permute-done.8.refs_1_, bf16[4,96,2048]{2,1,0:T(8,128)(2,1)} %collective-permute-done.9.refs_2_, ...), custom_call_target="tpu_custom_call" | custom-call | tf_op jit(solution)/shard_map/partial_sums/pallas_call | solution.py:133
  234.8 7.9 %collective-permute-start.36 = (bf16[3,64,1792]{2,1,0:T(8,128)(2,1)}, bf16[3,64,1792]{2,1,0:T(8,128)(2,1)}, u32[]{:S(2)}, u32[]{:S(2)}) collective-permute-start(bf16[3,64,1792]{2,1,0:T(8,128)(2,1)} %get-tuple-element.52), channel_id=1, source_target_pairs={{0,16},{8,24},{16,0},{24,8},{1,17},{9,25},{17,1},{25,9},{2,18},{10... | collective-permute-start | bytes 2064392 | tf_op jit(solution)/shard_map/ppermute | solution.py:37
  245.7 9.1 %collective-permute-done.37 = bf16[3,64,1792]{2,1,0:T(8,128)(2,1)} collective-permute-done((bf16[3,64,1792]{2,1,0:T(8,128)(2,1)}, bf16[3,64,1792]{2,1,0:T(8,128)(2,1)}, u32[]{:S(2)}, u32[]{:S(2)}) %collective-permute-start.37) | collective-permute-done | bytes 688160 | tf_op jit(solution)/shard_map/ppermute | solution.py:37
  256.8 41.9 %collective-permute-done.36 = bf16[3,64,1792]{2,1,0:T(8,128)(2,1)} collective-permute-done((bf16[3,64,1792]{2,1,0:T(8,128)(2,1)}, bf16[3,64,1792]{2,1,0:T(8,128)(2,1)}, u32[]{:S(2)}, u32[]{:S(2)}) %collective-permute-start.36) | collective-permute-done | bytes 688160 | tf_op jit(solution)/shard_map/ppermute | solution.py:37
  299.9 7.3 %collective-permute-done.35 = bf16[3,64,1792]{2,1,0:T(8,128)(2,1)} collective-permute-done((bf16[3,64,1792]{2,1,0:T(8,128)(2,1)}, bf16[3,64,1792]{2,1,0:T(8,128)(2,1)}, u32[]{:S(2)}, u32[]{:S(2)}) %collective-permute-start.35) | collective-permute-done | bytes 688160 | tf_op jit(solution)/shard_map/ppermute | solution.py:37
  314.4 11.1 %partial_sums.7 = (bf16[384,1792]{1,0:T(8,128)(2,1)S(1)}, bf16[384,1792]{1,0:T(8,128)(2,1)S(1)}) custom-call(s32[11]{0:T(128)S(1)} %stack.181.info, bf16[4,96,2048]{2,1,0:T(8,128)(2,1)} %bitcast.63.refs_0_, bf16[4,96,2048]{2,1,0:T(8,128)(2,1)} %collective-permute-done.8.refs_1_, bf16[4,96,2048]{2,1,0:T(8,128)(2,1)} %collective-permute-done.9.refs_2_, ...), custom_call_target="tpu_custom_call" | custom-call | tf_op jit(solution)/shard_map/partial_sums/pallas_call | solution.py:133
  343.2 5.4 %collective-permute-start.31 = (bf16[384,1792]{1,0:T(8,128)(2,1)}, bf16[384,1792]{1,0:T(8,128)(2,1)S(1)}, u32[]{:S(2)}, u32[]{:S(2)}) collective-permute-start(bf16[384,1792]{1,0:T(8,128)(2,1)} %add_convert_fusion.2), channel_id=1, source_target_pairs={{0,8},{8,16},{1,9},{9,17},{2,10},{10,18},{3,11},{11,19},{4,12},{12... | collective-permute-start | bytes 4128776 | tf_op jit(solution)/shard_map/ppermute | solution.py:300
  351.1 11.1 %partial_sums.6 = (bf16[384,1792]{1,0:T(8,128)(2,1)S(1)}, bf16[384,1792]{1,0:T(8,128)(2,1)S(1)}) custom-call(s32[11]{0:T(128)S(1)} %stack.179.info, bf16[4,96,2048]{2,1,0:T(8,128)(2,1)} %bitcast.63.refs_0_, bf16[4,96,2048]{2,1,0:T(8,128)(2,1)} %collective-permute-done.8.refs_1_, bf16[4,96,2048]{2,1,0:T(8,128)(2,1)} %collective-permute-done.9.refs_2_, ...), custom_call_target="tpu_custom_call" | custom-call | tf_op jit(solution)/shard_map/partial_sums/pallas_call | solution.py:133
  362.2 11.1 %partial_sums.9 = (bf16[384,1792]{1,0:T(8,128)(2,1)S(1)}, bf16[384,1792]{1,0:T(8,128)(2,1)S(1)}) custom-call(s32[11]{0:T(128)S(1)} %stack.185.info, bf16[4,96,2048]{2,1,0:T(8,128)(2,1)} %bitcast.63.refs_0_, bf16[4,96,2048]{2,1,0:T(8,128)(2,1)} %collective-permute-done.8.refs_1_, bf16[4,96,2048]{2,1,0:T(8,128)(2,1)} %collective-permute-done.9.refs_2_, ...), custom_call_target="tpu_custom_call" | custom-call | tf_op jit(solution)/shard_map/partial_sums/pallas_call | solution.py:133
  385.4 13.7 %collective-permute-done.31 = bf16[384,1792]{1,0:T(8,128)(2,1)S(1)} collective-permute-done((bf16[384,1792]{1,0:T(8,128)(2,1)}, bf16[384,1792]{1,0:T(8,128)(2,1)S(1)}, u32[]{:S(2)}, u32[]{:S(2)}) %collective-permute-start.31) | collective-permute-done | bytes 1376288 | tf_op jit(solution)/shard_map/ppermute | solution.py:300
  402.4 6.1 %collective-permute-done.33 = bf16[384,1792]{1,0:T(8,128)(2,1)S(1)} collective-permute-done((bf16[384,1792]{1,0:T(8,128)(2,1)}, bf16[384,1792]{1,0:T(8,128)(2,1)S(1)}, u32[]{:S(2)}, u32[]{:S(2)}) %collective-permute-start.33) | collective-permute-done | bytes 1376288 | tf_op jit(solution)/shard_map/ppermute | solution.py:301
  415.0 7.3 %copy.84 = f32[16,64,1792]{2,1,0:T(8,128)} copy(f32[16,64,1792]{2,0,1:T(8,128)S(1)} %fusion.5) | data formatting | bytes 14680064
  428.9 12.7 %partial_sums.5 = (f32[384,1792]{1,0:T(8,128)}, f32[384,1792]{1,0:T(8,128)}) custom-call(s32[11]{0:T(128)S(1)} %stack.164.info, bf16[4,96,2048]{2,1,0:T(8,128)(2,1)} %bitcast.63.refs_0_, bf16[4,96,2048]{2,1,0:T(8,128)(2,1)} %collective-permute-done.8.refs_1_, bf16[4,96,2048]{2,1,0:T(8,128)(2,1)} %collective-permute-done.9.refs_2_, ...), custom_call_target="tpu_custom_call" | custom-call | tf_op jit(solution)/shard_map/partial_sums/pallas_call | solution.py:133
  441.6 14.6 %collective-permute-done.32.left = bf16[384,1792]{1,0:T(8,128)(2,1)S(1)} collective-permute-done((bf16[384,1792]{1,0:T(8,128)(2,1)}, bf16[384,1792]{1,0:T(8,128)(2,1)S(1)}, u32[]{:S(2)}, u32[]{:S(2)}) %collective-permute-start.32) | collective-permute-done | bytes 1376288 | tf_op jit(solution)/shard_map/ppermute | solution.py:300
  456.2 9.6 %collective-permute-done.34.right = bf16[384,1792]{1,0:T(8,128)(2,1)S(1)} collective-permute-done((bf16[384,1792]{1,0:T(8,128)(2,1)}, bf16[384,1792]{1,0:T(8,128)(2,1)S(1)}, u32[]{:S(2)}, u32[]{:S(2)}) %collective-permute-start.34) | collective-permute-done | bytes 1376288 | tf_op jit(solution)/shard_map/ppermute | solution.py:301
  467.5 5.9 %finish.2 = (bf16[768,1792]{1,0:T(8,128)(2,1)}, bf16[768,1792]{1,0:T(8,128)(2,1)}) custom-call(f32[384,1792]{1,0:T(8,128)S(1)} %copy-done.2, bf16[384,1792]{1,0:T(8,128)(2,1)S(1)} %collective-permute-done.32.left, bf16[384,1792]{1,0:T(8,128)(2,1)S(1)} %collective-permute-done.34.right, bf16[768,1792]{1,0:T(8,128)(2,1)} %gate.3, bf16[768,1792]{1,0:T(8,128)(2,1)} %up.3), custom_call_target="tpu_custom_call" | custom-call | tf_op jit(solution)/shard_map/finish/pallas_call | solution.py:179
  473.4 5.9 %finish.3 = (bf16[768,1792]{1,0:T(8,128)(2,1)}, bf16[768,1792]{1,0:T(8,128)(2,1)}) custom-call(f32[384,1792]{1,0:T(8,128)S(1)} %copy-done.3, bf16[384,1792]{1,0:T(8,128)(2,1)S(1)} %collective-permute-done.26.left, bf16[384,1792]{1,0:T(8,128)(2,1)S(1)} %collective-permute-done.28.right, ...), custom_call_target="tpu_custom_call", output_to_operand_aliasing={{0}: (5, {}), {1}: (6, {})} | custom-call | tf_op jit(solution)/shard_map/finish/pallas_call | solution.py:179
  (227 shorter events, 158.1 us)
Async XLA Ops:
  6.2 58.4 %collective-permute-start.2 = (bf16[96,1024]{1,0:T(8,128)(2,1)S(1)}, bf16[96,1024]{1,0:T(8,128)(2,1)}, u32[]{:S(2)}, u32[]{:S(2)}) collective-permute-start(bf16[96,1024]{1,0:T(8,128)(2,1)S(1)} %get-tuple-element.63), channel_id=1, source_target_pairs={{0,2},{1,3},{2,10},{3,11},{4,18},{5,19},{6,26},{7,27},{8,4},{9,5},... | collective-permute-start | bytes 589832 | tf_op jit(solution)/shard_map/ppermute | solution.py:64
  9.7 71.6 %collective-permute-start.3 = (bf16[96,1024]{1,0:T(8,128)(2,1)S(1)}, bf16[96,1024]{1,0:T(8,128)(2,1)}, u32[]{:S(2)}, u32[]{:S(2)}) collective-permute-start(bf16[96,1024]{1,0:T(8,128)(2,1)S(1)} %get-tuple-element.62), channel_id=1, source_target_pairs={{0,3},{1,4},{2,11},{3,12},{4,19},{5,20},{6,27},{7,28},{8,5},{9,6},... | collective-permute-start | bytes 589832 | tf_op jit(solution)/shard_map/ppermute | solution.py:64
  10.8 72.1 %collective-permute-start.4 = (bf16[96,1024]{1,0:T(8,128)(2,1)S(1)}, bf16[96,1024]{1,0:T(8,128)(2,1)}, u32[]{:S(2)}, u32[]{:S(2)}) collective-permute-start(bf16[96,1024]{1,0:T(8,128)(2,1)S(1)} %get-tuple-element.61), channel_id=1, source_target_pairs={{0,4},{1,5},{2,12},{3,13},{4,20},{5,21},{6,28},{7,29},{8,6},{9,7},... | collective-permute-start | bytes 589832 | tf_op jit(solution)/shard_map/ppermute | solution.py:64
  22.9 61.6 %collective-permute-start.5 = (bf16[96,1024]{1,0:T(8,128)(2,1)}, bf16[96,1024]{1,0:T(8,128)(2,1)S(1)}, u32[]{:S(2)}, u32[]{:S(2)}) collective-permute-start(bf16[96,1024]{1,0:T(8,128)(2,1)} %get-tuple-element.60), channel_id=1, source_target_pairs={{0,5},{1,6},{2,13},{3,14},{4,21},{5,22},{6,29},{7,30},{8,7},{9,0},... | collective-permute-start | bytes 589832 | tf_op jit(solution)/shard_map/ppermute | solution.py:64
  37.3 50.0 %collective-permute-start.6 = (bf16[96,1024]{1,0:T(8,128)(2,1)}, bf16[96,1024]{1,0:T(8,128)(2,1)S(1)}, u32[]{:S(2)}, u32[]{:S(2)}) collective-permute-start(bf16[96,1024]{1,0:T(8,128)(2,1)} %get-tuple-element.59), channel_id=1, source_target_pairs={{0,6},{1,7},{2,14},{3,15},{4,22},{5,23},{6,30},{7,31},{8,0},{9,1},... | collective-permute-start | bytes 589832 | tf_op jit(solution)/shard_map/ppermute | solution.py:64
  81.3 50.0 %collective-permute-start.19 = (bf16[3,64,1024]{2,1,0:T(8,128)(2,1)}, bf16[3,64,1024]{2,1,0:T(8,128)(2,1)S(1)}, u32[]{:S(2)}, u32[]{:S(2)}) collective-permute-start(bf16[3,64,1024]{2,1,0:T(8,128)(2,1)} %get-tuple-element.55), channel_id=1, source_target_pairs={{0,24},{8,0},{16,8},{24,16},{1,25},{9,1},{17,9},{25,17},{2,26},{10... | collective-permute-start | bytes 1179656 | tf_op jit(solution)/shard_map/ppermute | solution.py:37
  82.9 48.3 %collective-permute-start.18 = (bf16[3,64,1024]{2,1,0:T(8,128)(2,1)}, bf16[3,64,1024]{2,1,0:T(8,128)(2,1)S(1)}, u32[]{:S(2)}, u32[]{:S(2)}) collective-permute-start(bf16[3,64,1024]{2,1,0:T(8,128)(2,1)} %get-tuple-element.56), channel_id=1, source_target_pairs={{0,16},{8,24},{16,0},{24,8},{1,17},{9,25},{17,1},{25,9},{2,18},{10... | collective-permute-start | bytes 1179656 | tf_op jit(solution)/shard_map/ppermute | solution.py:37
  84.5 46.7 %collective-permute-start.17 = (bf16[3,64,1024]{2,1,0:T(8,128)(2,1)}, bf16[3,64,1024]{2,1,0:T(8,128)(2,1)}, u32[]{:S(2)}, u32[]{:S(2)}) collective-permute-start(bf16[3,64,1024]{2,1,0:T(8,128)(2,1)} %get-tuple-element.57), channel_id=1, source_target_pairs={{0,8},{8,16},{16,24},{24,0},{1,9},{9,17},{17,25},{25,1},{2,10},{10... | collective-permute-start | bytes 1179656 | tf_op jit(solution)/shard_map/ppermute | solution.py:37
  94.8 78.8 %collective-permute-start.9 = (bf16[4,96,2048]{2,1,0:T(8,128)(2,1)}, bf16[4,96,2048]{2,1,0:T(8,128)(2,1)}, u32[]{:S(2)}, u32[]{:S(2)}) collective-permute-start(bf16[4,96,2048]{2,1,0:T(8,128)(2,1)} %bitcast.63.refs_0_), channel_id=1, source_target_pairs={{0,2},{1,3},{2,0},{3,1},{4,6},{5,7},{6,4},{7,5},{8,10},{9,11},{10,... | collective-permute-start | bytes 4718600 | tf_op jit(solution)/shard_map/ppermute | solution.py:83
  129.1 42.7 %collective-permute-start.11 = (bf16[4,96,2048]{2,1,0:T(8,128)(2,1)}, bf16[4,96,2048]{2,1,0:T(8,128)(2,1)}, u32[]{:S(2)}, u32[]{:S(2)}) collective-permute-start(bf16[4,96,2048]{2,1,0:T(8,128)(2,1)} %bitcast.63.refs_0_), channel_id=1, source_target_pairs={{0,4},{1,5},{2,6},{3,7},{4,0},{5,1},{6,2},{7,3},{8,12},{9,13},{10,... | collective-permute-start | bytes 4718600 | tf_op jit(solution)/shard_map/ppermute | solution.py:83
  171.8 42.1 %collective-permute-start.8 = (bf16[4,96,2048]{2,1,0:T(8,128)(2,1)}, bf16[4,96,2048]{2,1,0:T(8,128)(2,1)}, u32[]{:S(2)}, u32[]{:S(2)}) collective-permute-start(bf16[4,96,2048]{2,1,0:T(8,128)(2,1)} %bitcast.63.refs_0_), channel_id=1, source_target_pairs={{0,1},{1,0},{2,3},{3,2},{4,5},{5,4},{6,7},{7,6},{8,9},{9,8},{10,11... | collective-permute-start | bytes 4718600 | tf_op jit(solution)/shard_map/ppermute | solution.py:83
  226.1 99.5 %collective-permute-start.24 = (bf16[384,1792]{1,0:T(8,128)(2,1)}, bf16[384,1792]{1,0:T(8,128)(2,1)}, u32[]{:S(2)}, u32[]{:S(2)}) collective-permute-start(bf16[384,1792]{1,0:T(8,128)(2,1)} %get-tuple-element.21), channel_id=1, source_target_pairs={{24,16},{25,17},{26,18},{27,19},{28,20},{29,21},{30,22},{31,23}} | collective-permute-start | bytes 4128776 | tf_op jit(solution)/shard_map/ppermute | solution.py:301
  227.8 97.8 %collective-permute-start.23 = (bf16[384,1792]{1,0:T(8,128)(2,1)}, bf16[384,1792]{1,0:T(8,128)(2,1)}, u32[]{:S(2)}, u32[]{:S(2)}) collective-permute-start(bf16[384,1792]{1,0:T(8,128)(2,1)} %get-tuple-element.21), channel_id=1, source_target_pairs={{0,8},{1,9},{2,10},{3,11},{4,12},{5,13},{6,14},{7,15}} | collective-permute-start | bytes 4128776 | tf_op jit(solution)/shard_map/ppermute | solution.py:300
  234.8 63.8 %collective-permute-start.36 = (bf16[3,64,1792]{2,1,0:T(8,128)(2,1)}, bf16[3,64,1792]{2,1,0:T(8,128)(2,1)}, u32[]{:S(2)}, u32[]{:S(2)}) collective-permute-start(bf16[3,64,1792]{2,1,0:T(8,128)(2,1)} %get-tuple-element.52), channel_id=1, source_target_pairs={{0,16},{8,24},{16,0},{24,8},{1,17},{9,25},{17,1},{25,9},{2,18},{10... | collective-permute-start | bytes 2064392 | tf_op jit(solution)/shard_map/ppermute | solution.py:37
  242.7 64.5 %collective-permute-start.35 = (bf16[3,64,1792]{2,1,0:T(8,128)(2,1)}, bf16[3,64,1792]{2,1,0:T(8,128)(2,1)}, u32[]{:S(2)}, u32[]{:S(2)}) collective-permute-start(bf16[3,64,1792]{2,1,0:T(8,128)(2,1)} %get-tuple-element.53), channel_id=1, source_target_pairs={{0,8},{8,16},{16,24},{24,0},{1,9},{9,17},{17,25},{25,1},{2,10},{10... | collective-permute-start | bytes 2064392 | tf_op jit(solution)/shard_map/ppermute | solution.py:37
  254.8 84.4 %collective-permute-start.30 = (bf16[384,1792]{1,0:T(8,128)(2,1)}, bf16[384,1792]{1,0:T(8,128)(2,1)}, u32[]{:S(2)}, u32[]{:S(2)}) collective-permute-start(bf16[384,1792]{1,0:T(8,128)(2,1)} %copy-done.5), channel_id=1, source_target_pairs={{24,16},{25,17},{26,18},{27,19},{28,20},{29,21},{30,22},{31,23}} | collective-permute-start | bytes 4128776 | tf_op jit(solution)/shard_map/ppermute | solution.py:301
  329.4 45.2 %collective-permute-start.25 = (bf16[384,1792]{1,0:T(8,128)(2,1)}, bf16[384,1792]{1,0:T(8,128)(2,1)}, u32[]{:S(2)}, u32[]{:S(2)}) collective-permute-start(bf16[384,1792]{1,0:T(8,128)(2,1)} %add_convert_fusion.5), channel_id=1, source_target_pairs={{0,8},{8,16},{1,9},{9,17},{2,10},{10,18},{3,11},{11,19},{4,12},{12... | collective-permute-start | bytes 4128776 | tf_op jit(solution)/shard_map/ppermute | solution.py:300
  336.4 76.0 %collective-permute-start.39 = (f32[4,3,64,64]{3,2,1,0:T(8,128)S(1)}, f32[4,3,64,64]{3,2,1,0:T(8,128)S(1)}, u32[]{:S(2)}, u32[]{:S(2)}) collective-permute-start(f32[4,3,64,64]{3,2,1,0:T(8,128)S(1)} %add.388), channel_id=1, source_target_pairs={{0,2},{1,3},{2,0},{3,1},{4,6},{5,7},{6,4},{7,5},{8,10},{9,11},{10,... | collective-permute-start | bytes 589832 | tf_op jit(solution)/shard_map/ppermute | solution.py:24
  338.0 44.1 %collective-permute-start.27 = (bf16[384,1792]{1,0:T(8,128)(2,1)}, bf16[384,1792]{1,0:T(8,128)(2,1)S(1)}, u32[]{:S(2)}, u32[]{:S(2)}) collective-permute-start(bf16[384,1792]{1,0:T(8,128)(2,1)} %add_convert_fusion.5), channel_id=1, source_target_pairs={{24,16},{16,8},{25,17},{17,9},{26,18},{18,10},{27,19},{19,11},{28,... | collective-permute-start | bytes 4128776 | tf_op jit(solution)/shard_map/ppermute | solution.py:301
  343.2 56.0 %collective-permute-start.31 = (bf16[384,1792]{1,0:T(8,128)(2,1)}, bf16[384,1792]{1,0:T(8,128)(2,1)S(1)}, u32[]{:S(2)}, u32[]{:S(2)}) collective-permute-start(bf16[384,1792]{1,0:T(8,128)(2,1)} %add_convert_fusion.2), channel_id=1, source_target_pairs={{0,8},{8,16},{1,9},{9,17},{2,10},{10,18},{3,11},{11,19},{4,12},{12... | collective-permute-start | bytes 4128776 | tf_op jit(solution)/shard_map/ppermute | solution.py:300
  377.5 95.9 %collective-permute-start.26 = (bf16[384,1792]{1,0:T(8,128)(2,1)}, bf16[384,1792]{1,0:T(8,128)(2,1)S(1)}, u32[]{:S(2)}, u32[]{:S(2)}) collective-permute-start(bf16[384,1792]{1,0:T(8,128)(2,1)} %add_convert_fusion.4), channel_id=1, source_target_pairs={{0,8},{8,16},{16,24},{1,9},{9,17},{17,25},{2,10},{10,18},{18,26},{... | collective-permute-start | bytes 4128776 | tf_op jit(solution)/shard_map/ppermute | solution.py:300
  383.5 90.0 %collective-permute-start.28 = (bf16[384,1792]{1,0:T(8,128)(2,1)}, bf16[384,1792]{1,0:T(8,128)(2,1)S(1)}, u32[]{:S(2)}, u32[]{:S(2)}) collective-permute-start(bf16[384,1792]{1,0:T(8,128)(2,1)} %add_convert_fusion.3), channel_id=1, source_target_pairs={{24,16},{16,8},{8,0},{25,17},{17,9},{9,1},{26,18},{18,10},{10,2},{... | collective-permute-start | bytes 4128776 | tf_op jit(solution)/shard_map/ppermute | solution.py:301
  400.5 55.6 %collective-permute-start.32 = (bf16[384,1792]{1,0:T(8,128)(2,1)}, bf16[384,1792]{1,0:T(8,128)(2,1)S(1)}, u32[]{:S(2)}, u32[]{:S(2)}) collective-permute-start(bf16[384,1792]{1,0:T(8,128)(2,1)} %add_convert_fusion.1), channel_id=1, source_target_pairs={{0,8},{8,16},{16,24},{1,9},{9,17},{17,25},{2,10},{10,18},{18,26},{... | collective-permute-start | bytes 4128776 | tf_op jit(solution)/shard_map/ppermute | solution.py:300
  410.0 55.7 %collective-permute-start.34 = (bf16[384,1792]{1,0:T(8,128)(2,1)}, bf16[384,1792]{1,0:T(8,128)(2,1)S(1)}, u32[]{:S(2)}, u32[]{:S(2)}) collective-permute-start(bf16[384,1792]{1,0:T(8,128)(2,1)} %add_convert_fusion), channel_id=1, source_target_pairs={{24,16},{16,8},{8,0},{25,17},{17,9},{9,1},{26,18},{18,10},{10,2},{... | collective-permute-start | bytes 4128776 | tf_op jit(solution)/shard_map/ppermute | solution.py:301
  (49 other events, 975.5 us)

commit v3 on v2

v3 whole, which is shorter than its diff:
```python
import functools

import jax
import jax.numpy as jnp
from jax import lax
from jax.experimental import pallas as pl
from jax.experimental.pallas import tpu as pltpu
from jax.sharding import PartitionSpec as P

ADAPTER_RANK = 64
BLK = 64
VMEM_BYTES = 48 * 1024 * 1024


adapter_scale = 2.0


def sum_over_mp(x):
    size = lax.axis_size("mp")
    if size & (size - 1):
        return lax.psum(x, "mp")
    bit = 1
    while bit < size:
        x = x + lax.ppermute(x, "mp", [(i, i ^ bit) for i in range(size)])
        bit *= 2
    return x


def pack_kernel(count, capacity, info, *refs):
    sources, packets = refs[:-count], refs[-count:]
    step = pl.program_id(0)
    if len(sources) == capacity:
        values = [source[...] for source in sources]
    else:
        values = []
        for c in range(capacity):
            gate = sources[c][...].astype(jnp.float32)
            up = sources[capacity + c][...].astype(jnp.float32)
            values.append((gate * jax.nn.sigmoid(gate) * up).astype(jnp.bfloat16))
    for j in range(count):

        @pl.when(step == j)
        def _():
            for c in range(capacity):
                packets[j][c * BLK : (c + 1) * BLK, :] = values[c]


def pack(route, *sources):
    count, capacity = route.shape
    width = sources[0].shape[1]
    spec = [
        pl.BlockSpec((BLK, width), lambda i, info, c=c: (info[i * capacity + c], 0))
        for c in range(capacity)
    ]
    packets = pl.pallas_call(
        functools.partial(pack_kernel, count, capacity),
        grid_spec=pltpu.PrefetchScalarGridSpec(
            num_scalar_prefetch=1,
            grid=(count,),
            in_specs=spec * len(sources),
            out_specs=[
                pl.BlockSpec((capacity * BLK, width), lambda i, info: (0, 0)) for _ in range(count)
            ],
        ),
        out_shape=[jax.ShapeDtypeStruct((capacity * BLK, width), sources[0].dtype)] * count,
        compiler_params=pltpu.CompilerParams(vmem_limit_bytes=VMEM_BYTES),
        name="pack",
    )(route.reshape(-1), *[s for s in sources for _ in range(capacity)])
    return list(packets)


def all_to_all_of(parts):
    got = lax.all_to_all(jnp.stack(parts), "dp", split_axis=0, concat_axis=0, tiled=True)
    return [got[g] for g in range(len(parts))]


def swap_over_dp(x, bits, only=None):
    size = lax.axis_size("dp")
    return lax.ppermute(x, "dp", [(i, i ^ bits) for i in range(size) if only is None or i in only])


def factor_kernel(capacity, slots, *refs):
    weights, packets, result = refs[:capacity], refs[capacity:-1], refs[-1]
    step = pl.program_id(0)
    for j, packet in enumerate(packets):

        @pl.when(step == j)
        def _():
            for c in range(capacity):
                result[c] = lax.dot_general(
                    packet[c * BLK : (c + 1) * BLK, :],
                    weights[c][0],
                    (((1,), (1,)), ((), ())),
                    preferred_element_type=jnp.float32,
                )


def factor_parts(packets, weight, slots):
    count, capacity = slots.shape
    rank, width = weight.shape[1:]
    return pl.pallas_call(
        functools.partial(factor_kernel, capacity),
        grid_spec=pltpu.PrefetchScalarGridSpec(
            num_scalar_prefetch=1,
            grid=(count,),
            in_specs=[
                pl.BlockSpec((1, rank, width), lambda i, slots, c=c: (slots[i * capacity + c], 0, 0))
                for c in range(capacity)
            ]
            + [pl.BlockSpec((capacity * BLK, width), lambda i, slots: (0, 0)) for _ in packets],
            out_specs=pl.BlockSpec((capacity, BLK, rank), lambda i, slots: (i, 0, 0)),
        ),
        out_shape=jax.ShapeDtypeStruct((count * capacity, BLK, rank), jnp.float32),
        compiler_params=pltpu.CompilerParams(vmem_limit_bytes=VMEM_BYTES),
        name="factor_parts",
    )(slots.reshape(-1), *[weight] * capacity, *packets)


def slices_of_tokens(out, groups, members, block_rows):
    tok_rows, d_local = out.shape
    share = tok_rows // members
    moved = lax.all_to_all(
        out.reshape(members, share, d_local), "mp", split_axis=0, concat_axis=0, tiled=True
    )
    if members % groups or share % 16 or groups != 4 or tok_rows // groups != block_rows:
        moved = moved.transpose(1, 0, 2).reshape(share, groups, -1).transpose(1, 0, 2)
        return moved[:, None], False
    return moved.reshape(groups, members // groups, share, d_local), True


def partial_kernel(capacity, info, units_ref, w_ref, factor_ref, *rest):
    a_refs, outs, rows_ref, total_ref = rest[:capacity], rest[capacity:-2], rest[-2], rest[-1]

    @pl.when(pl.program_id(0) == 0)
    def _():
        members, _, parts, rows, columns = units_ref.shape
        for m in range(members):
            for q in range(parts):
                rows_ref[m * rows : (m + 1) * rows, q * columns : (q + 1) * columns] = units_ref[
                    m, 0, q
                ]

    total_ref[...] = lax.dot_general(
        rows_ref[...], w_ref[...], (((1,), (1,)), ((), ())), preferred_element_type=jnp.float32
    )
    for c in range(capacity):

        @pl.when(info[2 + 3 * c] > 0)
        def _():
            rows = pl.ds(pl.multiple_of(info[3 + 3 * c] * BLK, BLK), BLK)
            total_ref[rows, :] += jnp.dot(
                factor_ref[0, c], a_refs[c][0], preferred_element_type=jnp.float32
            )

    half = outs[0].shape[0]
    for h, out in enumerate(outs):
        out[...] = total_ref[h * half : (h + 1) * half, :].astype(out.dtype)


def partial_sums(info, units, weight, factors, first, tok_rows, halves, dtype):
    ff_local, width = weight.shape
    capacity, _, rank = factors.shape[1:]
    tile = 256 if ff_local % 256 == 0 else ff_local
    members, _, parts, rows, columns = units.shape
    return pl.pallas_call(
        functools.partial(partial_kernel, capacity),
        grid_spec=pltpu.PrefetchScalarGridSpec(
            num_scalar_prefetch=1,
            grid=(ff_local // tile,),
            in_specs=[
                pl.BlockSpec(
                    (members, 1, parts, rows, columns), lambda n, info: (0, info[0], 0, 0, 0)
                ),
                pl.BlockSpec((tile, width), lambda n, info: (n, 0)),
                pl.BlockSpec((1, capacity, BLK, rank), lambda n, info: (info[1], 0, 0, 0)),
            ]
            + [
                pl.BlockSpec((1, rank, tile), lambda n, info, c=c: (info[4 + 3 * c], 0, n))
                for c in range(capacity)
            ],
            out_specs=[
                pl.BlockSpec((tok_rows // halves, tile), lambda n, info: (0, n))
                for _ in range(halves)
            ],
            scratch_shapes=[
                pltpu.VMEM((tok_rows, width), jnp.bfloat16),
                pltpu.VMEM((tok_rows, tile), jnp.float32),
            ],
        ),
        out_shape=[
            jax.ShapeDtypeStruct((tok_rows // halves, ff_local), dtype) for _ in range(halves)
        ],
        compiler_params=pltpu.CompilerParams(vmem_limit_bytes=VMEM_BYTES),
        name="partial_sums",
    )(info, units, weight, factors, *[first] * capacity)


def finish_kernel(own, left, right, gate, up, *rest):
    d_gate, d_up = rest[-2:]
    d_hidden = own[...] + left[...].astype(jnp.float32) + right[...].astype(jnp.float32)
    gate_float = gate[...].astype(jnp.float32)
    up_float = up[...].astype(jnp.float32)
    squash = jax.nn.sigmoid(gate_float)
    d_gate[...] = (d_hidden * up_float * squash * (1.0 + gate_float * (1.0 - squash))).astype(
        d_gate.dtype
    )
    d_up[...] = (d_hidden * (gate_float * squash)).astype(d_up.dtype)


def finish(own, left, right, gate, up, part, earlier):
    rows, ff_local = own.shape
    step = 128 if rows % 128 == 0 else rows
    steps = rows // step
    here = pl.BlockSpec((step, ff_local), lambda i: (i, 0))
    there = pl.BlockSpec((step, ff_local), lambda i: (part * steps + i, 0))
    before = [] if earlier is None else list(earlier)
    return pl.pallas_call(
        finish_kernel,
        grid=(steps,),
        in_specs=[here, here, here, there, there] + [pl.BlockSpec(memory_space=pl.ANY)] * len(before),
        out_specs=[there, there],
        out_shape=[jax.ShapeDtypeStruct(gate.shape, gate.dtype) for _ in range(2)],
        input_output_aliases={5: 0, 6: 1} if before else {},
        compiler_params=pltpu.CompilerParams(vmem_limit_bytes=VMEM_BYTES),
        name="finish",
    )(own, left, right, gate, up, *before)


def shards(
    output_gradient,
    saved_gate_value,
    saved_up_value,
    down_weight,
    adapter_first_weight,
    adapter_second_weight,
    adapter_of_block,
    slot_of_adapter,
):
    groups = lax.axis_size("dp")
    members = lax.axis_size("mp")
    my_group = lax.axis_index("dp")
    tok_rows = output_gradient.shape[0]
    blocks = tok_rows // BLK
    owner_totals = adapter_first_weight.shape[0]
    adapters = slot_of_adapter.shape[0]
    ff_local = saved_gate_value.shape[1]
    d_local = output_gradient.shape[1]
    capacity = (blocks + groups - 1) // groups
    halves = 1

    match_table = adapter_of_block[:, None] == jnp.arange(adapters, dtype=jnp.int32)[None, :]
    slot_of_block = jnp.sum(jnp.where(match_table, slot_of_adapter[None, :], 0), axis=1)
    owners = (slot_of_block // owner_totals).reshape(groups, blocks)
    local_slot = (slot_of_block % owner_totals).reshape(groups, blocks)
    block_index = jnp.arange(blocks, dtype=jnp.int32)
    earlier = (owners[:, :, None] == owners[:, None, :]) & (
        block_index[None, None, :] < block_index[None, :, None]
    )
    ranks = jnp.sum(earlier.astype(jnp.int32), axis=2)
    rank_values = jnp.arange(capacity, dtype=jnp.int32)
    hits = (owners == my_group)[:, None, :] & (ranks[:, None, :] == rank_values[None, :, None])
    incoming_valid = jnp.any(hits, axis=2)
    arriving_slot = jnp.sum(jnp.where(hits, local_slot[:, None, :], 0), axis=2)
    own_owner = lax.dynamic_index_in_dim(owners, my_group, 0, keepdims=False)
    own_rank = lax.dynamic_index_in_dim(ranks, my_group, 0, keepdims=False)
    group_values = jnp.arange(groups, dtype=jnp.int32)
    route_table = (own_owner[None, None, :] == group_values[:, None, None]) & (
        own_rank[None, None, :] == rank_values[None, :, None]
    )
    route_block = jnp.sum(jnp.where(route_table, block_index[None, None, :], 0), axis=2)

    moved, by_units = slices_of_tokens(output_gradient, groups, members, capacity * BLK)
    order = jnp.arange(groups, dtype=jnp.int32)
    origin = (my_group ^ order) if by_units else order
    place = origin
    routes = jnp.take(route_block, origin, axis=0)
    send_o = pack(routes, output_gradient)
    send_h = pack(routes, saved_gate_value, saved_up_value)
    slots = jnp.take(arriving_slot, origin, axis=0)
    valid = jnp.take(incoming_valid, origin, axis=0)
    last = groups - 1

    def target_of(reach, side):
        right = jnp.minimum(my_group + reach, last)
        left = jnp.maximum(my_group - reach, 0)
        if side:
            return right if side > 0 else left
        return jnp.where(my_group + reach <= last, right, left)

    def unit_of(group):
        unit = lax.dynamic_index_in_dim(moved, group, 0, keepdims=False)
        return unit.reshape(-1, d_local)

    if by_units:
        recv_o = send_o[:1] + [swap_over_dp(send_o[j], j) for j in range(1, groups)]
        recv_o, moved = lax.optimization_barrier((recv_o, moved))
        far = swap_over_dp(
            jnp.concatenate([send_h[3], unit_of(target_of(3, 0))], axis=1), 3, (0, 3)
        )
        far_h, far = far[:, :ff_local], far[:, ff_local:]
    else:
        recv_o, recv_h = all_to_all_of(send_o), all_to_all_of(send_h)
        units = lax.all_to_all(moved[:, 0], "dp", split_axis=0, concat_axis=0, tiled=True)
        others = lax.all_gather(units, "mp", axis=1, tiled=True)[None, :, None]

    def by_block(factor):
        return factor.reshape(groups, capacity, BLK, ADAPTER_RANK).astype(jnp.bfloat16)

    back_factor = by_block(
        adapter_scale * sum_over_mp(factor_parts(recv_o, adapter_second_weight, slots))
    )
    if by_units:
        far, back_factor, moved = lax.optimization_barrier((far, back_factor, moved))

        def gathered(*units):
            return lax.all_gather(
                jnp.stack([u.reshape(moved.shape[1:]) for u in units]), "mp", axis=0
            )

        far = gathered(far)
        pairs = [(i, i + 2) for i in range(groups - 2)] + [(i + 2, i) for i in range(groups - 2)]
        others = [
            lax.ppermute(unit_of(target_of(2, 0)), "dp", pairs),
            lax.ppermute(unit_of(target_of(1, -1)), "dp", [(i + 1, i) for i in range(last)]),
            lax.ppermute(unit_of(target_of(1, 1)), "dp", [(i, i + 1) for i in range(last)]),
        ]
        send_h[1], back_factor = lax.optimization_barrier((send_h[1], back_factor))
        recv_h = [send_h[0], swap_over_dp(send_h[1], 1), None, None]
        others, recv_h[1], back_factor = lax.optimization_barrier((others, recv_h[1], back_factor))
        others, _ = lax.optimization_barrier((others, far))
        others = gathered(*others, unit_of(my_group))

    table = jnp.stack(
        [
            incoming_valid.astype(jnp.int32),
            jnp.sum(jnp.where(hits, block_index, 0), axis=2),
            arriving_slot,
        ],
        axis=2,
    ).reshape(groups, 3 * capacity)
    table = jnp.concatenate([place[:, None], table], axis=1).astype(jnp.int32)

    def partial_for(target, reach, side, dtype=jnp.bfloat16):
        if not by_units:
            source, unit = others, target
        elif reach == 3:
            source, unit = far, 0
        else:
            source, unit = others, {2: 0, 1: 1 if side > 0 else 2, 0: 3}[reach]
        info = lax.dynamic_index_in_dim(table, target, 0, keepdims=False)
        info = jnp.concatenate([jnp.full((1,), unit, jnp.int32), info])
        return partial_sums(
            info, source, down_weight, back_factor, adapter_first_weight, tok_rows, halves, dtype
        )

    def joined(a, *more):
        total = a.astype(jnp.float32)
        for m in more:
            total = total + m.astype(jnp.float32)
        return total.astype(jnp.bfloat16)

    from_left = from_right = None
    for step in range(1, groups):
        reach = groups - step
        pairs_r = [(i, i + 1) for i in range(step)]
        pairs_l = [(last - i, last - 1 - i) for i in range(step)]
        if step <= reach:
            part = partial_for(target_of(reach, 0), reach, 0)
            if step > 1:
                came = [from_left] if from_right is None else [from_left, from_right]
                part = [joined(*each) for each in zip(part, *came)]
            send_r = send_l = part
            if step == last // 2 + 1 or not by_units:
                recv_h, send_r = lax.optimization_barrier((recv_h, send_r))
                send_l = send_r
                down_factor = by_block(
                    sum_over_mp(factor_parts(recv_h, adapter_first_weight, slots))
                )
        else:
            send_r = [joined(p, a) for p, a in zip(partial_for(target_of(reach, 1), reach, 1), from_left)]
            send_l = [joined(p, a) for p, a in zip(partial_for(target_of(reach, -1), reach, -1), from_right)]
        if by_units and step == last:
            send_r, send_l, late_h, late_o, late_factor = lax.optimization_barrier(
                (send_r, send_l, recv_h, recv_o, back_factor)
            )
            late_factor, down_factor = lax.optimization_barrier((late_factor, down_factor))
        if step < reach:
            from_left = [lax.ppermute(s, "dp", pairs_r + pairs_l) for s in send_r]
            from_right = None
            if by_units:
                middle_h = swap_over_dp(send_h[3], 3, (1, 2))
                recv_h[3] = jnp.where((my_group == 0) | (my_group == last), far_h, middle_h)
                recv_h[2] = swap_over_dp(send_h[2], 2)
        else:
            from_left = [lax.ppermute(s, "dp", pairs_r) for s in send_r]
            from_right = [lax.ppermute(s, "dp", pairs_l) for s in send_l]
    if by_units:
        recv_h, recv_o, back_factor = late_h, late_o, late_factor
    own = partial_for(my_group, 0, 0, jnp.float32)
    done = None
    for h in range(halves):
        done = finish(
            own[h], from_left[h], from_right[h], saved_gate_value, saved_up_value, h, done
        )
    d_gate, d_up = done

    def pieces(factor, packets):
        return jnp.stack(
            [
                jnp.einsum(
                    "ctr,ctf->crf",
                    factor[j],
                    packets[j].reshape(capacity, BLK, -1),
                    preferred_element_type=jnp.float32,
                )
                for j in range(groups)
            ]
        )

    terms_a = pieces(back_factor, recv_h).astype(jnp.bfloat16)
    terms_b = (adapter_scale * pieces(down_factor, recv_o)).astype(jnp.bfloat16)
    flat_slot = slots.reshape(groups * capacity)
    flat_valid = valid.reshape(groups * capacity)
    selector = (
        (flat_slot[None, :] == jnp.arange(owner_totals, dtype=jnp.int32)[:, None])
        & flat_valid[None, :]
    ).astype(jnp.bfloat16)
    grad_a = jnp.dot(
        selector,
        terms_a.reshape(groups * capacity, ADAPTER_RANK * ff_local),
        preferred_element_type=jnp.float32,
    ).reshape(owner_totals, ADAPTER_RANK, ff_local)
    grad_b = jnp.dot(
        selector,
        terms_b.reshape(groups * capacity, ADAPTER_RANK * d_local),
        preferred_element_type=jnp.float32,
    ).reshape(owner_totals, ADAPTER_RANK, d_local)
    return (d_gate, d_up, grad_a, grad_b)


def solution(mesh):
    in_specs = (
        P("dp", "mp"),
        P("dp", "mp"),
        P("dp", "mp"),
        P("mp", "dp"),
        P("dp", None, "mp"),
        P("dp", None, "mp"),
        P(),
        P(),
    )
    out_specs = (P("dp", "mp"), P("dp", "mp"), P("dp", None, "mp"), P("dp", None, "mp"))
    return jax.shard_map(shards, mesh=mesh, in_specs=in_specs, out_specs=out_specs, check_vma=False)
```

time: 481 us -> 376 us (0.78)
  starting transfers between devices: 152 us -> 40.9 us
  local copies, waits for them, and re-layouts: 64.8 us -> 25.7 us
  Pallas kernels: 69.9 us -> 92.1 us
  waiting for transfers between devices: 145 us -> 166 us
  between operations: 1.59 us -> 14.5 us
  other arithmetic: 35.1 us -> 25.8 us
    ppermute x23 -> x11, starting transfers between devices: 118 us -> 21.3 us  [the longest x7 11.2 us: swap_over_dp(): lax.ppermute(x, 'dp', [(i, i ^ bits) for i in range(size) if only is None...]
    all_gather x0 -> x2, waiting for transfers between devices: none -> 35.5 us  [gathered(): lax.all_gather(jnp.stack([u.reshape(moved.shape[1:]) for u in units]), 'm...]
    pallas_call x5 -> x9, Pallas kernels: 58.1 us -> 82.4 us  [the longest x5 68.6 us: partial_sums(): pl.pallas_call(functools.partial(partial_kernel, capacity), grid_spec=plt...]
    gather x7 -> x3, local copies, waits for them, and re-layouts: 21.6 us -> 1.68 us  [the longest x1 0.56 us: shards(): valid = jnp.take(incoming_valid, origin, axis=0)]
    ppermute x6 -> x2, waiting for transfers between devices: 15.7 us -> 4.12 us  [shards(): from_right = [lax.ppermute(s, 'dp', pairs_l) for s in send_l]]
    ppermute x6 -> x2, starting transfers between devices: 16.4 us -> 5.95 us  [shards(): from_left = [lax.ppermute(s, 'dp', pairs_r) for s in send_r]]
    select_n x4 -> x1, local copies, waits for them, and re-layouts: 7.5 us -> 0.09 us  [shards(): valid = jnp.take(incoming_valid, origin, axis=0)]
    unnamed x73 -> x46, local copies, waits for them, and re-layouts: 23.9 us -> 16.9 us
  transfers between devices with their start and end apart: 41 -> 24, of which waited for: 13 -> 17; matrix products, arithmetic and copies ran while one was open for 22% -> 11% of each run, Pallas kernels for 11% -> 22%
where the time goes in v3:
time: 376 us; the launch traced here: 373 us
  waiting for transfers between devices  166 us (44%)
  Pallas kernels  92.1 us (24%)
  starting transfers between devices  40.9 us (11%)
  other arithmetic  25.8 us (7%)
  local copies, waits for them, and re-layouts  25.7 us (7%)
  between operations  14.5 us (4%)
  matrix products  7.95 us (2%)
    pallas_call x5, Pallas kernels, partial_sums(): pl.pallas_call(functools.partial(partial_kernel, capacity), grid_spec=plt...  68.6 us
    ppermute x7, waiting for transfers between devices, swap_over_dp(): lax.ppermute(x, 'dp', [(i, i ^ bits) for i in range(size) if only is None...  43.2 us
    all_gather x2, waiting for transfers between devices, gathered(): lax.all_gather(jnp.stack([u.reshape(moved.shape[1:]) for u in units]), 'm...  35.5 us
    ppermute x6, waiting for transfers between devices, sum_over_mp(): x = x + lax.ppermute(x, 'mp', [(i, i ^ bit) for i in range(size)])  33.2 us
    ppermute x2, waiting for transfers between devices, shards(): from_left = [lax.ppermute(s, 'dp', pairs_r) for s in send_r]  28.2 us
    unnamed x46, local copies, waits for them, and re-layouts  16.9 us
    ppermute x1, waiting for transfers between devices, shards(): lax.ppermute(unit_of(target_of(2, 0)), 'dp', pairs)  16.8 us
    convert_element_type x3, other arithmetic, joined(): return total.astype(jnp.bfloat16)  12.2 us
  transfers between devices with their start and end apart: 24, of which 17 were waited for; matrix products, arithmetic and copies ran while one was open for 11% of the time, Pallas kernels for 22%

profile of v3, /device:TPU:10, one launch (start us, length us, event | category | flops | bytes accessed | tf_op | source)
XLA Modules:
  0.0 372.7 jit_solution(13591701987263169269)
XLA Ops:
  7.2 4.8 %all-to-all-start = ((bf16[8,96,1024]{2,1,0:T(8,128)(2,1)}), bf16[8,96,1024]{2,1,0:T(8,128)(2,1)}, u32[]{:S(2)}, u32[]{:S(2)}) async-start(bf16[8,96,1024]{2,1,0:T(8,128)(2,1)} %bitcast.114), calls=%async_computation | async-start | bytes 3145728 | tf_op jit(solution)/shard_map/all_to_all | solution.py:122
  22.9 5.3 %pack.2 = (bf16[192,1792]{1,0:T(8,128)(2,1)S(1)}, bf16[192,1792]{1,0:T(8,128)(2,1)S(1)}, bf16[192,1792]{1,0:T(8,128)(2,1)}, bf16[192,1792]{1,0:T(8,128)(2,1)}) custom-call(s32[12]{0:T(128)S(1)} %reshape.288.info, bf16[768,1792]{1,0:T(8,128)(2,1)S(1)} %copy-done.1, bf16[768,1792]{1,0:T(8,128)(2,1)S(1)} %copy-done.1, bf16[768,1792]{1,0:T(8,128)(2,1)S(1)} %copy-done.1, ...), custom_call_target="tpu_custom_call" | custom-call | tf_op jit(solution)/shard_map/pack/pallas_call | solution.py:55
  29.9 6.6 %collective-permute-done.refs_4_ = bf16[192,1024]{1,0:T(8,128)(2,1)S(1)} collective-permute-done((bf16[192,1024]{1,0:T(8,128)(2,1)}, bf16[192,1024]{1,0:T(8,128)(2,1)S(1)}, u32[]{:S(2)}, u32[]{:S(2)}) %collective-permute-start) | collective-permute-done | bytes 393248 | tf_op jit(solution)/shard_map/ppermute | solution.py:79
  36.6 12.6 %collective-permute-done.1.refs_5_ = bf16[192,1024]{1,0:T(8,128)(2,1)} collective-permute-done((bf16[192,1024]{1,0:T(8,128)(2,1)}, bf16[192,1024]{1,0:T(8,128)(2,1)}, u32[]{:S(2)}, u32[]{:S(2)}) %collective-permute-start.1) | collective-permute-done | bytes 393248 | tf_op jit(solution)/shard_map/ppermute | solution.py:79
  49.2 8.3 %collective-permute-done.2.refs_6_ = bf16[192,1024]{1,0:T(8,128)(2,1)} collective-permute-done((bf16[192,1024]{1,0:T(8,128)(2,1)}, bf16[192,1024]{1,0:T(8,128)(2,1)}, u32[]{:S(2)}, u32[]{:S(2)}) %collective-permute-start.2) | collective-permute-done | bytes 393248 | tf_op jit(solution)/shard_map/ppermute | solution.py:79
  67.3 10.8 %collective-permute-done.5 = f32[12,64,64]{2,1,0:T(8,128)S(1)} collective-permute-done((f32[12,64,64]{2,1,0:T(8,128)S(1)}, f32[12,64,64]{2,1,0:T(8,128)S(1)}, u32[]{:S(2)}, u32[]{:S(2)}) %collective-permute-start.5) | collective-permute-done | bytes 196640 | tf_op jit(solution)/shard_map/ppermute | solution.py:24
  79.7 8.8 %collective-permute-done.6 = f32[12,64,64]{2,1,0:T(8,128)S(1)} collective-permute-done((f32[12,64,64]{2,1,0:T(8,128)S(1)}, f32[12,64,64]{2,1,0:T(8,128)S(1)}, u32[]{:S(2)}, u32[]{:S(2)}) %collective-permute-start.6) | collective-permute-done | bytes 196640 | tf_op jit(solution)/shard_map/ppermute | solution.py:24
  101.7 16.8 %collective-permute-done.7 = bf16[192,1024]{1,0:T(8,128)(2,1)} collective-permute-done((bf16[192,1024]{1,0:T(8,128)(2,1)S(1)}, bf16[192,1024]{1,0:T(8,128)(2,1)}, u32[]{:S(2)}, u32[]{:S(2)}) %collective-permute-start.7) | collective-permute-done | bytes 393248 | tf_op jit(solution)/shard_map/ppermute | solution.py:323
  128.4 13.1 %partial_sums.7 = bf16[768,1792]{1,0:T(8,128)(2,1)} custom-call(s32[11]{0:T(128)S(1)} %pad_add_fusion.2.info, bf16[8,1,2,96,1024]{4,3,2,1,0:T(8,128)(2,1)S(1)} %copy-done.4, bf16[1792,2048]{1,0:T(8,128)(2,1)} %w_ref.9, bf16[4,3,64,64]{3,2,1,0:T(8,128)(2,1)S(1)} %bitcast.115, bf16[16,64,1792]{2,1,0:T(8,128)(2,1)} %rest_2_.9, bf16[16,64,1792]{2,1,0:T(8,128)(2,1)} %rest_2_.9, ...), custom_call_target="tpu_custom_call" | custom-call | tf_op jit(solution)/shard_map/partial_sums/pallas_call | solution.py:165
  148.9 14.4 %collective-permute-done.12 = bf16[192,1792]{1,0:T(8,128)(2,1)S(1)} collective-permute-done((bf16[192,1792]{1,0:T(8,128)(2,1)}, bf16[192,1792]{1,0:T(8,128)(2,1)S(1)}, u32[]{:S(2)}, u32[]{:S(2)}) %collective-permute-start.12) | collective-permute-done | bytes 688160 | tf_op jit(solution)/shard_map/ppermute | solution.py:79
  164.6 35.5 %all-gather.6.cloned.1.call-done = bf16[32,2,96,1024]{3,2,1,0:T(8,128)(2,1)} async-done(((bf16[4,2,96,1024]{3,2,1,0:T(8,128)(2,1)}), bf16[32,2,96,1024]{3,2,1,0:T(8,128)(2,1)}) %all-gather.6.cloned.1.call-update) | async-done | bytes 12582928 | tf_op jit(solution)/shard_map/all_gather | solution.py:316
  200.1 13.7 %partial_sums.6 = bf16[768,1792]{1,0:T(8,128)(2,1)S(1)} custom-call(s32[11]{0:T(128)S(1)} %pad_add_fusion.3.info, bf16[8,4,2,96,1024]{4,3,2,1,0:T(8,128)(2,1)} %bitcast.130, bf16[1792,2048]{1,0:T(8,128)(2,1)} %w_ref.9, bf16[4,3,64,64]{3,2,1,0:T(8,128)(2,1)S(1)} %bitcast.116, bf16[16,64,1792]{2,1,0:T(8,128)(2,1)} %rest_2_.9, bf16[16,64,1792]{2,1,0:T(8,128)(2,1)} %rest_2_.9, ...), custom_call_target="tpu_custom_call" | custom-call | tf_op jit(solution)/shard_map/partial_sums/pallas_call | solution.py:165
  213.8 4.1 %add_convert_fusion.2 = bf16[768,1792]{1,0:T(8,128)(2,1)} fusion(bf16[768,1792]{1,0:T(8,128)(2,1)} %collective-permute-done.13, bf16[768,1792]{1,0:T(8,128)(2,1)S(1)} %partial_sums.6), kind=kLoop, calls=%fused_computation.5 | loop fusion | flops 5505024 | bytes 8257536 | tf_op jit(solution)/shard_map/convert_element_type | solution.py:360
  231.8 10.7 %collective-permute-done.17 = f32[12,64,64]{2,1,0:T(8,128)} collective-permute-done((f32[12,64,64]{2,1,0:T(8,128)}, f32[12,64,64]{2,1,0:T(8,128)}, u32[]{:S(2)}, u32[]{:S(2)}) %collective-permute-start.17) | collective-permute-done | bytes 196640 | tf_op jit(solution)/shard_map/ppermute | solution.py:24
  244.5 13.7 %partial_sums.5 = bf16[768,1792]{1,0:T(8,128)(2,1)S(1)} custom-call(s32[11]{0:T(128)S(1)} %pad_add_fusion.5.info, bf16[8,4,2,96,1024]{4,3,2,1,0:T(8,128)(2,1)} %bitcast.131, bf16[1792,2048]{1,0:T(8,128)(2,1)} %w_ref.9, bf16[4,3,64,64]{3,2,1,0:T(8,128)(2,1)S(1)} %bitcast.117, bf16[16,64,1792]{2,1,0:T(8,128)(2,1)} %rest_2_.9, bf16[16,64,1792]{2,1,0:T(8,128)(2,1)} %rest_2_.9, ...), custom_call_target="tpu_custom_call" | custom-call | tf_op jit(solution)/shard_map/partial_sums/pallas_call | solution.py:165
  258.1 13.7 %partial_sums.8 = bf16[768,1792]{1,0:T(8,128)(2,1)S(1)} custom-call(s32[11]{0:T(128)S(1)} %pad_add_fusion.6.info, bf16[8,4,2,96,1024]{4,3,2,1,0:T(8,128)(2,1)} %bitcast.132, bf16[1792,2048]{1,0:T(8,128)(2,1)} %w_ref.9, bf16[4,3,64,64]{3,2,1,0:T(8,128)(2,1)S(1)} %bitcast.118, bf16[16,64,1792]{2,1,0:T(8,128)(2,1)} %rest_2_.9, bf16[16,64,1792]{2,1,0:T(8,128)(2,1)} %rest_2_.9, ...), custom_call_target="tpu_custom_call" | custom-call | tf_op jit(solution)/shard_map/partial_sums/pallas_call | solution.py:165
  272.6 9.5 %collective-permute-done.14 = bf16[768,1792]{1,0:T(8,128)(2,1)} collective-permute-done((bf16[768,1792]{1,0:T(8,128)(2,1)}, bf16[768,1792]{1,0:T(8,128)(2,1)}, u32[]{:S(2)}, u32[]{:S(2)}) %collective-permute-start.14) | collective-permute-done | bytes 2752544 | tf_op jit(solution)/shard_map/ppermute | solution.py:395
  286.0 4.1 %add_convert_fusion = bf16[768,1792]{1,0:T(8,128)(2,1)} fusion(bf16[768,1792]{1,0:T(8,128)(2,1)} %collective-permute-done.15, bf16[768,1792]{1,0:T(8,128)(2,1)S(1)} %partial_sums.8), kind=kLoop, calls=%fused_computation.3 | loop fusion | flops 5505024 | bytes 8257536 | tf_op jit(solution)/shard_map/convert_element_type | solution.py:360
  297.5 14.4 %partial_sums.9.own = f32[768,1792]{1,0:T(8,128)} custom-call(s32[11]{0:T(128)S(1)} %pad_add_fusion.4.info, bf16[8,4,2,96,1024]{4,3,2,1,0:T(8,128)(2,1)} %bitcast.133, bf16[1792,2048]{1,0:T(8,128)(2,1)} %w_ref.9, bf16[4,3,64,64]{3,2,1,0:T(8,128)(2,1)S(1)} %bitcast.119, bf16[16,64,1792]{2,1,0:T(8,128)(2,1)S(1)} %copy-done, bf16[16,64,1792]{2,1,0:T(8,128)(2,1)S(1)} %copy-done, ...), custom_call_target="tpu_custom_call" | custom-call | tf_op jit(solution)/shard_map/partial_sums/pallas_call | solution.py:165
  316.4 7.3 %copy.89 = f32[16,64,1792]{2,1,0:T(8,128)} copy(f32[16,64,1792]{2,0,1:T(8,128)S(1)} %fusion) | data formatting | bytes 14680064
  328.9 4.4 %copy.90 = f32[16,64,1024]{2,1,0:T(8,128)} copy(f32[16,64,1024]{2,0,1:T(8,128)S(1)} %fusion.7) | data formatting | bytes 8388608
  333.3 18.7 %collective-permute-done.19.left = bf16[768,1792]{1,0:T(8,128)(2,1)} collective-permute-done((bf16[768,1792]{1,0:T(8,128)(2,1)}, bf16[768,1792]{1,0:T(8,128)(2,1)}, u32[]{:S(2)}, u32[]{:S(2)}) %collective-permute-start.19) | collective-permute-done | bytes 2752544 | tf_op jit(solution)/shard_map/ppermute | solution.py:395
  352.0 4.1 %collective-permute-done.20.right = bf16[768,1792]{1,0:T(8,128)(2,1)} collective-permute-done((bf16[768,1792]{1,0:T(8,128)(2,1)}, bf16[768,1792]{1,0:T(8,128)(2,1)}, u32[]{:S(2)}, u32[]{:S(2)}) %collective-permute-start.20) | collective-permute-done | bytes 2752544 | tf_op jit(solution)/shard_map/ppermute | solution.py:396
  356.1 9.7 %finish.1 = (bf16[768,1792]{1,0:T(8,128)(2,1)}, bf16[768,1792]{1,0:T(8,128)(2,1)}) custom-call(f32[768,1792]{1,0:T(8,128)} %partial_sums.9.own, bf16[768,1792]{1,0:T(8,128)(2,1)} %collective-permute-done.19.left, bf16[768,1792]{1,0:T(8,128)(2,1)} %collective-permute-done.20.right, bf16[768,1792]{1,0:T(8,128)(2,1)} %gate.1, bf16[768,1792]{1,0:T(8,128)(2,1)} %up.1), custom_call_target="tpu_custom_call" | custom-call | tf_op jit(solution)/shard_map/finish/pallas_call | solution.py:217
  (156 shorter events, 93.0 us)
Async XLA Ops:
  7.2 50.3 %all-to-all-start = ((bf16[8,96,1024]{2,1,0:T(8,128)(2,1)}), bf16[8,96,1024]{2,1,0:T(8,128)(2,1)}, u32[]{:S(2)}, u32[]{:S(2)}) async-start(bf16[8,96,1024]{2,1,0:T(8,128)(2,1)} %bitcast.114), calls=%async_computation | async-start | bytes 3145728 | tf_op jit(solution)/shard_map/all_to_all | solution.py:122
  12.0 112.8 %all-gather.4.cloned.1.call-start = ((), (), s32[]{:S(2)}) async-start(), calls=%async_computation.1 | async-start | bytes 3538944 | tf_op jit(solution)/shard_map/all_gather | solution.py:316
  19.5 17.1 %collective-permute-start = (bf16[192,1024]{1,0:T(8,128)(2,1)}, bf16[192,1024]{1,0:T(8,128)(2,1)S(1)}, u32[]{:S(2)}, u32[]{:S(2)}) collective-permute-start(bf16[192,1024]{1,0:T(8,128)(2,1)} %get-tuple-element.53), channel_id=1, source_target_pairs={{0,8},{8,0},{16,24},{24,16},{1,9},{9,1},{17,25},{25,17},{2,10},{10... | collective-permute-start | bytes 1179656 | tf_op jit(solution)/shard_map/ppermute | solution.py:79
  19.5 29.7 %collective-permute-start.1 = (bf16[192,1024]{1,0:T(8,128)(2,1)}, bf16[192,1024]{1,0:T(8,128)(2,1)}, u32[]{:S(2)}, u32[]{:S(2)}) collective-permute-start(bf16[192,1024]{1,0:T(8,128)(2,1)} %get-tuple-element.54), channel_id=1, source_target_pairs={{0,16},{8,24},{16,0},{24,8},{1,17},{9,25},{17,1},{25,9},{2,18},{10... | collective-permute-start | bytes 1179656 | tf_op jit(solution)/shard_map/ppermute | solution.py:79
  22.5 35.0 %collective-permute-start.2 = (bf16[192,1024]{1,0:T(8,128)(2,1)}, bf16[192,1024]{1,0:T(8,128)(2,1)}, u32[]{:S(2)}, u32[]{:S(2)}) collective-permute-start(bf16[192,1024]{1,0:T(8,128)(2,1)} %get-tuple-element.55), channel_id=1, source_target_pairs={{0,24},{8,16},{16,8},{24,0},{1,25},{9,17},{17,9},{25,1},{2,26},{10... | collective-permute-start | bytes 1179656 | tf_op jit(solution)/shard_map/ppermute | solution.py:79
  60.6 28.0 %collective-permute-start.3 = (bf16[192,2816]{1,0:T(8,128)(2,1)}, bf16[192,2816]{1,0:T(8,128)(2,1)}, u32[]{:S(2)}, u32[]{:S(2)}) collective-permute-start(bf16[192,2816]{1,0:T(8,128)(2,1)} %pad_maximum_fusion.2), channel_id=1, source_target_pairs={{0,24},{24,0},{1,25},{25,1},{2,26},{26,2},{3,27},{27,3},{4,28},{28... | collective-permute-start | bytes 3244040 | tf_op jit(solution)/shard_map/ppermute | solution.py:79
  65.1 1.8 collective-permute-start.4
  66.9 11.2 %collective-permute-start.5 = (f32[12,64,64]{2,1,0:T(8,128)S(1)}, f32[12,64,64]{2,1,0:T(8,128)S(1)}, u32[]{:S(2)}, u32[]{:S(2)}) collective-permute-start(f32[12,64,64]{2,1,0:T(8,128)S(1)} %add.114), channel_id=1, source_target_pairs={{0,2},{1,3},{2,0},{3,1},{4,6},{5,7},{6,4},{7,5},{8,10},{9,11},{10,... | collective-permute-start | bytes 589832 | tf_op jit(solution)/shard_map/ppermute | solution.py:24
  78.2 10.4 %collective-permute-start.6 = (f32[12,64,64]{2,1,0:T(8,128)S(1)}, f32[12,64,64]{2,1,0:T(8,128)S(1)}, u32[]{:S(2)}, u32[]{:S(2)}) collective-permute-start(f32[12,64,64]{2,1,0:T(8,128)S(1)} %add.115), channel_id=1, source_target_pairs={{0,4},{1,5},{2,6},{3,7},{4,0},{5,1},{6,2},{7,3},{8,12},{9,13},{10,... | collective-permute-start | bytes 589832 | tf_op jit(solution)/shard_map/ppermute | solution.py:24
  90.4 109.7 %all-gather.6.cloned.1.call-start = ((), (), s32[]{:S(2)}) async-start(), calls=%async_computation.2 | async-start | bytes 14155776 | tf_op jit(solution)/shard_map/all_gather | solution.py:316
  90.5 32.7 %collective-permute-start.10 = (bf16[192,1792]{1,0:T(8,128)(2,1)S(1)}, bf16[192,1792]{1,0:T(8,128)(2,1)S(1)}, u32[]{:S(2)}, u32[]{:S(2)}) collective-permute-start(bf16[192,1792]{1,0:T(8,128)(2,1)S(1)} %copy-done.14), channel_id=1, source_target_pairs={{0,8},{8,0},{16,24},{24,16},{1,9},{9,1},{17,25},{25,17},{2,10},{10... | collective-permute-start | bytes 2064392 | tf_op jit(solution)/shard_map/ppermute | solution.py:79
  92.9 25.6 %collective-permute-start.7 = (bf16[192,1024]{1,0:T(8,128)(2,1)S(1)}, bf16[192,1024]{1,0:T(8,128)(2,1)}, u32[]{:S(2)}, u32[]{:S(2)}) collective-permute-start(bf16[192,1024]{1,0:T(8,128)(2,1)S(1)} %bitcast.142), channel_id=1, source_target_pairs={{0,16},{8,24},{16,0},{24,8},{1,17},{9,25},{17,1},{25,9},{2,18},{10... | collective-permute-start | bytes 1179656 | tf_op jit(solution)/shard_map/ppermute | solution.py:323
  95.9 25.1 %collective-permute-start.8 = (bf16[192,1024]{1,0:T(8,128)(2,1)S(1)}, bf16[192,1024]{1,0:T(8,128)(2,1)}, u32[]{:S(2)}, u32[]{:S(2)}) collective-permute-start(bf16[192,1024]{1,0:T(8,128)(2,1)S(1)} %bitcast.141), channel_id=1, source_target_pairs={{8,0},{16,8},{24,16},{9,1},{17,9},{25,17},{10,2},{18,10},{26,18},{... | collective-permute-start | bytes 1179656 | tf_op jit(solution)/shard_map/ppermute | solution.py:324
  97.8 25.3 %collective-permute-start.9 = (bf16[192,1024]{1,0:T(8,128)(2,1)S(1)}, bf16[192,1024]{1,0:T(8,128)(2,1)S(1)}, u32[]{:S(2)}, u32[]{:S(2)}) collective-permute-start(bf16[192,1024]{1,0:T(8,128)(2,1)S(1)} %bitcast.140), channel_id=1, source_target_pairs={{0,8},{8,16},{16,24},{1,9},{9,17},{17,25},{2,10},{10,18},{18,26},{... | collective-permute-start | bytes 1179656 | tf_op jit(solution)/shard_map/ppermute | solution.py:325
  141.5 72.3 %collective-permute-start.13 = (bf16[768,1792]{1,0:T(8,128)(2,1)}, bf16[768,1792]{1,0:T(8,128)(2,1)}, u32[]{:S(2)}, u32[]{:S(2)}) collective-permute-start(bf16[768,1792]{1,0:T(8,128)(2,1)} %partial_sums.7), channel_id=1, source_target_pairs={{0,8},{24,16},{1,9},{25,17},{2,10},{26,18},{3,11},{27,19},{4,12},{... | collective-permute-start | bytes 8257544 | tf_op jit(solution)/shard_map/ppermute | solution.py:388
  142.8 20.5 %collective-permute-start.12 = (bf16[192,1792]{1,0:T(8,128)(2,1)}, bf16[192,1792]{1,0:T(8,128)(2,1)S(1)}, u32[]{:S(2)}, u32[]{:S(2)}) collective-permute-start(bf16[192,1792]{1,0:T(8,128)(2,1)} %get-tuple-element.51), channel_id=1, source_target_pairs={{8,16},{16,8},{9,17},{17,9},{10,18},{18,10},{11,19},{19,11},{12,20... | collective-permute-start | bytes 2064392 | tf_op jit(solution)/shard_map/ppermute | solution.py:79
  146.4 72.8 %collective-permute-start.11 = (bf16[192,1792]{1,0:T(8,128)(2,1)}, bf16[192,1792]{1,0:T(8,128)(2,1)S(1)}, u32[]{:S(2)}, u32[]{:S(2)}) collective-permute-start(bf16[192,1792]{1,0:T(8,128)(2,1)} %get-tuple-element.76), channel_id=1, source_target_pairs={{0,16},{8,24},{16,0},{24,8},{1,17},{9,25},{17,1},{25,9},{2,18},{10... | collective-permute-start | bytes 2064392 | tf_op jit(solution)/shard_map/ppermute | solution.py:79
  219.2 62.9 %collective-permute-start.14 = (bf16[768,1792]{1,0:T(8,128)(2,1)}, bf16[768,1792]{1,0:T(8,128)(2,1)}, u32[]{:S(2)}, u32[]{:S(2)}) collective-permute-start(bf16[768,1792]{1,0:T(8,128)(2,1)} %add_convert_fusion.2), channel_id=1, source_target_pairs={{0,8},{8,16},{1,9},{9,17},{2,10},{10,18},{3,11},{11,19},{4,12},{12... | collective-permute-start | bytes 8257544 | tf_op jit(solution)/shard_map/ppermute | solution.py:395
  221.8 64.3 %collective-permute-start.15 = (bf16[768,1792]{1,0:T(8,128)(2,1)}, bf16[768,1792]{1,0:T(8,128)(2,1)}, u32[]{:S(2)}, u32[]{:S(2)}) collective-permute-start(bf16[768,1792]{1,0:T(8,128)(2,1)} %add_convert_fusion.2), channel_id=1, source_target_pairs={{24,16},{16,8},{25,17},{17,9},{26,18},{18,10},{27,19},{19,11},{28,... | collective-permute-start | bytes 8257544 | tf_op jit(solution)/shard_map/ppermute | solution.py:396
  227.3 1.9 collective-permute-start.16
  231.0 11.5 %collective-permute-start.17 = (f32[12,64,64]{2,1,0:T(8,128)}, f32[12,64,64]{2,1,0:T(8,128)}, u32[]{:S(2)}, u32[]{:S(2)}) collective-permute-start(f32[12,64,64]{2,1,0:T(8,128)} %add.124), channel_id=1, source_target_pairs={{0,2},{1,3},{2,0},{3,1},{4,6},{5,7},{6,4},{7,5},{8,10},{9,11},{10,... | collective-permute-start | bytes 589832 | tf_op jit(solution)/shard_map/ppermute | solution.py:24
  243.6 28.2 %collective-permute-start.18 = (f32[12,64,64]{2,1,0:T(8,128)S(1)}, f32[12,64,64]{2,1,0:T(8,128)S(1)}, u32[]{:S(2)}, u32[]{:S(2)}) collective-permute-start(f32[12,64,64]{2,1,0:T(8,128)S(1)} %add.125), channel_id=1, source_target_pairs={{0,4},{1,5},{2,6},{3,7},{4,0},{5,1},{6,2},{7,3},{8,12},{9,13},{10,... | collective-permute-start | bytes 589832 | tf_op jit(solution)/shard_map/ppermute | solution.py:24
  290.2 61.8 %collective-permute-start.19 = (bf16[768,1792]{1,0:T(8,128)(2,1)}, bf16[768,1792]{1,0:T(8,128)(2,1)}, u32[]{:S(2)}, u32[]{:S(2)}) collective-permute-start(bf16[768,1792]{1,0:T(8,128)(2,1)} %add_convert_fusion.1), channel_id=1, source_target_pairs={{0,8},{8,16},{16,24},{1,9},{9,17},{17,25},{2,10},{10,18},{18,26},{... | collective-permute-start | bytes 8257544 | tf_op jit(solution)/shard_map/ppermute | solution.py:395
  293.6 62.5 %collective-permute-start.20 = (bf16[768,1792]{1,0:T(8,128)(2,1)}, bf16[768,1792]{1,0:T(8,128)(2,1)}, u32[]{:S(2)}, u32[]{:S(2)}) collective-permute-start(bf16[768,1792]{1,0:T(8,128)(2,1)} %add_convert_fusion), channel_id=1, source_target_pairs={{24,16},{16,8},{8,0},{25,17},{17,9},{9,1},{26,18},{18,10},{10,2},{... | collective-permute-start | bytes 8257544 | tf_op jit(solution)/shard_map/ppermute | solution.py:396
  (22 other events, 249.3 us)
Sparse Core Ops, SparseCore 0:
  90.6 32.3 all-gather.3
  127.8 72.3 all-gather.5

commit v4 on v3

--- a/solution.py
+++ b/solution.py
@@ -197,14 +197,15 @@
 
 def finish_kernel(own, left, right, gate, up, *rest):
     d_gate, d_up = rest[-2:]
-    d_hidden = own[...] + left[...].astype(jnp.float32) + right[...].astype(jnp.float32)
+    d_hidden = own[...].astype(jnp.float32) + left[...].astype(jnp.float32)
+    d_hidden += right[...].astype(jnp.float32)
     gate_float = gate[...].astype(jnp.float32)
     up_float = up[...].astype(jnp.float32)
     squash = jax.nn.sigmoid(gate_float)
-    d_gate[...] = (d_hidden * up_float * squash * (1.0 + gate_float * (1.0 - squash))).astype(
-        d_gate.dtype
-    )
-    d_up[...] = (d_hidden * (gate_float * squash)).astype(d_up.dtype)
+    activated = gate_float * squash
+    slope = squash + activated * (1.0 - squash)
+    d_gate[...] = (d_hidden * up_float * slope).astype(d_gate.dtype)
+    d_up[...] = (d_hidden * activated).astype(d_up.dtype)
 
 
 def finish(own, left, right, gate, up, part, earlier):
@@ -293,11 +294,9 @@
 
     if by_units:
         recv_o = send_o[:1] + [swap_over_dp(send_o[j], j) for j in range(1, groups)]
-        recv_o, moved = lax.optimization_barrier((recv_o, moved))
-        far = swap_over_dp(
-            jnp.concatenate([send_h[3], unit_of(target_of(3, 0))], axis=1), 3, (0, 3)
-        )
-        far_h, far = far[:, :ff_local], far[:, ff_local:]
+        far = swap_over_dp(unit_of(target_of(3, 0)), 3, (0, 3))
+        recv_o, far, send_h[3] = lax.optimization_barrier((recv_o, far, send_h[3]))
+        far_h = swap_over_dp(send_h[3], 3, (0, 3))
     else:
         recv_o, recv_h = all_to_all_of(send_o), all_to_all_of(send_h)
         units = lax.all_to_all(moved[:, 0], "dp", split_axis=0, concat_axis=0, tiled=True)
@@ -310,7 +309,7 @@
         adapter_scale * sum_over_mp(factor_parts(recv_o, adapter_second_weight, slots))
     )
     if by_units:
-        far, back_factor, moved = lax.optimization_barrier((far, back_factor, moved))
+        far, far_h, back_factor, moved = lax.optimization_barrier((far, far_h, back_factor, moved))
 
         def gathered(*units):
             return lax.all_gather(
@@ -396,7 +395,7 @@
             from_right = [lax.ppermute(s, "dp", pairs_l) for s in send_l]
     if by_units:
         recv_h, recv_o, back_factor = late_h, late_o, late_factor
-    own = partial_for(my_group, 0, 0, jnp.float32)
+    own = partial_for(my_group, 0, 0)
     done = None
     for h in range(halves):
         done = finish(

time: 376 us -> 374 us (level)
  other arithmetic: 25.8 us -> 20.2 us
    all_to_all x1, waiting for transfers between devices: 0.01 us -> 9.79 us  [slices_of_tokens(): lax.all_to_all(out.reshape(members, share, d_local), 'mp', split_axis=0,...]
    ppermute x7 -> x8, waiting for transfers between devices: 43.2 us -> 41.2 us  [swap_over_dp(): lax.ppermute(x, 'dp', [(i, i ^ bits) for i in range(size) if only is None...]
    ppermute x7 -> x8, starting transfers between devices: 11.2 us -> 13.2 us  [swap_over_dp(): lax.ppermute(x, 'dp', [(i, i ^ bits) for i in range(size) if only is None...]
    unnamed x46 -> x44, local copies, waits for them, and re-layouts: 16.9 us -> 16.8 us
  transfers between devices with their start and end apart: 24 -> 25, of which waited for: 17 -> 17; matrix products, arithmetic and copies ran while one was open for 11% -> 11% of each run, Pallas kernels for 22% -> 21%
where the time goes in v4:
time: 374 us; the launch traced here: 371 us
  waiting for transfers between devices  169 us (45%)
  Pallas kernels  91.2 us (24%)
  starting transfers between devices  42.8 us (11%)
  local copies, waits for them, and re-layouts  23.8 us (6%)
  other arithmetic  20.2 us (5%)
  between operations  14.6 us (4%)
  matrix products  8.86 us (2%)
    pallas_call x5, Pallas kernels, partial_sums(): pl.pallas_call(functools.partial(partial_kernel, capacity), grid_spec=plt...  67.8 us
    ppermute x8, waiting for transfers between devices, swap_over_dp(): lax.ppermute(x, 'dp', [(i, i ^ bits) for i in range(size) if only is None...  41.2 us
    all_gather x2, waiting for transfers between devices, gathered(): lax.all_gather(jnp.stack([u.reshape(moved.shape[1:]) for u in units]), 'm...  34.3 us
    ppermute x6, waiting for transfers between devices, sum_over_mp(): x = x + lax.ppermute(x, 'mp', [(i, i ^ bit) for i in range(size)])  32.1 us
    ppermute x2, waiting for transfers between devices, shards(): from_left = [lax.ppermute(s, 'dp', pairs_r) for s in send_r]  26.6 us
    ppermute x1, waiting for transfers between devices, shards(): lax.ppermute(unit_of(target_of(2, 0)), 'dp', pairs)  17.4 us
    unnamed x44, local copies, waits for them, and re-layouts  16.8 us
    ppermute x8, starting transfers between devices, swap_over_dp(): lax.ppermute(x, 'dp', [(i, i ^ bits) for i in range(size) if only is None...  13.2 us
  transfers between devices with their start and end apart: 25, of which 17 were waited for; matrix products, arithmetic and copies ran while one was open for 11% of the time, Pallas kernels for 21%

profile of v4, /device:TPU:10, one launch (start us, length us, event | category | flops | bytes accessed | tf_op | source)
XLA Modules:
  0.0 370.6 jit_solution(13099954725056055062)
XLA Ops:
  7.2 4.8 %all-to-all-start = ((bf16[8,96,1024]{2,1,0:T(8,128)(2,1)}), bf16[8,96,1024]{2,1,0:T(8,128)(2,1)}, u32[]{:S(2)}, u32[]{:S(2)}) async-start(bf16[8,96,1024]{2,1,0:T(8,128)(2,1)} %bitcast.114), calls=%async_computation | async-start | bytes 3145728 | tf_op jit(solution)/shard_map/all_to_all | solution.py:122
  21.9 9.8 %all-to-all-done = bf16[8,96,1024]{2,1,0:T(8,128)(2,1)} async-done(((bf16[8,96,1024]{2,1,0:T(8,128)(2,1)}), bf16[8,96,1024]{2,1,0:T(8,128)(2,1)}, u32[]{:S(2)}, u32[]{:S(2)}) %all-to-all-start) | async-done | bytes 1572896 | tf_op jit(solution)/shard_map/all_to_all | solution.py:122
  35.0 5.1 %pack.3 = (bf16[192,1792]{1,0:T(8,128)(2,1)S(1)}, bf16[192,1792]{1,0:T(8,128)(2,1)S(1)}, bf16[192,1792]{1,0:T(8,128)(2,1)}, bf16[192,1792]{1,0:T(8,128)(2,1)S(1)}) custom-call(s32[12]{0:T(128)S(1)} %reshape.288.info, bf16[768,1792]{1,0:T(8,128)(2,1)S(1)} %copy-done, bf16[768,1792]{1,0:T(8,128)(2,1)S(1)} %copy-done, bf16[768,1792]{1,0:T(8,128)(2,1)S(1)} %copy-done, ...), custom_call_target="tpu_custom_call" | custom-call | tf_op jit(solution)/shard_map/pack/pallas_call | solution.py:55
  40.1 16.4 %collective-permute-done.1.refs_5_ = bf16[192,1024]{1,0:T(8,128)(2,1)} collective-permute-done((bf16[192,1024]{1,0:T(8,128)(2,1)}, bf16[192,1024]{1,0:T(8,128)(2,1)}, u32[]{:S(2)}, u32[]{:S(2)}) %collective-permute-start.1) | collective-permute-done | bytes 393248 | tf_op jit(solution)/shard_map/ppermute | solution.py:79
  56.5 8.3 %collective-permute-done.2.refs_6_ = bf16[192,1024]{1,0:T(8,128)(2,1)} collective-permute-done((bf16[192,1024]{1,0:T(8,128)(2,1)}, bf16[192,1024]{1,0:T(8,128)(2,1)}, u32[]{:S(2)}, u32[]{:S(2)}) %collective-permute-start.2) | collective-permute-done | bytes 393248 | tf_op jit(solution)/shard_map/ppermute | solution.py:79
  69.9 10.8 %collective-permute-done.6 = f32[12,64,64]{2,1,0:T(8,128)S(1)} collective-permute-done((f32[12,64,64]{2,1,0:T(8,128)S(1)}, f32[12,64,64]{2,1,0:T(8,128)S(1)}, u32[]{:S(2)}, u32[]{:S(2)}) %collective-permute-start.6) | collective-permute-done | bytes 196640 | tf_op jit(solution)/shard_map/ppermute | solution.py:24
  82.3 8.9 %collective-permute-done.7 = f32[12,64,64]{2,1,0:T(8,128)S(1)} collective-permute-done((f32[12,64,64]{2,1,0:T(8,128)S(1)}, f32[12,64,64]{2,1,0:T(8,128)S(1)}, u32[]{:S(2)}, u32[]{:S(2)}) %collective-permute-start.7) | collective-permute-done | bytes 196640 | tf_op jit(solution)/shard_map/ppermute | solution.py:24
  101.8 17.4 %collective-permute-done.8 = bf16[192,1024]{1,0:T(8,128)(2,1)S(1)} collective-permute-done((bf16[192,1024]{1,0:T(8,128)(2,1)S(1)}, bf16[192,1024]{1,0:T(8,128)(2,1)S(1)}, u32[]{:S(2)}, u32[]{:S(2)}) %collective-permute-start.8) | collective-permute-done | bytes 393248 | tf_op jit(solution)/shard_map/ppermute | solution.py:322
  130.1 13.1 %partial_sums.7 = bf16[768,1792]{1,0:T(8,128)(2,1)} custom-call(s32[11]{0:T(128)S(1)} %pad_add_fusion.2.info, bf16[8,1,2,96,1024]{4,3,2,1,0:T(8,128)(2,1)S(1)} %copy-done.5, bf16[1792,2048]{1,0:T(8,128)(2,1)} %w_ref.9, bf16[4,3,64,64]{3,2,1,0:T(8,128)(2,1)S(1)} %bitcast.115, bf16[16,64,1792]{2,1,0:T(8,128)(2,1)} %rest_2_.9, bf16[16,64,1792]{2,1,0:T(8,128)(2,1)} %rest_2_.9, ...), custom_call_target="tpu_custom_call" | custom-call | tf_op jit(solution)/shard_map/partial_sums/pallas_call | solution.py:165
  144.5 4.2 %collective-permute-start.13 = (bf16[192,1792]{1,0:T(8,128)(2,1)S(1)}, bf16[192,1792]{1,0:T(8,128)(2,1)}, u32[]{:S(2)}, u32[]{:S(2)}) collective-permute-start(bf16[192,1792]{1,0:T(8,128)(2,1)S(1)} %copy-done.14), channel_id=1, source_target_pairs={{8,16},{16,8},{9,17},{17,9},{10,18},{18,10},{11,19},{19,11},{12,20... | collective-permute-start | bytes 2064392 | tf_op jit(solution)/shard_map/ppermute | solution.py:79
  152.0 13.2 %collective-permute-done.13 = bf16[192,1792]{1,0:T(8,128)(2,1)} collective-permute-done((bf16[192,1792]{1,0:T(8,128)(2,1)S(1)}, bf16[192,1792]{1,0:T(8,128)(2,1)}, u32[]{:S(2)}, u32[]{:S(2)}) %collective-permute-start.13) | collective-permute-done | bytes 688160 | tf_op jit(solution)/shard_map/ppermute | solution.py:79
  166.3 34.3 %all-gather.6.cloned.1.call-done = bf16[32,2,96,1024]{3,2,1,0:T(8,128)(2,1)} async-done(((bf16[4,2,96,1024]{3,2,1,0:T(8,128)(2,1)}), bf16[32,2,96,1024]{3,2,1,0:T(8,128)(2,1)}) %all-gather.6.cloned.1.call-update) | async-done | bytes 12582928 | tf_op jit(solution)/shard_map/all_gather | solution.py:315
  200.6 13.7 %partial_sums.6 = bf16[768,1792]{1,0:T(8,128)(2,1)S(1)} custom-call(s32[11]{0:T(128)S(1)} %pad_add_fusion.3.info, bf16[8,4,2,96,1024]{4,3,2,1,0:T(8,128)(2,1)} %bitcast.129, bf16[1792,2048]{1,0:T(8,128)(2,1)} %w_ref.9, bf16[4,3,64,64]{3,2,1,0:T(8,128)(2,1)S(1)} %bitcast.116, bf16[16,64,1792]{2,1,0:T(8,128)(2,1)} %rest_2_.9, bf16[16,64,1792]{2,1,0:T(8,128)(2,1)} %rest_2_.9, ...), custom_call_target="tpu_custom_call" | custom-call | tf_op jit(solution)/shard_map/partial_sums/pallas_call | solution.py:165
  214.3 4.1 %add_convert_fusion.2 = bf16[768,1792]{1,0:T(8,128)(2,1)} fusion(bf16[768,1792]{1,0:T(8,128)(2,1)} %collective-permute-done.14, bf16[768,1792]{1,0:T(8,128)(2,1)S(1)} %partial_sums.6), kind=kLoop, calls=%fused_computation.5 | loop fusion | flops 5505024 | bytes 8257536 | tf_op jit(solution)/shard_map/convert_element_type | solution.py:359
  225.6 4.9 %factor_parts.3 = f32[12,64,64]{2,1,0:T(8,128)} custom-call(s32[12]{0:T(128)S(1)} %reshape.292.slots, bf16[16,64,1792]{2,1,0:T(8,128)(2,1)} %rest_2_.9, bf16[16,64,1792]{2,1,0:T(8,128)(2,1)} %rest_2_.9, bf16[16,64,1792]{2,1,0:T(8,128)(2,1)} %rest_2_.9, bf16[192,1792]{1,0:T(8,128)(2,1)S(1)} %copy-done.7, ...), custom_call_target="tpu_custom_call" | custom-call | tf_op jit(solution)/shard_map/factor_parts/pallas_call | solution.py:101
  234.3 10.4 %collective-permute-done.18 = f32[12,64,64]{2,1,0:T(8,128)S(1)} collective-permute-done((f32[12,64,64]{2,1,0:T(8,128)S(1)}, f32[12,64,64]{2,1,0:T(8,128)S(1)}, u32[]{:S(2)}, u32[]{:S(2)}) %collective-permute-start.18) | collective-permute-done | bytes 196640 | tf_op jit(solution)/shard_map/ppermute | solution.py:24
  245.4 13.7 %partial_sums.5 = bf16[768,1792]{1,0:T(8,128)(2,1)S(1)} custom-call(s32[11]{0:T(128)S(1)} %pad_add_fusion.5.info, bf16[8,4,2,96,1024]{4,3,2,1,0:T(8,128)(2,1)} %bitcast.130, bf16[1792,2048]{1,0:T(8,128)(2,1)} %w_ref.9, bf16[4,3,64,64]{3,2,1,0:T(8,128)(2,1)S(1)} %bitcast.117, bf16[16,64,1792]{2,1,0:T(8,128)(2,1)} %rest_2_.9, bf16[16,64,1792]{2,1,0:T(8,128)(2,1)} %rest_2_.9, ...), custom_call_target="tpu_custom_call" | custom-call | tf_op jit(solution)/shard_map/partial_sums/pallas_call | solution.py:165
  259.1 13.7 %partial_sums.8 = bf16[768,1792]{1,0:T(8,128)(2,1)S(1)} custom-call(s32[11]{0:T(128)S(1)} %pad_add_fusion.6.info, bf16[8,4,2,96,1024]{4,3,2,1,0:T(8,128)(2,1)} %bitcast.131, bf16[1792,2048]{1,0:T(8,128)(2,1)} %w_ref.9, bf16[4,3,64,64]{3,2,1,0:T(8,128)(2,1)S(1)} %bitcast.118, bf16[16,64,1792]{2,1,0:T(8,128)(2,1)} %rest_2_.9, bf16[16,64,1792]{2,1,0:T(8,128)(2,1)} %rest_2_.9, ...), custom_call_target="tpu_custom_call" | custom-call | tf_op jit(solution)/shard_map/partial_sums/pallas_call | solution.py:165
  272.8 9.9 %collective-permute-done.15 = bf16[768,1792]{1,0:T(8,128)(2,1)} collective-permute-done((bf16[768,1792]{1,0:T(8,128)(2,1)}, bf16[768,1792]{1,0:T(8,128)(2,1)}, u32[]{:S(2)}, u32[]{:S(2)}) %collective-permute-start.15) | collective-permute-done | bytes 2752544 | tf_op jit(solution)/shard_map/ppermute | solution.py:394
  298.3 13.7 %partial_sums.9.own = bf16[768,1792]{1,0:T(8,128)(2,1)S(1)} custom-call(s32[11]{0:T(128)S(1)} %pad_add_fusion.4.info, bf16[8,4,2,96,1024]{4,3,2,1,0:T(8,128)(2,1)} %bitcast.132, bf16[1792,2048]{1,0:T(8,128)(2,1)} %w_ref.9, bf16[4,3,64,64]{3,2,1,0:T(8,128)(2,1)S(1)} %bitcast.119, bf16[16,64,1792]{2,1,0:T(8,128)(2,1)} %rest_2_.9, ...), custom_call_target="tpu_custom_call" | custom-call | tf_op jit(solution)/shard_map/partial_sums/pallas_call | solution.py:165
  316.8 7.3 %copy.89 = f32[16,64,1792]{2,1,0:T(8,128)} copy(f32[16,64,1792]{2,0,1:T(8,128)S(1)} %fusion) | data formatting | bytes 14680064
  330.1 4.4 %copy.90 = f32[16,64,1024]{2,1,0:T(8,128)} copy(f32[16,64,1024]{2,0,1:T(8,128)S(1)} %fusion.7) | data formatting | bytes 8388608
  334.6 16.6 %collective-permute-done.20.left = bf16[768,1792]{1,0:T(8,128)(2,1)} collective-permute-done((bf16[768,1792]{1,0:T(8,128)(2,1)}, bf16[768,1792]{1,0:T(8,128)(2,1)}, u32[]{:S(2)}, u32[]{:S(2)}) %collective-permute-start.20) | collective-permute-done | bytes 2752544 | tf_op jit(solution)/shard_map/ppermute | solution.py:394
  355.0 8.7 %finish.1 = (bf16[768,1792]{1,0:T(8,128)(2,1)}, bf16[768,1792]{1,0:T(8,128)(2,1)}) custom-call(bf16[768,1792]{1,0:T(8,128)(2,1)S(1)} %partial_sums.9.own, bf16[768,1792]{1,0:T(8,128)(2,1)} %collective-permute-done.20.left, bf16[768,1792]{1,0:T(8,128)(2,1)} %collective-permute-done.21.right, bf16[768,1792]{1,0:T(8,128)(2,1)} %gate.1, bf16[768,1792]{1,0:T(8,128)(2,1)} %up.1), custom_call_target="tpu_custom_call" | custom-call | tf_op jit(solution)/shard_map/finish/pallas_call | solution.py:218
  (154 shorter events, 88.7 us)
Async XLA Ops:
  7.2 24.5 %all-to-all-start = ((bf16[8,96,1024]{2,1,0:T(8,128)(2,1)}), bf16[8,96,1024]{2,1,0:T(8,128)(2,1)}, u32[]{:S(2)}, u32[]{:S(2)}) async-start(bf16[8,96,1024]{2,1,0:T(8,128)(2,1)} %bitcast.114), calls=%async_computation | async-start | bytes 3145728 | tf_op jit(solution)/shard_map/all_to_all | solution.py:122
  12.0 112.7 %all-gather.4.cloned.1.call-start = ((), (), s32[]{:S(2)}) async-start(), calls=%async_computation.1 | async-start | bytes 3538944 | tf_op jit(solution)/shard_map/all_gather | solution.py:315
  18.4 21.7 %collective-permute-start = (bf16[192,1024]{1,0:T(8,128)(2,1)}, bf16[192,1024]{1,0:T(8,128)(2,1)}, u32[]{:S(2)}, u32[]{:S(2)}) collective-permute-start(bf16[192,1024]{1,0:T(8,128)(2,1)} %get-tuple-element.54), channel_id=1, source_target_pairs={{0,8},{8,0},{16,24},{24,16},{1,9},{9,1},{17,25},{25,17},{2,10},{10... | collective-permute-start | bytes 1179656 | tf_op jit(solution)/shard_map/ppermute | solution.py:79
  18.4 38.1 %collective-permute-start.1 = (bf16[192,1024]{1,0:T(8,128)(2,1)}, bf16[192,1024]{1,0:T(8,128)(2,1)}, u32[]{:S(2)}, u32[]{:S(2)}) collective-permute-start(bf16[192,1024]{1,0:T(8,128)(2,1)} %get-tuple-element.55), channel_id=1, source_target_pairs={{0,16},{8,24},{16,0},{24,8},{1,17},{9,25},{17,1},{25,9},{2,18},{10... | collective-permute-start | bytes 1179656 | tf_op jit(solution)/shard_map/ppermute | solution.py:79
  21.4 43.4 %collective-permute-start.2 = (bf16[192,1024]{1,0:T(8,128)(2,1)}, bf16[192,1024]{1,0:T(8,128)(2,1)}, u32[]{:S(2)}, u32[]{:S(2)}) collective-permute-start(bf16[192,1024]{1,0:T(8,128)(2,1)} %get-tuple-element.56), channel_id=1, source_target_pairs={{0,24},{8,16},{16,8},{24,0},{1,25},{9,17},{17,9},{25,1},{2,26},{10... | collective-permute-start | bytes 1179656 | tf_op jit(solution)/shard_map/ppermute | solution.py:79
  33.4 31.4 %collective-permute-start.3 = (bf16[192,1024]{1,0:T(8,128)(2,1)}, bf16[192,1024]{1,0:T(8,128)(2,1)}, u32[]{:S(2)}, u32[]{:S(2)}) collective-permute-start(bf16[192,1024]{1,0:T(8,128)(2,1)} %bitcast.7), channel_id=1, source_target_pairs={{0,24},{24,0},{1,25},{25,1},{2,26},{26,2},{3,27},{27,3},{4,28},{28... | collective-permute-start | bytes 1179656 | tf_op jit(solution)/shard_map/ppermute | solution.py:79
  67.8 23.5 %collective-permute-start.4 = (bf16[192,1792]{1,0:T(8,128)(2,1)S(1)}, bf16[192,1792]{1,0:T(8,128)(2,1)S(1)}, u32[]{:S(2)}, u32[]{:S(2)}) collective-permute-start(bf16[192,1792]{1,0:T(8,128)(2,1)S(1)} %get-tuple-element.59), channel_id=1, source_target_pairs={{0,24},{24,0},{1,25},{25,1},{2,26},{26,2},{3,27},{27,3},{4,28},{28... | collective-permute-start | bytes 2064392 | tf_op jit(solution)/shard_map/ppermute | solution.py:79
  69.5 11.2 %collective-permute-start.6 = (f32[12,64,64]{2,1,0:T(8,128)S(1)}, f32[12,64,64]{2,1,0:T(8,128)S(1)}, u32[]{:S(2)}, u32[]{:S(2)}) collective-permute-start(f32[12,64,64]{2,1,0:T(8,128)S(1)} %add.114), channel_id=1, source_target_pairs={{0,2},{1,3},{2,0},{3,1},{4,6},{5,7},{6,4},{7,5},{8,10},{9,11},{10,... | collective-permute-start | bytes 589832 | tf_op jit(solution)/shard_map/ppermute | solution.py:24
  80.8 10.4 %collective-permute-start.7 = (f32[12,64,64]{2,1,0:T(8,128)S(1)}, f32[12,64,64]{2,1,0:T(8,128)S(1)}, u32[]{:S(2)}, u32[]{:S(2)}) collective-permute-start(f32[12,64,64]{2,1,0:T(8,128)S(1)} %add.115), channel_id=1, source_target_pairs={{0,4},{1,5},{2,6},{3,7},{4,0},{5,1},{6,2},{7,3},{8,12},{9,13},{10,... | collective-permute-start | bytes 589832 | tf_op jit(solution)/shard_map/ppermute | solution.py:24
  91.3 109.3 %all-gather.6.cloned.1.call-start = ((), (), s32[]{:S(2)}) async-start(), calls=%async_computation.2 | async-start | bytes 14155776 | tf_op jit(solution)/shard_map/all_gather | solution.py:315
  91.3 33.4 %collective-permute-start.11 = (bf16[192,1792]{1,0:T(8,128)(2,1)S(1)}, bf16[192,1792]{1,0:T(8,128)(2,1)S(1)}, u32[]{:S(2)}, u32[]{:S(2)}) collective-permute-start(bf16[192,1792]{1,0:T(8,128)(2,1)S(1)} %copy-done.16), channel_id=1, source_target_pairs={{0,8},{8,0},{16,24},{24,16},{1,9},{9,1},{17,25},{25,17},{2,10},{10... | collective-permute-start | bytes 2064392 | tf_op jit(solution)/shard_map/ppermute | solution.py:79
  92.9 26.3 %collective-permute-start.8 = (bf16[192,1024]{1,0:T(8,128)(2,1)S(1)}, bf16[192,1024]{1,0:T(8,128)(2,1)S(1)}, u32[]{:S(2)}, u32[]{:S(2)}) collective-permute-start(bf16[192,1024]{1,0:T(8,128)(2,1)S(1)} %bitcast.141), channel_id=1, source_target_pairs={{0,16},{8,24},{16,0},{24,8},{1,17},{9,25},{17,1},{25,9},{2,18},{10... | collective-permute-start | bytes 1179656 | tf_op jit(solution)/shard_map/ppermute | solution.py:322
  96.0 25.8 %collective-permute-start.9 = (bf16[192,1024]{1,0:T(8,128)(2,1)S(1)}, bf16[192,1024]{1,0:T(8,128)(2,1)S(1)}, u32[]{:S(2)}, u32[]{:S(2)}) collective-permute-start(bf16[192,1024]{1,0:T(8,128)(2,1)S(1)} %bitcast.140), channel_id=1, source_target_pairs={{8,0},{16,8},{24,16},{9,1},{17,9},{25,17},{10,2},{18,10},{26,18},{... | collective-permute-start | bytes 1179656 | tf_op jit(solution)/shard_map/ppermute | solution.py:323
  97.9 26.1 %collective-permute-start.10 = (bf16[192,1024]{1,0:T(8,128)(2,1)S(1)}, bf16[192,1024]{1,0:T(8,128)(2,1)S(1)}, u32[]{:S(2)}, u32[]{:S(2)}) collective-permute-start(bf16[192,1024]{1,0:T(8,128)(2,1)S(1)} %bitcast.139), channel_id=1, source_target_pairs={{0,8},{8,16},{16,24},{1,9},{9,17},{17,25},{2,10},{10,18},{18,26},{... | collective-permute-start | bytes 1179656 | tf_op jit(solution)/shard_map/ppermute | solution.py:324
  143.2 71.1 %collective-permute-start.14 = (bf16[768,1792]{1,0:T(8,128)(2,1)}, bf16[768,1792]{1,0:T(8,128)(2,1)}, u32[]{:S(2)}, u32[]{:S(2)}) collective-permute-start(bf16[768,1792]{1,0:T(8,128)(2,1)} %partial_sums.7), channel_id=1, source_target_pairs={{0,8},{24,16},{1,9},{25,17},{2,10},{26,18},{3,11},{27,19},{4,12},{... | collective-permute-start | bytes 8257544 | tf_op jit(solution)/shard_map/ppermute | solution.py:387
  144.5 20.7 %collective-permute-start.13 = (bf16[192,1792]{1,0:T(8,128)(2,1)S(1)}, bf16[192,1792]{1,0:T(8,128)(2,1)}, u32[]{:S(2)}, u32[]{:S(2)}) collective-permute-start(bf16[192,1792]{1,0:T(8,128)(2,1)S(1)} %copy-done.14), channel_id=1, source_target_pairs={{8,16},{16,8},{9,17},{17,9},{10,18},{18,10},{11,19},{19,11},{12,20... | collective-permute-start | bytes 2064392 | tf_op jit(solution)/shard_map/ppermute | solution.py:79
  148.7 72.9 %collective-permute-start.12 = (bf16[192,1792]{1,0:T(8,128)(2,1)}, bf16[192,1792]{1,0:T(8,128)(2,1)S(1)}, u32[]{:S(2)}, u32[]{:S(2)}) collective-permute-start(bf16[192,1792]{1,0:T(8,128)(2,1)} %get-tuple-element.79), channel_id=1, source_target_pairs={{0,16},{8,24},{16,0},{24,8},{1,17},{9,25},{17,1},{25,9},{2,18},{10... | collective-permute-start | bytes 2064392 | tf_op jit(solution)/shard_map/ppermute | solution.py:79
  221.6 61.1 %collective-permute-start.15 = (bf16[768,1792]{1,0:T(8,128)(2,1)}, bf16[768,1792]{1,0:T(8,128)(2,1)}, u32[]{:S(2)}, u32[]{:S(2)}) collective-permute-start(bf16[768,1792]{1,0:T(8,128)(2,1)} %add_convert_fusion.2), channel_id=1, source_target_pairs={{0,8},{8,16},{1,9},{9,17},{2,10},{10,18},{3,11},{11,19},{4,12},{12... | collective-permute-start | bytes 8257544 | tf_op jit(solution)/shard_map/ppermute | solution.py:394
  224.1 62.7 %collective-permute-start.16 = (bf16[768,1792]{1,0:T(8,128)(2,1)}, bf16[768,1792]{1,0:T(8,128)(2,1)}, u32[]{:S(2)}, u32[]{:S(2)}) collective-permute-start(bf16[768,1792]{1,0:T(8,128)(2,1)} %add_convert_fusion.2), channel_id=1, source_target_pairs={{24,16},{16,8},{25,17},{17,9},{26,18},{18,10},{27,19},{19,11},{28,... | collective-permute-start | bytes 8257544 | tf_op jit(solution)/shard_map/ppermute | solution.py:395
  230.5 1.9 collective-permute-start.17
  233.5 11.2 %collective-permute-start.18 = (f32[12,64,64]{2,1,0:T(8,128)S(1)}, f32[12,64,64]{2,1,0:T(8,128)S(1)}, u32[]{:S(2)}, u32[]{:S(2)}) collective-permute-start(f32[12,64,64]{2,1,0:T(8,128)S(1)} %add.124), channel_id=1, source_target_pairs={{0,2},{1,3},{2,0},{3,1},{4,6},{5,7},{6,4},{7,5},{8,10},{9,11},{10,... | collective-permute-start | bytes 589832 | tf_op jit(solution)/shard_map/ppermute | solution.py:24
  244.7 28.0 %collective-permute-start.19 = (f32[12,64,64]{2,1,0:T(8,128)S(1)}, f32[12,64,64]{2,1,0:T(8,128)S(1)}, u32[]{:S(2)}, u32[]{:S(2)}) collective-permute-start(f32[12,64,64]{2,1,0:T(8,128)S(1)} %add.125), channel_id=1, source_target_pairs={{0,4},{1,5},{2,6},{3,7},{4,0},{5,1},{6,2},{7,3},{8,12},{9,13},{10,... | collective-permute-start | bytes 589832 | tf_op jit(solution)/shard_map/ppermute | solution.py:24
  290.8 60.4 %collective-permute-start.20 = (bf16[768,1792]{1,0:T(8,128)(2,1)}, bf16[768,1792]{1,0:T(8,128)(2,1)}, u32[]{:S(2)}, u32[]{:S(2)}) collective-permute-start(bf16[768,1792]{1,0:T(8,128)(2,1)} %add_convert_fusion.1), channel_id=1, source_target_pairs={{0,8},{8,16},{16,24},{1,9},{9,17},{17,25},{2,10},{10,18},{18,26},{... | collective-permute-start | bytes 8257544 | tf_op jit(solution)/shard_map/ppermute | solution.py:394
  294.2 60.8 %collective-permute-start.21 = (bf16[768,1792]{1,0:T(8,128)(2,1)}, bf16[768,1792]{1,0:T(8,128)(2,1)}, u32[]{:S(2)}, u32[]{:S(2)}) collective-permute-start(bf16[768,1792]{1,0:T(8,128)(2,1)} %add_convert_fusion), channel_id=1, source_target_pairs={{24,16},{16,8},{8,0},{25,17},{17,9},{9,1},{26,18},{18,10},{10,2},{... | collective-permute-start | bytes 8257544 | tf_op jit(solution)/shard_map/ppermute | solution.py:395
  (22 other events, 410.9 us)
Sparse Core Ops, SparseCore 0:
  91.4 32.3 all-gather.3
  127.6 72.9 all-gather.5

commit v5 on v4

--- a/solution.py
+++ b/solution.py
@@ -195,10 +195,9 @@
     )(info, units, weight, factors, *[first] * capacity)
 
 
-def finish_kernel(own, left, right, gate, up, *rest):
+def finish_kernel(own, right, gate, up, *rest):
     d_gate, d_up = rest[-2:]
-    d_hidden = own[...].astype(jnp.float32) + left[...].astype(jnp.float32)
-    d_hidden += right[...].astype(jnp.float32)
+    d_hidden = own[...].astype(jnp.float32) + right[...].astype(jnp.float32)
     gate_float = gate[...].astype(jnp.float32)
     up_float = up[...].astype(jnp.float32)
     squash = jax.nn.sigmoid(gate_float)
@@ -208,7 +207,7 @@
     d_up[...] = (d_hidden * activated).astype(d_up.dtype)
 
 
-def finish(own, left, right, gate, up, part, earlier):
+def finish(own, right, gate, up, part, earlier):
     rows, ff_local = own.shape
     step = 128 if rows % 128 == 0 else rows
     steps = rows // step
@@ -218,13 +217,13 @@
     return pl.pallas_call(
         finish_kernel,
         grid=(steps,),
-        in_specs=[here, here, here, there, there] + [pl.BlockSpec(memory_space=pl.ANY)] * len(before),
+        in_specs=[here, here, there, there] + [pl.BlockSpec(memory_space=pl.ANY)] * len(before),
         out_specs=[there, there],
         out_shape=[jax.ShapeDtypeStruct(gate.shape, gate.dtype) for _ in range(2)],
-        input_output_aliases={5: 0, 6: 1} if before else {},
+        input_output_aliases={4: 0, 5: 1} if before else {},
         compiler_params=pltpu.CompilerParams(vmem_limit_bytes=VMEM_BYTES),
         name="finish",
-    )(own, left, right, gate, up, *before)
+    )(own, right, gate, up, *before)
 
 
 def shards(
@@ -399,7 +398,7 @@
     done = None
     for h in range(halves):
         done = finish(
-            own[h], from_left[h], from_right[h], saved_gate_value, saved_up_value, h, done
+            joined(own[h], from_left[h]), from_right[h], saved_gate_value, saved_up_value, h, done
         )
     d_gate, d_up = done
 

time: 374 us -> 377 us (level)
    convert_element_type x3 -> x4, other arithmetic: 12.1 us -> 14.6 us  [joined(): return total.astype(jnp.bfloat16)]
    unnamed x44 -> x32, local copies, waits for them, and re-layouts: 16.8 us -> 15.9 us
  transfers between devices with their start and end apart: 25 -> 25, of which waited for: 17 -> 17; matrix products, arithmetic and copies ran while one was open for 11% -> 12% of each run, Pallas kernels for 21% -> 21%
where the time goes in v5:
time: 377 us; the launch traced here: 372 us
  waiting for transfers between devices  169 us (45%)
  Pallas kernels  90.7 us (24%)
  starting transfers between devices  42.3 us (11%)
  other arithmetic  23 us (6%)
  local copies, waits for them, and re-layouts  22.9 us (6%)
  between operations  14.5 us (4%)
  matrix products  8.87 us (2%)
    pallas_call x5, Pallas kernels, partial_sums(): pl.pallas_call(functools.partial(partial_kernel, capacity), grid_spec=plt...  68 us
    ppermute x8, waiting for transfers between devices, swap_over_dp(): lax.ppermute(x, 'dp', [(i, i ^ bits) for i in range(size) if only is None...  42.4 us
    all_gather x2, waiting for transfers between devices, gathered(): lax.all_gather(jnp.stack([u.reshape(moved.shape[1:]) for u in units]), 'm...  34.7 us
    ppermute x6, waiting for transfers between devices, sum_over_mp(): x = x + lax.ppermute(x, 'mp', [(i, i ^ bit) for i in range(size)])  32.5 us
    ppermute x2, waiting for transfers between devices, shards(): from_left = [lax.ppermute(s, 'dp', pairs_r) for s in send_r]  27.7 us
    ppermute x1, waiting for transfers between devices, shards(): lax.ppermute(unit_of(target_of(2, 0)), 'dp', pairs)  17.4 us
    unnamed x32, local copies, waits for them, and re-layouts  15.9 us
    convert_element_type x4, other arithmetic, joined(): return total.astype(jnp.bfloat16)  14.6 us
  transfers between devices with their start and end apart: 25, of which 17 were waited for; matrix products, arithmetic and copies ran while one was open for 12% of the time, Pallas kernels for 21%

profile of v5, /device:TPU:10, one launch (start us, length us, event | category | flops | bytes accessed | tf_op | source)
XLA Modules:
  0.0 371.7 jit_solution(2902294036080795067)
XLA Ops:
  7.2 4.9 %all-to-all-start = ((bf16[8,96,1024]{2,1,0:T(8,128)(2,1)}), bf16[8,96,1024]{2,1,0:T(8,128)(2,1)}, u32[]{:S(2)}, u32[]{:S(2)}) async-start(bf16[8,96,1024]{2,1,0:T(8,128)(2,1)} %bitcast.114), calls=%async_computation | async-start | bytes 3145728 | tf_op jit(solution)/shard_map/all_to_all | solution.py:122
  21.9 9.8 %all-to-all-done = bf16[8,96,1024]{2,1,0:T(8,128)(2,1)} async-done(((bf16[8,96,1024]{2,1,0:T(8,128)(2,1)}), bf16[8,96,1024]{2,1,0:T(8,128)(2,1)}, u32[]{:S(2)}, u32[]{:S(2)}) %all-to-all-start) | async-done | bytes 1572896 | tf_op jit(solution)/shard_map/all_to_all | solution.py:122
  35.0 5.1 %pack.3 = (bf16[192,1792]{1,0:T(8,128)(2,1)S(1)}, bf16[192,1792]{1,0:T(8,128)(2,1)S(1)}, bf16[192,1792]{1,0:T(8,128)(2,1)}, bf16[192,1792]{1,0:T(8,128)(2,1)S(1)}) custom-call(s32[12]{0:T(128)S(1)} %reshape.288.info, bf16[768,1792]{1,0:T(8,128)(2,1)S(1)} %copy-done, bf16[768,1792]{1,0:T(8,128)(2,1)S(1)} %copy-done, bf16[768,1792]{1,0:T(8,128)(2,1)S(1)} %copy-done, ...), custom_call_target="tpu_custom_call" | custom-call | tf_op jit(solution)/shard_map/pack/pallas_call | solution.py:55
  40.1 16.4 %collective-permute-done.1.refs_5_ = bf16[192,1024]{1,0:T(8,128)(2,1)} collective-permute-done((bf16[192,1024]{1,0:T(8,128)(2,1)}, bf16[192,1024]{1,0:T(8,128)(2,1)}, u32[]{:S(2)}, u32[]{:S(2)}) %collective-permute-start.1) | collective-permute-done | bytes 393248 | tf_op jit(solution)/shard_map/ppermute | solution.py:79
  56.6 8.3 %collective-permute-done.2.refs_6_ = bf16[192,1024]{1,0:T(8,128)(2,1)} collective-permute-done((bf16[192,1024]{1,0:T(8,128)(2,1)}, bf16[192,1024]{1,0:T(8,128)(2,1)}, u32[]{:S(2)}, u32[]{:S(2)}) %collective-permute-start.2) | collective-permute-done | bytes 393248 | tf_op jit(solution)/shard_map/ppermute | solution.py:79
  69.9 10.8 %collective-permute-done.6 = f32[12,64,64]{2,1,0:T(8,128)S(1)} collective-permute-done((f32[12,64,64]{2,1,0:T(8,128)S(1)}, f32[12,64,64]{2,1,0:T(8,128)S(1)}, u32[]{:S(2)}, u32[]{:S(2)}) %collective-permute-start.6) | collective-permute-done | bytes 196640 | tf_op jit(solution)/shard_map/ppermute | solution.py:24
  82.3 8.8 %collective-permute-done.7 = f32[12,64,64]{2,1,0:T(8,128)S(1)} collective-permute-done((f32[12,64,64]{2,1,0:T(8,128)S(1)}, f32[12,64,64]{2,1,0:T(8,128)S(1)}, u32[]{:S(2)}, u32[]{:S(2)}) %collective-permute-start.7) | collective-permute-done | bytes 196640 | tf_op jit(solution)/shard_map/ppermute | solution.py:24
  102.7 17.4 %collective-permute-done.8 = bf16[192,1024]{1,0:T(8,128)(2,1)S(1)} collective-permute-done((bf16[192,1024]{1,0:T(8,128)(2,1)S(1)}, bf16[192,1024]{1,0:T(8,128)(2,1)S(1)}, u32[]{:S(2)}, u32[]{:S(2)}) %collective-permute-start.8) | collective-permute-done | bytes 393248 | tf_op jit(solution)/shard_map/ppermute | solution.py:321
  128.8 13.1 %partial_sums.7 = bf16[768,1792]{1,0:T(8,128)(2,1)} custom-call(s32[11]{0:T(128)S(1)} %pad_add_fusion.2.info, bf16[8,1,2,96,1024]{4,3,2,1,0:T(8,128)(2,1)S(1)} %copy-done.3, bf16[1792,2048]{1,0:T(8,128)(2,1)} %w_ref.9, bf16[4,3,64,64]{3,2,1,0:T(8,128)(2,1)S(1)} %bitcast.115, bf16[16,64,1792]{2,1,0:T(8,128)(2,1)} %rest_2_.9, bf16[16,64,1792]{2,1,0:T(8,128)(2,1)} %rest_2_.9, ...), custom_call_target="tpu_custom_call" | custom-call | tf_op jit(solution)/shard_map/partial_sums/pallas_call | solution.py:165
  150.1 13.5 %collective-permute-done.13 = bf16[192,1792]{1,0:T(8,128)(2,1)} collective-permute-done((bf16[192,1792]{1,0:T(8,128)(2,1)S(1)}, bf16[192,1792]{1,0:T(8,128)(2,1)}, u32[]{:S(2)}, u32[]{:S(2)}) %collective-permute-start.13) | collective-permute-done | bytes 688160 | tf_op jit(solution)/shard_map/ppermute | solution.py:79
  164.7 34.7 %all-gather.6.cloned.1.call-done = bf16[32,2,96,1024]{3,2,1,0:T(8,128)(2,1)} async-done(((bf16[4,2,96,1024]{3,2,1,0:T(8,128)(2,1)}), bf16[32,2,96,1024]{3,2,1,0:T(8,128)(2,1)}) %all-gather.6.cloned.1.call-update) | async-done | bytes 12582928 | tf_op jit(solution)/shard_map/all_gather | solution.py:314
  199.4 13.7 %partial_sums.6 = bf16[768,1792]{1,0:T(8,128)(2,1)S(1)} custom-call(s32[11]{0:T(128)S(1)} %pad_add_fusion.3.info, bf16[8,4,2,96,1024]{4,3,2,1,0:T(8,128)(2,1)} %bitcast.129, bf16[1792,2048]{1,0:T(8,128)(2,1)} %w_ref.9, bf16[4,3,64,64]{3,2,1,0:T(8,128)(2,1)S(1)} %bitcast.116, bf16[16,64,1792]{2,1,0:T(8,128)(2,1)} %rest_2_.9, bf16[16,64,1792]{2,1,0:T(8,128)(2,1)} %rest_2_.9, ...), custom_call_target="tpu_custom_call" | custom-call | tf_op jit(solution)/shard_map/partial_sums/pallas_call | solution.py:165
  217.1 4.2 %collective-permute-done.12.refs_5_ = bf16[192,1792]{1,0:T(8,128)(2,1)S(1)} collective-permute-done((bf16[192,1792]{1,0:T(8,128)(2,1)}, bf16[192,1792]{1,0:T(8,128)(2,1)S(1)}, u32[]{:S(2)}, u32[]{:S(2)}) %collective-permute-start.12) | collective-permute-done | bytes 688160 | tf_op jit(solution)/shard_map/ppermute | solution.py:79
  225.4 4.9 %factor_parts.3 = f32[12,64,64]{2,1,0:T(8,128)} custom-call(s32[12]{0:T(128)S(1)} %reshape.292.slots, bf16[16,64,1792]{2,1,0:T(8,128)(2,1)} %rest_2_.9, bf16[16,64,1792]{2,1,0:T(8,128)(2,1)} %rest_2_.9, bf16[16,64,1792]{2,1,0:T(8,128)(2,1)} %rest_2_.9, bf16[192,1792]{1,0:T(8,128)(2,1)S(1)} %copy-done.5, ...), custom_call_target="tpu_custom_call" | custom-call | tf_op jit(solution)/shard_map/factor_parts/pallas_call | solution.py:101
  235.0 10.7 %collective-permute-done.18 = f32[12,64,64]{2,1,0:T(8,128)} collective-permute-done((f32[12,64,64]{2,1,0:T(8,128)}, f32[12,64,64]{2,1,0:T(8,128)}, u32[]{:S(2)}, u32[]{:S(2)}) %collective-permute-start.18) | collective-permute-done | bytes 196640 | tf_op jit(solution)/shard_map/ppermute | solution.py:24
  247.7 13.7 %partial_sums.5 = bf16[768,1792]{1,0:T(8,128)(2,1)S(1)} custom-call(s32[11]{0:T(128)S(1)} %pad_add_fusion.5.info, bf16[8,4,2,96,1024]{4,3,2,1,0:T(8,128)(2,1)} %bitcast.130, bf16[1792,2048]{1,0:T(8,128)(2,1)} %w_ref.9, bf16[4,3,64,64]{3,2,1,0:T(8,128)(2,1)S(1)} %bitcast.117, bf16[16,64,1792]{2,1,0:T(8,128)(2,1)} %rest_2_.9, bf16[16,64,1792]{2,1,0:T(8,128)(2,1)} %rest_2_.9, ...), custom_call_target="tpu_custom_call" | custom-call | tf_op jit(solution)/shard_map/partial_sums/pallas_call | solution.py:165
  261.4 13.7 %partial_sums.8 = bf16[768,1792]{1,0:T(8,128)(2,1)S(1)} custom-call(s32[11]{0:T(128)S(1)} %pad_add_fusion.6.info, bf16[8,4,2,96,1024]{4,3,2,1,0:T(8,128)(2,1)} %bitcast.131, bf16[1792,2048]{1,0:T(8,128)(2,1)} %w_ref.9, bf16[4,3,64,64]{3,2,1,0:T(8,128)(2,1)S(1)} %bitcast.118, bf16[16,64,1792]{2,1,0:T(8,128)(2,1)} %rest_2_.9, bf16[16,64,1792]{2,1,0:T(8,128)(2,1)} %rest_2_.9, ...), custom_call_target="tpu_custom_call" | custom-call | tf_op jit(solution)/shard_map/partial_sums/pallas_call | solution.py:165
  275.1 9.1 %collective-permute-done.15 = bf16[768,1792]{1,0:T(8,128)(2,1)} collective-permute-done((bf16[768,1792]{1,0:T(8,128)(2,1)}, bf16[768,1792]{1,0:T(8,128)(2,1)}, u32[]{:S(2)}, u32[]{:S(2)}) %collective-permute-start.15) | collective-permute-done | bytes 2752544 | tf_op jit(solution)/shard_map/ppermute | solution.py:393
  294.9 4.7 %collective-permute-start.21 = (bf16[768,1792]{1,0:T(8,128)(2,1)}, bf16[768,1792]{1,0:T(8,128)(2,1)}, u32[]{:S(2)}, u32[]{:S(2)}) collective-permute-start(bf16[768,1792]{1,0:T(8,128)(2,1)} %add_convert_fusion.1), channel_id=1, source_target_pairs={{24,16},{16,8},{8,0},{25,17},{17,9},{9,1},{26,18},{18,10},{10,2},{... | collective-permute-start | bytes 8257544 | tf_op jit(solution)/shard_map/ppermute | solution.py:394
  301.6 13.9 %partial_sums.9 = bf16[768,1792]{1,0:T(8,128)(2,1)S(1)} custom-call(s32[11]{0:T(128)S(1)} %pad_add_fusion.4.info, bf16[8,4,2,96,1024]{4,3,2,1,0:T(8,128)(2,1)} %bitcast.132, bf16[1792,2048]{1,0:T(8,128)(2,1)} %w_ref.9, bf16[4,3,64,64]{3,2,1,0:T(8,128)(2,1)S(1)} %bitcast.123, bf16[16,64,1792]{2,1,0:T(8,128)(2,1)} %rest_2_.9, bf16[16,64,1792]{2,1,0:T(8,128)(2,1)} %rest_2_.9, ...), custom_call_target="tpu_custom_call" | custom-call | tf_op jit(solution)/shard_map/partial_sums/pallas_call | solution.py:165
  317.8 7.3 %copy.89 = f32[16,64,1792]{2,1,0:T(8,128)} copy(f32[16,64,1792]{2,0,1:T(8,128)S(1)} %fusion) | data formatting | bytes 14680064
  331.2 4.4 %copy.90 = f32[16,64,1024]{2,1,0:T(8,128)} copy(f32[16,64,1024]{2,0,1:T(8,128)S(1)} %fusion.7) | data formatting | bytes 8388608
  335.6 18.5 %collective-permute-done.20 = bf16[768,1792]{1,0:T(8,128)(2,1)} collective-permute-done((bf16[768,1792]{1,0:T(8,128)(2,1)}, bf16[768,1792]{1,0:T(8,128)(2,1)}, u32[]{:S(2)}, u32[]{:S(2)}) %collective-permute-start.20) | collective-permute-done | bytes 2752544 | tf_op jit(solution)/shard_map/ppermute | solution.py:393
  356.8 8.0 %finish.1 = (bf16[768,1792]{1,0:T(8,128)(2,1)}, bf16[768,1792]{1,0:T(8,128)(2,1)}) custom-call(bf16[768,1792]{1,0:T(8,128)(2,1)S(1)} %add_convert_fusion.own, bf16[768,1792]{1,0:T(8,128)(2,1)} %collective-permute-done.21.right, bf16[768,1792]{1,0:T(8,128)(2,1)} %gate.1, bf16[768,1792]{1,0:T(8,128)(2,1)} %up.1), custom_call_target="tpu_custom_call" | custom-call | tf_op jit(solution)/shard_map/finish/pallas_call | solution.py:217
  (143 shorter events, 87.7 us)
Async XLA Ops:
  7.2 24.5 %all-to-all-start = ((bf16[8,96,1024]{2,1,0:T(8,128)(2,1)}), bf16[8,96,1024]{2,1,0:T(8,128)(2,1)}, u32[]{:S(2)}, u32[]{:S(2)}) async-start(bf16[8,96,1024]{2,1,0:T(8,128)(2,1)} %bitcast.114), calls=%async_computation | async-start | bytes 3145728 | tf_op jit(solution)/shard_map/all_to_all | solution.py:122
  12.0 112.8 %all-gather.4.cloned.1.call-start = ((), (), s32[]{:S(2)}) async-start(), calls=%async_computation.1 | async-start | bytes 3538944 | tf_op jit(solution)/shard_map/all_gather | solution.py:314
  18.4 21.7 %collective-permute-start = (bf16[192,1024]{1,0:T(8,128)(2,1)}, bf16[192,1024]{1,0:T(8,128)(2,1)}, u32[]{:S(2)}, u32[]{:S(2)}) collective-permute-start(bf16[192,1024]{1,0:T(8,128)(2,1)} %get-tuple-element.54), channel_id=1, source_target_pairs={{0,8},{8,0},{16,24},{24,16},{1,9},{9,1},{17,25},{25,17},{2,10},{10... | collective-permute-start | bytes 1179656 | tf_op jit(solution)/shard_map/ppermute | solution.py:79
  18.5 38.1 %collective-permute-start.1 = (bf16[192,1024]{1,0:T(8,128)(2,1)}, bf16[192,1024]{1,0:T(8,128)(2,1)}, u32[]{:S(2)}, u32[]{:S(2)}) collective-permute-start(bf16[192,1024]{1,0:T(8,128)(2,1)} %get-tuple-element.55), channel_id=1, source_target_pairs={{0,16},{8,24},{16,0},{24,8},{1,17},{9,25},{17,1},{25,9},{2,18},{10... | collective-permute-start | bytes 1179656 | tf_op jit(solution)/shard_map/ppermute | solution.py:79
  21.5 43.4 %collective-permute-start.2 = (bf16[192,1024]{1,0:T(8,128)(2,1)}, bf16[192,1024]{1,0:T(8,128)(2,1)}, u32[]{:S(2)}, u32[]{:S(2)}) collective-permute-start(bf16[192,1024]{1,0:T(8,128)(2,1)} %get-tuple-element.56), channel_id=1, source_target_pairs={{0,24},{8,16},{16,8},{24,0},{1,25},{9,17},{17,9},{25,1},{2,26},{10... | collective-permute-start | bytes 1179656 | tf_op jit(solution)/shard_map/ppermute | solution.py:79
  33.4 31.4 %collective-permute-start.3 = (bf16[192,1024]{1,0:T(8,128)(2,1)}, bf16[192,1024]{1,0:T(8,128)(2,1)}, u32[]{:S(2)}, u32[]{:S(2)}) collective-permute-start(bf16[192,1024]{1,0:T(8,128)(2,1)} %bitcast.7), channel_id=1, source_target_pairs={{0,24},{24,0},{1,25},{25,1},{2,26},{26,2},{3,27},{27,3},{4,28},{28... | collective-permute-start | bytes 1179656 | tf_op jit(solution)/shard_map/ppermute | solution.py:79
  67.8 23.5 %collective-permute-start.4 = (bf16[192,1792]{1,0:T(8,128)(2,1)S(1)}, bf16[192,1792]{1,0:T(8,128)(2,1)S(1)}, u32[]{:S(2)}, u32[]{:S(2)}) collective-permute-start(bf16[192,1792]{1,0:T(8,128)(2,1)S(1)} %get-tuple-element.59), channel_id=1, source_target_pairs={{0,24},{24,0},{1,25},{25,1},{2,26},{26,2},{3,27},{27,3},{4,28},{28... | collective-permute-start | bytes 2064392 | tf_op jit(solution)/shard_map/ppermute | solution.py:79
  69.5 11.2 %collective-permute-start.6 = (f32[12,64,64]{2,1,0:T(8,128)S(1)}, f32[12,64,64]{2,1,0:T(8,128)S(1)}, u32[]{:S(2)}, u32[]{:S(2)}) collective-permute-start(f32[12,64,64]{2,1,0:T(8,128)S(1)} %add.117), channel_id=1, source_target_pairs={{0,2},{1,3},{2,0},{3,1},{4,6},{5,7},{6,4},{7,5},{8,10},{9,11},{10,... | collective-permute-start | bytes 589832 | tf_op jit(solution)/shard_map/ppermute | solution.py:24
  80.8 10.4 %collective-permute-start.7 = (f32[12,64,64]{2,1,0:T(8,128)S(1)}, f32[12,64,64]{2,1,0:T(8,128)S(1)}, u32[]{:S(2)}, u32[]{:S(2)}) collective-permute-start(f32[12,64,64]{2,1,0:T(8,128)S(1)} %add.118), channel_id=1, source_target_pairs={{0,4},{1,5},{2,6},{3,7},{4,0},{5,1},{6,2},{7,3},{8,12},{9,13},{10,... | collective-permute-start | bytes 589832 | tf_op jit(solution)/shard_map/ppermute | solution.py:24
  92.1 107.3 %all-gather.6.cloned.1.call-start = ((), (), s32[]{:S(2)}) async-start(), calls=%async_computation.2 | async-start | bytes 14155776 | tf_op jit(solution)/shard_map/all_gather | solution.py:314
  92.2 32.7 %collective-permute-start.11 = (bf16[192,1792]{1,0:T(8,128)(2,1)S(1)}, bf16[192,1792]{1,0:T(8,128)(2,1)S(1)}, u32[]{:S(2)}, u32[]{:S(2)}) collective-permute-start(bf16[192,1792]{1,0:T(8,128)(2,1)S(1)} %copy-done.9), channel_id=1, source_target_pairs={{0,8},{8,0},{16,24},{24,16},{1,9},{9,1},{17,25},{25,17},{2,10},{10... | collective-permute-start | bytes 2064392 | tf_op jit(solution)/shard_map/ppermute | solution.py:79
  93.8 26.3 %collective-permute-start.8 = (bf16[192,1024]{1,0:T(8,128)(2,1)S(1)}, bf16[192,1024]{1,0:T(8,128)(2,1)S(1)}, u32[]{:S(2)}, u32[]{:S(2)}) collective-permute-start(bf16[192,1024]{1,0:T(8,128)(2,1)S(1)} %bitcast.141), channel_id=1, source_target_pairs={{0,16},{8,24},{16,0},{24,8},{1,17},{9,25},{17,1},{25,9},{2,18},{10... | collective-permute-start | bytes 1179656 | tf_op jit(solution)/shard_map/ppermute | solution.py:321
  96.9 25.8 %collective-permute-start.9 = (bf16[192,1024]{1,0:T(8,128)(2,1)S(1)}, bf16[192,1024]{1,0:T(8,128)(2,1)S(1)}, u32[]{:S(2)}, u32[]{:S(2)}) collective-permute-start(bf16[192,1024]{1,0:T(8,128)(2,1)S(1)} %bitcast.140), channel_id=1, source_target_pairs={{8,0},{16,8},{24,16},{9,1},{17,9},{25,17},{10,2},{18,10},{26,18},{... | collective-permute-start | bytes 1179656 | tf_op jit(solution)/shard_map/ppermute | solution.py:322
  98.8 26.1 %collective-permute-start.10 = (bf16[192,1024]{1,0:T(8,128)(2,1)S(1)}, bf16[192,1024]{1,0:T(8,128)(2,1)S(1)}, u32[]{:S(2)}, u32[]{:S(2)}) collective-permute-start(bf16[192,1024]{1,0:T(8,128)(2,1)S(1)} %bitcast.139), channel_id=1, source_target_pairs={{0,8},{8,16},{16,24},{1,9},{9,17},{17,25},{2,10},{10,18},{18,26},{... | collective-permute-start | bytes 1179656 | tf_op jit(solution)/shard_map/ppermute | solution.py:323
  141.9 71.1 %collective-permute-start.14 = (bf16[768,1792]{1,0:T(8,128)(2,1)}, bf16[768,1792]{1,0:T(8,128)(2,1)}, u32[]{:S(2)}, u32[]{:S(2)}) collective-permute-start(bf16[768,1792]{1,0:T(8,128)(2,1)} %partial_sums.7), channel_id=1, source_target_pairs={{0,8},{24,16},{1,9},{25,17},{2,10},{26,18},{3,11},{27,19},{4,12},{... | collective-permute-start | bytes 8257544 | tf_op jit(solution)/shard_map/ppermute | solution.py:386
  143.2 20.3 %collective-permute-start.13 = (bf16[192,1792]{1,0:T(8,128)(2,1)S(1)}, bf16[192,1792]{1,0:T(8,128)(2,1)}, u32[]{:S(2)}, u32[]{:S(2)}) collective-permute-start(bf16[192,1792]{1,0:T(8,128)(2,1)S(1)} %copy-done.7), channel_id=1, source_target_pairs={{8,16},{16,8},{9,17},{17,9},{10,18},{18,10},{11,19},{19,11},{12,20... | collective-permute-start | bytes 2064392 | tf_op jit(solution)/shard_map/ppermute | solution.py:79
  146.8 74.5 %collective-permute-start.12 = (bf16[192,1792]{1,0:T(8,128)(2,1)}, bf16[192,1792]{1,0:T(8,128)(2,1)S(1)}, u32[]{:S(2)}, u32[]{:S(2)}) collective-permute-start(bf16[192,1792]{1,0:T(8,128)(2,1)} %get-tuple-element.79), channel_id=1, source_target_pairs={{0,16},{8,24},{16,0},{24,8},{1,17},{9,25},{17,1},{25,9},{2,18},{10... | collective-permute-start | bytes 2064392 | tf_op jit(solution)/shard_map/ppermute | solution.py:79
  221.3 62.9 %collective-permute-start.15 = (bf16[768,1792]{1,0:T(8,128)(2,1)}, bf16[768,1792]{1,0:T(8,128)(2,1)}, u32[]{:S(2)}, u32[]{:S(2)}) collective-permute-start(bf16[768,1792]{1,0:T(8,128)(2,1)} %add_convert_fusion.3), channel_id=1, source_target_pairs={{0,8},{8,16},{1,9},{9,17},{2,10},{10,18},{3,11},{11,19},{4,12},{12... | collective-permute-start | bytes 8257544 | tf_op jit(solution)/shard_map/ppermute | solution.py:393
  223.9 64.4 %collective-permute-start.16 = (bf16[768,1792]{1,0:T(8,128)(2,1)}, bf16[768,1792]{1,0:T(8,128)(2,1)}, u32[]{:S(2)}, u32[]{:S(2)}) collective-permute-start(bf16[768,1792]{1,0:T(8,128)(2,1)} %add_convert_fusion.3), channel_id=1, source_target_pairs={{24,16},{16,8},{25,17},{17,9},{26,18},{18,10},{27,19},{19,11},{28,... | collective-permute-start | bytes 8257544 | tf_op jit(solution)/shard_map/ppermute | solution.py:394
  230.2 2.1 collective-permute-start.17
  234.2 11.5 %collective-permute-start.18 = (f32[12,64,64]{2,1,0:T(8,128)}, f32[12,64,64]{2,1,0:T(8,128)}, u32[]{:S(2)}, u32[]{:S(2)}) collective-permute-start(f32[12,64,64]{2,1,0:T(8,128)} %add.127), channel_id=1, source_target_pairs={{0,2},{1,3},{2,0},{3,1},{4,6},{5,7},{6,4},{7,5},{8,10},{9,11},{10,... | collective-permute-start | bytes 589832 | tf_op jit(solution)/shard_map/ppermute | solution.py:24
  246.9 28.2 %collective-permute-start.19 = (f32[12,64,64]{2,1,0:T(8,128)S(1)}, f32[12,64,64]{2,1,0:T(8,128)S(1)}, u32[]{:S(2)}, u32[]{:S(2)}) collective-permute-start(f32[12,64,64]{2,1,0:T(8,128)S(1)} %add.128), channel_id=1, source_target_pairs={{0,4},{1,5},{2,6},{3,7},{4,0},{5,1},{6,2},{7,3},{8,12},{9,13},{10,... | collective-permute-start | bytes 589832 | tf_op jit(solution)/shard_map/ppermute | solution.py:24
  292.3 61.9 %collective-permute-start.20 = (bf16[768,1792]{1,0:T(8,128)(2,1)}, bf16[768,1792]{1,0:T(8,128)(2,1)}, u32[]{:S(2)}, u32[]{:S(2)}) collective-permute-start(bf16[768,1792]{1,0:T(8,128)(2,1)} %add_convert_fusion.2), channel_id=1, source_target_pairs={{0,8},{8,16},{16,24},{1,9},{9,17},{17,25},{2,10},{10,18},{18,26},{... | collective-permute-start | bytes 8257544 | tf_op jit(solution)/shard_map/ppermute | solution.py:393
  294.9 61.9 %collective-permute-start.21 = (bf16[768,1792]{1,0:T(8,128)(2,1)}, bf16[768,1792]{1,0:T(8,128)(2,1)}, u32[]{:S(2)}, u32[]{:S(2)}) collective-permute-start(bf16[768,1792]{1,0:T(8,128)(2,1)} %add_convert_fusion.1), channel_id=1, source_target_pairs={{24,16},{16,8},{8,0},{25,17},{17,9},{9,1},{26,18},{18,10},{10,2},{... | collective-permute-start | bytes 8257544 | tf_op jit(solution)/shard_map/ppermute | solution.py:394
  (16 other events, 229.9 us)
Sparse Core Ops, SparseCore 0:
  92.2 32.4 all-gather.3
  127.2 72.1 all-gather.5

commit v6 on v4

--- a/solution.py
+++ b/solution.py
@@ -210,7 +210,7 @@
 
 def finish(own, left, right, gate, up, part, earlier):
     rows, ff_local = own.shape
-    step = 128 if rows % 128 == 0 else rows
+    step = 64 if rows % 64 == 0 else rows
     steps = rows // step
     here = pl.BlockSpec((step, ff_local), lambda i: (i, 0))
     there = pl.BlockSpec((step, ff_local), lambda i: (part * steps + i, 0))

time: 374 us -> 377 us (level)
  no operation moved by 1% of the time
where the time goes in v6:
time: 377 us; the launch traced here: 373 us
  waiting for transfers between devices  169 us (45%)
  Pallas kernels  94.1 us (25%)
  starting transfers between devices  42.8 us (11%)
  local copies, waits for them, and re-layouts  23.8 us (6%)
  other arithmetic  20.2 us (5%)
  between operations  14.6 us (4%)
  matrix products  8.86 us (2%)
    pallas_call x5, Pallas kernels, partial_sums(): pl.pallas_call(functools.partial(partial_kernel, capacity), grid_spec=plt...  67.8 us
    ppermute x8, waiting for transfers between devices, swap_over_dp(): lax.ppermute(x, 'dp', [(i, i ^ bits) for i in range(size) if only is None...  41.2 us
    all_gather x2, waiting for transfers between devices, gathered(): lax.all_gather(jnp.stack([u.reshape(moved.shape[1:]) for u in units]), 'm...  34.3 us
    ppermute x6, waiting for transfers between devices, sum_over_mp(): x = x + lax.ppermute(x, 'mp', [(i, i ^ bit) for i in range(size)])  32.1 us
    ppermute x2, waiting for transfers between devices, shards(): from_left = [lax.ppermute(s, 'dp', pairs_r) for s in send_r]  26.6 us
    ppermute x1, waiting for transfers between devices, shards(): lax.ppermute(unit_of(target_of(2, 0)), 'dp', pairs)  17.4 us
    unnamed x44, local copies, waits for them, and re-layouts  16.8 us
    ppermute x8, starting transfers between devices, swap_over_dp(): lax.ppermute(x, 'dp', [(i, i ^ bits) for i in range(size) if only is None...  13.2 us
  transfers between devices with their start and end apart: 25, of which 17 were waited for; matrix products, arithmetic and copies ran while one was open for 11% of the time, Pallas kernels for 21%

profile of v6, /device:TPU:10, one launch (start us, length us, event | category | flops | bytes accessed | tf_op | source)
XLA Modules:
  0.0 373.5 jit_solution(3883358645750226316)
XLA Ops:
  7.2 4.8 %all-to-all-start = ((bf16[8,96,1024]{2,1,0:T(8,128)(2,1)}), bf16[8,96,1024]{2,1,0:T(8,128)(2,1)}, u32[]{:S(2)}, u32[]{:S(2)}) async-start(bf16[8,96,1024]{2,1,0:T(8,128)(2,1)} %bitcast.114), calls=%async_computation | async-start | bytes 3145728 | tf_op jit(solution)/shard_map/all_to_all | solution.py:122
  21.9 9.8 %all-to-all-done = bf16[8,96,1024]{2,1,0:T(8,128)(2,1)} async-done(((bf16[8,96,1024]{2,1,0:T(8,128)(2,1)}), bf16[8,96,1024]{2,1,0:T(8,128)(2,1)}, u32[]{:S(2)}, u32[]{:S(2)}) %all-to-all-start) | async-done | bytes 1572896 | tf_op jit(solution)/shard_map/all_to_all | solution.py:122
  35.0 5.1 %pack.3 = (bf16[192,1792]{1,0:T(8,128)(2,1)S(1)}, bf16[192,1792]{1,0:T(8,128)(2,1)S(1)}, bf16[192,1792]{1,0:T(8,128)(2,1)}, bf16[192,1792]{1,0:T(8,128)(2,1)S(1)}) custom-call(s32[12]{0:T(128)S(1)} %reshape.288.info, bf16[768,1792]{1,0:T(8,128)(2,1)S(1)} %copy-done, bf16[768,1792]{1,0:T(8,128)(2,1)S(1)} %copy-done, bf16[768,1792]{1,0:T(8,128)(2,1)S(1)} %copy-done, ...), custom_call_target="tpu_custom_call" | custom-call | tf_op jit(solution)/shard_map/pack/pallas_call | solution.py:55
  40.1 16.4 %collective-permute-done.1.refs_5_ = bf16[192,1024]{1,0:T(8,128)(2,1)} collective-permute-done((bf16[192,1024]{1,0:T(8,128)(2,1)}, bf16[192,1024]{1,0:T(8,128)(2,1)}, u32[]{:S(2)}, u32[]{:S(2)}) %collective-permute-start.1) | collective-permute-done | bytes 393248 | tf_op jit(solution)/shard_map/ppermute | solution.py:79
  56.5 8.3 %collective-permute-done.2.refs_6_ = bf16[192,1024]{1,0:T(8,128)(2,1)} collective-permute-done((bf16[192,1024]{1,0:T(8,128)(2,1)}, bf16[192,1024]{1,0:T(8,128)(2,1)}, u32[]{:S(2)}, u32[]{:S(2)}) %collective-permute-start.2) | collective-permute-done | bytes 393248 | tf_op jit(solution)/shard_map/ppermute | solution.py:79
  69.9 10.8 %collective-permute-done.6 = f32[12,64,64]{2,1,0:T(8,128)S(1)} collective-permute-done((f32[12,64,64]{2,1,0:T(8,128)S(1)}, f32[12,64,64]{2,1,0:T(8,128)S(1)}, u32[]{:S(2)}, u32[]{:S(2)}) %collective-permute-start.6) | collective-permute-done | bytes 196640 | tf_op jit(solution)/shard_map/ppermute | solution.py:24
  82.3 8.9 %collective-permute-done.7 = f32[12,64,64]{2,1,0:T(8,128)S(1)} collective-permute-done((f32[12,64,64]{2,1,0:T(8,128)S(1)}, f32[12,64,64]{2,1,0:T(8,128)S(1)}, u32[]{:S(2)}, u32[]{:S(2)}) %collective-permute-start.7) | collective-permute-done | bytes 196640 | tf_op jit(solution)/shard_map/ppermute | solution.py:24
  101.8 17.4 %collective-permute-done.8 = bf16[192,1024]{1,0:T(8,128)(2,1)S(1)} collective-permute-done((bf16[192,1024]{1,0:T(8,128)(2,1)S(1)}, bf16[192,1024]{1,0:T(8,128)(2,1)S(1)}, u32[]{:S(2)}, u32[]{:S(2)}) %collective-permute-start.8) | collective-permute-done | bytes 393248 | tf_op jit(solution)/shard_map/ppermute | solution.py:322
  130.1 13.1 %partial_sums.7 = bf16[768,1792]{1,0:T(8,128)(2,1)} custom-call(s32[11]{0:T(128)S(1)} %pad_add_fusion.2.info, bf16[8,1,2,96,1024]{4,3,2,1,0:T(8,128)(2,1)S(1)} %copy-done.5, bf16[1792,2048]{1,0:T(8,128)(2,1)} %w_ref.9, bf16[4,3,64,64]{3,2,1,0:T(8,128)(2,1)S(1)} %bitcast.115, bf16[16,64,1792]{2,1,0:T(8,128)(2,1)} %rest_2_.9, bf16[16,64,1792]{2,1,0:T(8,128)(2,1)} %rest_2_.9, ...), custom_call_target="tpu_custom_call" | custom-call | tf_op jit(solution)/shard_map/partial_sums/pallas_call | solution.py:165
  144.5 4.2 %collective-permute-start.13 = (bf16[192,1792]{1,0:T(8,128)(2,1)S(1)}, bf16[192,1792]{1,0:T(8,128)(2,1)}, u32[]{:S(2)}, u32[]{:S(2)}) collective-permute-start(bf16[192,1792]{1,0:T(8,128)(2,1)S(1)} %copy-done.14), channel_id=1, source_target_pairs={{8,16},{16,8},{9,17},{17,9},{10,18},{18,10},{11,19},{19,11},{12,20... | collective-permute-start | bytes 2064392 | tf_op jit(solution)/shard_map/ppermute | solution.py:79
  152.0 13.2 %collective-permute-done.13 = bf16[192,1792]{1,0:T(8,128)(2,1)} collective-permute-done((bf16[192,1792]{1,0:T(8,128)(2,1)S(1)}, bf16[192,1792]{1,0:T(8,128)(2,1)}, u32[]{:S(2)}, u32[]{:S(2)}) %collective-permute-start.13) | collective-permute-done | bytes 688160 | tf_op jit(solution)/shard_map/ppermute | solution.py:79
  166.3 34.3 %all-gather.6.cloned.1.call-done = bf16[32,2,96,1024]{3,2,1,0:T(8,128)(2,1)} async-done(((bf16[4,2,96,1024]{3,2,1,0:T(8,128)(2,1)}), bf16[32,2,96,1024]{3,2,1,0:T(8,128)(2,1)}) %all-gather.6.cloned.1.call-update) | async-done | bytes 12582928 | tf_op jit(solution)/shard_map/all_gather | solution.py:315
  200.6 13.7 %partial_sums.6 = bf16[768,1792]{1,0:T(8,128)(2,1)S(1)} custom-call(s32[11]{0:T(128)S(1)} %pad_add_fusion.3.info, bf16[8,4,2,96,1024]{4,3,2,1,0:T(8,128)(2,1)} %bitcast.129, bf16[1792,2048]{1,0:T(8,128)(2,1)} %w_ref.9, bf16[4,3,64,64]{3,2,1,0:T(8,128)(2,1)S(1)} %bitcast.116, bf16[16,64,1792]{2,1,0:T(8,128)(2,1)} %rest_2_.9, bf16[16,64,1792]{2,1,0:T(8,128)(2,1)} %rest_2_.9, ...), custom_call_target="tpu_custom_call" | custom-call | tf_op jit(solution)/shard_map/partial_sums/pallas_call | solution.py:165
  214.3 4.1 %add_convert_fusion.2 = bf16[768,1792]{1,0:T(8,128)(2,1)} fusion(bf16[768,1792]{1,0:T(8,128)(2,1)} %collective-permute-done.14, bf16[768,1792]{1,0:T(8,128)(2,1)S(1)} %partial_sums.6), kind=kLoop, calls=%fused_computation.5 | loop fusion | flops 5505024 | bytes 8257536 | tf_op jit(solution)/shard_map/convert_element_type | solution.py:359
  225.6 4.9 %factor_parts.3 = f32[12,64,64]{2,1,0:T(8,128)} custom-call(s32[12]{0:T(128)S(1)} %reshape.292.slots, bf16[16,64,1792]{2,1,0:T(8,128)(2,1)} %rest_2_.9, bf16[16,64,1792]{2,1,0:T(8,128)(2,1)} %rest_2_.9, bf16[16,64,1792]{2,1,0:T(8,128)(2,1)} %rest_2_.9, bf16[192,1792]{1,0:T(8,128)(2,1)S(1)} %copy-done.7, ...), custom_call_target="tpu_custom_call" | custom-call | tf_op jit(solution)/shard_map/factor_parts/pallas_call | solution.py:101
  234.3 10.4 %collective-permute-done.18 = f32[12,64,64]{2,1,0:T(8,128)S(1)} collective-permute-done((f32[12,64,64]{2,1,0:T(8,128)S(1)}, f32[12,64,64]{2,1,0:T(8,128)S(1)}, u32[]{:S(2)}, u32[]{:S(2)}) %collective-permute-start.18) | collective-permute-done | bytes 196640 | tf_op jit(solution)/shard_map/ppermute | solution.py:24
  245.4 13.7 %partial_sums.5 = bf16[768,1792]{1,0:T(8,128)(2,1)S(1)} custom-call(s32[11]{0:T(128)S(1)} %pad_add_fusion.5.info, bf16[8,4,2,96,1024]{4,3,2,1,0:T(8,128)(2,1)} %bitcast.130, bf16[1792,2048]{1,0:T(8,128)(2,1)} %w_ref.9, bf16[4,3,64,64]{3,2,1,0:T(8,128)(2,1)S(1)} %bitcast.117, bf16[16,64,1792]{2,1,0:T(8,128)(2,1)} %rest_2_.9, bf16[16,64,1792]{2,1,0:T(8,128)(2,1)} %rest_2_.9, ...), custom_call_target="tpu_custom_call" | custom-call | tf_op jit(solution)/shard_map/partial_sums/pallas_call | solution.py:165
  259.1 13.7 %partial_sums.8 = bf16[768,1792]{1,0:T(8,128)(2,1)S(1)} custom-call(s32[11]{0:T(128)S(1)} %pad_add_fusion.6.info, bf16[8,4,2,96,1024]{4,3,2,1,0:T(8,128)(2,1)} %bitcast.131, bf16[1792,2048]{1,0:T(8,128)(2,1)} %w_ref.9, bf16[4,3,64,64]{3,2,1,0:T(8,128)(2,1)S(1)} %bitcast.118, bf16[16,64,1792]{2,1,0:T(8,128)(2,1)} %rest_2_.9, bf16[16,64,1792]{2,1,0:T(8,128)(2,1)} %rest_2_.9, ...), custom_call_target="tpu_custom_call" | custom-call | tf_op jit(solution)/shard_map/partial_sums/pallas_call | solution.py:165
  272.8 9.9 %collective-permute-done.15 = bf16[768,1792]{1,0:T(8,128)(2,1)} collective-permute-done((bf16[768,1792]{1,0:T(8,128)(2,1)}, bf16[768,1792]{1,0:T(8,128)(2,1)}, u32[]{:S(2)}, u32[]{:S(2)}) %collective-permute-start.15) | collective-permute-done | bytes 2752544 | tf_op jit(solution)/shard_map/ppermute | solution.py:394
  298.3 13.7 %partial_sums.9.own = bf16[768,1792]{1,0:T(8,128)(2,1)S(1)} custom-call(s32[11]{0:T(128)S(1)} %pad_add_fusion.4.info, bf16[8,4,2,96,1024]{4,3,2,1,0:T(8,128)(2,1)} %bitcast.132, bf16[1792,2048]{1,0:T(8,128)(2,1)} %w_ref.9, bf16[4,3,64,64]{3,2,1,0:T(8,128)(2,1)S(1)} %bitcast.119, bf16[16,64,1792]{2,1,0:T(8,128)(2,1)} %rest_2_.9, ...), custom_call_target="tpu_custom_call" | custom-call | tf_op jit(solution)/shard_map/partial_sums/pallas_call | solution.py:165
  316.8 7.3 %copy.89 = f32[16,64,1792]{2,1,0:T(8,128)} copy(f32[16,64,1792]{2,0,1:T(8,128)S(1)} %fusion) | data formatting | bytes 14680064
  330.1 4.4 %copy.90 = f32[16,64,1024]{2,1,0:T(8,128)} copy(f32[16,64,1024]{2,0,1:T(8,128)S(1)} %fusion.7) | data formatting | bytes 8388608
  334.6 16.6 %collective-permute-done.20.left = bf16[768,1792]{1,0:T(8,128)(2,1)} collective-permute-done((bf16[768,1792]{1,0:T(8,128)(2,1)}, bf16[768,1792]{1,0:T(8,128)(2,1)}, u32[]{:S(2)}, u32[]{:S(2)}) %collective-permute-start.20) | collective-permute-done | bytes 2752544 | tf_op jit(solution)/shard_map/ppermute | solution.py:394
  355.0 11.7 %finish.1 = (bf16[768,1792]{1,0:T(8,128)(2,1)}, bf16[768,1792]{1,0:T(8,128)(2,1)}) custom-call(bf16[768,1792]{1,0:T(8,128)(2,1)S(1)} %partial_sums.9.own, bf16[768,1792]{1,0:T(8,128)(2,1)} %collective-permute-done.20.left, bf16[768,1792]{1,0:T(8,128)(2,1)} %collective-permute-done.21.right, bf16[768,1792]{1,0:T(8,128)(2,1)} %gate.1, bf16[768,1792]{1,0:T(8,128)(2,1)} %up.1), custom_call_target="tpu_custom_call" | custom-call | tf_op jit(solution)/shard_map/finish/pallas_call | solution.py:218
  (154 shorter events, 88.7 us)
Async XLA Ops:
  7.2 24.5 %all-to-all-start = ((bf16[8,96,1024]{2,1,0:T(8,128)(2,1)}), bf16[8,96,1024]{2,1,0:T(8,128)(2,1)}, u32[]{:S(2)}, u32[]{:S(2)}) async-start(bf16[8,96,1024]{2,1,0:T(8,128)(2,1)} %bitcast.114), calls=%async_computation | async-start | bytes 3145728 | tf_op jit(solution)/shard_map/all_to_all | solution.py:122
  12.0 112.7 %all-gather.4.cloned.1.call-start = ((), (), s32[]{:S(2)}) async-start(), calls=%async_computation.1 | async-start | bytes 3538944 | tf_op jit(solution)/shard_map/all_gather | solution.py:315
  18.4 21.7 %collective-permute-start = (bf16[192,1024]{1,0:T(8,128)(2,1)}, bf16[192,1024]{1,0:T(8,128)(2,1)}, u32[]{:S(2)}, u32[]{:S(2)}) collective-permute-start(bf16[192,1024]{1,0:T(8,128)(2,1)} %get-tuple-element.54), channel_id=1, source_target_pairs={{0,8},{8,0},{16,24},{24,16},{1,9},{9,1},{17,25},{25,17},{2,10},{10... | collective-permute-start | bytes 1179656 | tf_op jit(solution)/shard_map/ppermute | solution.py:79
  18.4 38.1 %collective-permute-start.1 = (bf16[192,1024]{1,0:T(8,128)(2,1)}, bf16[192,1024]{1,0:T(8,128)(2,1)}, u32[]{:S(2)}, u32[]{:S(2)}) collective-permute-start(bf16[192,1024]{1,0:T(8,128)(2,1)} %get-tuple-element.55), channel_id=1, source_target_pairs={{0,16},{8,24},{16,0},{24,8},{1,17},{9,25},{17,1},{25,9},{2,18},{10... | collective-permute-start | bytes 1179656 | tf_op jit(solution)/shard_map/ppermute | solution.py:79
  21.4 43.4 %collective-permute-start.2 = (bf16[192,1024]{1,0:T(8,128)(2,1)}, bf16[192,1024]{1,0:T(8,128)(2,1)}, u32[]{:S(2)}, u32[]{:S(2)}) collective-permute-start(bf16[192,1024]{1,0:T(8,128)(2,1)} %get-tuple-element.56), channel_id=1, source_target_pairs={{0,24},{8,16},{16,8},{24,0},{1,25},{9,17},{17,9},{25,1},{2,26},{10... | collective-permute-start | bytes 1179656 | tf_op jit(solution)/shard_map/ppermute | solution.py:79
  33.4 31.4 %collective-permute-start.3 = (bf16[192,1024]{1,0:T(8,128)(2,1)}, bf16[192,1024]{1,0:T(8,128)(2,1)}, u32[]{:S(2)}, u32[]{:S(2)}) collective-permute-start(bf16[192,1024]{1,0:T(8,128)(2,1)} %bitcast.7), channel_id=1, source_target_pairs={{0,24},{24,0},{1,25},{25,1},{2,26},{26,2},{3,27},{27,3},{4,28},{28... | collective-permute-start | bytes 1179656 | tf_op jit(solution)/shard_map/ppermute | solution.py:79
  67.8 23.5 %collective-permute-start.4 = (bf16[192,1792]{1,0:T(8,128)(2,1)S(1)}, bf16[192,1792]{1,0:T(8,128)(2,1)S(1)}, u32[]{:S(2)}, u32[]{:S(2)}) collective-permute-start(bf16[192,1792]{1,0:T(8,128)(2,1)S(1)} %get-tuple-element.59), channel_id=1, source_target_pairs={{0,24},{24,0},{1,25},{25,1},{2,26},{26,2},{3,27},{27,3},{4,28},{28... | collective-permute-start | bytes 2064392 | tf_op jit(solution)/shard_map/ppermute | solution.py:79
  69.5 11.2 %collective-permute-start.6 = (f32[12,64,64]{2,1,0:T(8,128)S(1)}, f32[12,64,64]{2,1,0:T(8,128)S(1)}, u32[]{:S(2)}, u32[]{:S(2)}) collective-permute-start(f32[12,64,64]{2,1,0:T(8,128)S(1)} %add.114), channel_id=1, source_target_pairs={{0,2},{1,3},{2,0},{3,1},{4,6},{5,7},{6,4},{7,5},{8,10},{9,11},{10,... | collective-permute-start | bytes 589832 | tf_op jit(solution)/shard_map/ppermute | solution.py:24
  80.8 10.4 %collective-permute-start.7 = (f32[12,64,64]{2,1,0:T(8,128)S(1)}, f32[12,64,64]{2,1,0:T(8,128)S(1)}, u32[]{:S(2)}, u32[]{:S(2)}) collective-permute-start(f32[12,64,64]{2,1,0:T(8,128)S(1)} %add.115), channel_id=1, source_target_pairs={{0,4},{1,5},{2,6},{3,7},{4,0},{5,1},{6,2},{7,3},{8,12},{9,13},{10,... | collective-permute-start | bytes 589832 | tf_op jit(solution)/shard_map/ppermute | solution.py:24
  91.3 109.3 %all-gather.6.cloned.1.call-start = ((), (), s32[]{:S(2)}) async-start(), calls=%async_computation.2 | async-start | bytes 14155776 | tf_op jit(solution)/shard_map/all_gather | solution.py:315
  91.3 33.4 %collective-permute-start.11 = (bf16[192,1792]{1,0:T(8,128)(2,1)S(1)}, bf16[192,1792]{1,0:T(8,128)(2,1)S(1)}, u32[]{:S(2)}, u32[]{:S(2)}) collective-permute-start(bf16[192,1792]{1,0:T(8,128)(2,1)S(1)} %copy-done.16), channel_id=1, source_target_pairs={{0,8},{8,0},{16,24},{24,16},{1,9},{9,1},{17,25},{25,17},{2,10},{10... | collective-permute-start | bytes 2064392 | tf_op jit(solution)/shard_map/ppermute | solution.py:79
  92.9 26.3 %collective-permute-start.8 = (bf16[192,1024]{1,0:T(8,128)(2,1)S(1)}, bf16[192,1024]{1,0:T(8,128)(2,1)S(1)}, u32[]{:S(2)}, u32[]{:S(2)}) collective-permute-start(bf16[192,1024]{1,0:T(8,128)(2,1)S(1)} %bitcast.141), channel_id=1, source_target_pairs={{0,16},{8,24},{16,0},{24,8},{1,17},{9,25},{17,1},{25,9},{2,18},{10... | collective-permute-start | bytes 1179656 | tf_op jit(solution)/shard_map/ppermute | solution.py:322
  96.0 25.8 %collective-permute-start.9 = (bf16[192,1024]{1,0:T(8,128)(2,1)S(1)}, bf16[192,1024]{1,0:T(8,128)(2,1)S(1)}, u32[]{:S(2)}, u32[]{:S(2)}) collective-permute-start(bf16[192,1024]{1,0:T(8,128)(2,1)S(1)} %bitcast.140), channel_id=1, source_target_pairs={{8,0},{16,8},{24,16},{9,1},{17,9},{25,17},{10,2},{18,10},{26,18},{... | collective-permute-start | bytes 1179656 | tf_op jit(solution)/shard_map/ppermute | solution.py:323
  97.9 26.1 %collective-permute-start.10 = (bf16[192,1024]{1,0:T(8,128)(2,1)S(1)}, bf16[192,1024]{1,0:T(8,128)(2,1)S(1)}, u32[]{:S(2)}, u32[]{:S(2)}) collective-permute-start(bf16[192,1024]{1,0:T(8,128)(2,1)S(1)} %bitcast.139), channel_id=1, source_target_pairs={{0,8},{8,16},{16,24},{1,9},{9,17},{17,25},{2,10},{10,18},{18,26},{... | collective-permute-start | bytes 1179656 | tf_op jit(solution)/shard_map/ppermute | solution.py:324
  143.2 71.1 %collective-permute-start.14 = (bf16[768,1792]{1,0:T(8,128)(2,1)}, bf16[768,1792]{1,0:T(8,128)(2,1)}, u32[]{:S(2)}, u32[]{:S(2)}) collective-permute-start(bf16[768,1792]{1,0:T(8,128)(2,1)} %partial_sums.7), channel_id=1, source_target_pairs={{0,8},{24,16},{1,9},{25,17},{2,10},{26,18},{3,11},{27,19},{4,12},{... | collective-permute-start | bytes 8257544 | tf_op jit(solution)/shard_map/ppermute | solution.py:387
  144.5 20.7 %collective-permute-start.13 = (bf16[192,1792]{1,0:T(8,128)(2,1)S(1)}, bf16[192,1792]{1,0:T(8,128)(2,1)}, u32[]{:S(2)}, u32[]{:S(2)}) collective-permute-start(bf16[192,1792]{1,0:T(8,128)(2,1)S(1)} %copy-done.14), channel_id=1, source_target_pairs={{8,16},{16,8},{9,17},{17,9},{10,18},{18,10},{11,19},{19,11},{12,20... | collective-permute-start | bytes 2064392 | tf_op jit(solution)/shard_map/ppermute | solution.py:79
  148.7 72.9 %collective-permute-start.12 = (bf16[192,1792]{1,0:T(8,128)(2,1)}, bf16[192,1792]{1,0:T(8,128)(2,1)S(1)}, u32[]{:S(2)}, u32[]{:S(2)}) collective-permute-start(bf16[192,1792]{1,0:T(8,128)(2,1)} %get-tuple-element.79), channel_id=1, source_target_pairs={{0,16},{8,24},{16,0},{24,8},{1,17},{9,25},{17,1},{25,9},{2,18},{10... | collective-permute-start | bytes 2064392 | tf_op jit(solution)/shard_map/ppermute | solution.py:79
  221.6 61.1 %collective-permute-start.15 = (bf16[768,1792]{1,0:T(8,128)(2,1)}, bf16[768,1792]{1,0:T(8,128)(2,1)}, u32[]{:S(2)}, u32[]{:S(2)}) collective-permute-start(bf16[768,1792]{1,0:T(8,128)(2,1)} %add_convert_fusion.2), channel_id=1, source_target_pairs={{0,8},{8,16},{1,9},{9,17},{2,10},{10,18},{3,11},{11,19},{4,12},{12... | collective-permute-start | bytes 8257544 | tf_op jit(solution)/shard_map/ppermute | solution.py:394
  224.1 62.7 %collective-permute-start.16 = (bf16[768,1792]{1,0:T(8,128)(2,1)}, bf16[768,1792]{1,0:T(8,128)(2,1)}, u32[]{:S(2)}, u32[]{:S(2)}) collective-permute-start(bf16[768,1792]{1,0:T(8,128)(2,1)} %add_convert_fusion.2), channel_id=1, source_target_pairs={{24,16},{16,8},{25,17},{17,9},{26,18},{18,10},{27,19},{19,11},{28,... | collective-permute-start | bytes 8257544 | tf_op jit(solution)/shard_map/ppermute | solution.py:395
  230.5 1.9 collective-permute-start.17
  233.5 11.2 %collective-permute-start.18 = (f32[12,64,64]{2,1,0:T(8,128)S(1)}, f32[12,64,64]{2,1,0:T(8,128)S(1)}, u32[]{:S(2)}, u32[]{:S(2)}) collective-permute-start(f32[12,64,64]{2,1,0:T(8,128)S(1)} %add.124), channel_id=1, source_target_pairs={{0,2},{1,3},{2,0},{3,1},{4,6},{5,7},{6,4},{7,5},{8,10},{9,11},{10,... | collective-permute-start | bytes 589832 | tf_op jit(solution)/shard_map/ppermute | solution.py:24
  244.7 28.0 %collective-permute-start.19 = (f32[12,64,64]{2,1,0:T(8,128)S(1)}, f32[12,64,64]{2,1,0:T(8,128)S(1)}, u32[]{:S(2)}, u32[]{:S(2)}) collective-permute-start(f32[12,64,64]{2,1,0:T(8,128)S(1)} %add.125), channel_id=1, source_target_pairs={{0,4},{1,5},{2,6},{3,7},{4,0},{5,1},{6,2},{7,3},{8,12},{9,13},{10,... | collective-permute-start | bytes 589832 | tf_op jit(solution)/shard_map/ppermute | solution.py:24
  290.8 60.4 %collective-permute-start.20 = (bf16[768,1792]{1,0:T(8,128)(2,1)}, bf16[768,1792]{1,0:T(8,128)(2,1)}, u32[]{:S(2)}, u32[]{:S(2)}) collective-permute-start(bf16[768,1792]{1,0:T(8,128)(2,1)} %add_convert_fusion.1), channel_id=1, source_target_pairs={{0,8},{8,16},{16,24},{1,9},{9,17},{17,25},{2,10},{10,18},{18,26},{... | collective-permute-start | bytes 8257544 | tf_op jit(solution)/shard_map/ppermute | solution.py:394
  294.2 60.8 %collective-permute-start.21 = (bf16[768,1792]{1,0:T(8,128)(2,1)}, bf16[768,1792]{1,0:T(8,128)(2,1)}, u32[]{:S(2)}, u32[]{:S(2)}) collective-permute-start(bf16[768,1792]{1,0:T(8,128)(2,1)} %add_convert_fusion), channel_id=1, source_target_pairs={{24,16},{16,8},{8,0},{25,17},{17,9},{9,1},{26,18},{18,10},{10,2},{... | collective-permute-start | bytes 8257544 | tf_op jit(solution)/shard_map/ppermute | solution.py:395
  (22 other events, 410.9 us)
Sparse Core Ops, SparseCore 0:
  91.4 32.3 all-gather.3
  127.6 72.9 all-gather.5
